TPU v7x, 256 devices: a whole 4x4x8 slice. The times are simulated.
256 devices in a mesh: dp: 16 (over z, core), mp: 16 (over y, x).
Axes of the slice: x: 4, y: 4, z: 8, core: 2. Of those that a mesh axis runs over, the one named last changes fastest.
Arguments:
- residual: bfloat16 [2048, 4096], P('dp'), may hold values from -6 to 6
- norm_gain: float32 [4096], replicated, may hold values from 0.5 to 1.5
- head_weight: bfloat16 [4096, 38912], P('dp', 'mp'), may hold values from -8 to 8
- token_ids: int32 [2048], P('dp'), may hold values from 0 to 38911
- old_logp: float32 [2048], P('dp'), may hold values from -40 to 0
- advantages: float32 [2048], P('dp'), may hold values from -4 to 4
- resp_mask: int32 [2048], P('dp'), may hold values 0 or 1
- routes: int32 [2048, 8], P('dp'), may hold values from 0 to 63, all different within a row; in each aligned block of 128 rows (0 to 127, 128 to 255, ...) at most 32 rows name the same one
- combine_weights: bfloat16 [2048, 8], P('dp'), may hold values from 0.019897461 to 0.29882812
- expert_acts: bfloat16 [64, 16, 32, 1536], P('mp', 'dp'), may hold values from -6 to 6
- down_weight: bfloat16 [64, 1536, 4096], P('mp', None, 'dp'), may hold values from -0.15625 to 0.15625
Outputs:
- resid_grad: float32 [2048, 4096], P('dp', 'mp')
- down_grad: bfloat16 [64, 1536, 4096], P('mp', None, 'dp')
- gate_grad: float32 [2048, 8], P('dp')
Inputs may be any that keep to these rules, and one draw needn't show every extreme that they name: `routes`: each row names 8 different experts. Among the 128 rows of one data group no expert is named more than 32 times, a bound that some block reaches.
All inputs are finite; a program needn't handle non-finite values. No bound on the sum of `resp_mask` on one device may be relied on, other than what follows from the above.
Results may differ from a plain program's by a relative error of at most 0.012.
The roundings to bfloat16 on the way count: a program that leaves them out, or rounds other values in their place, can miss the bound.
Values may be sent and summed in bfloat16 or wider, within the bound.
No kernel may reach another device: no remote copies, remote signals or barrier semaphores. Data moves between devices by JAX's collectives and lax.ppermute only.
A program may use at most 128 MiB of HBM per device.

v0:
```python
import jax
import jax.numpy as jnp
from jax import lax
from jax.sharding import PartitionSpec as P

clip_low = 0.8
clip_high = 1.2
norm_eps = 1e-06


def token_coef(picked, row_top, row_total, old_logp, advantages, resp_mask):
    logp = picked - row_top - jnp.log(row_total)
    prob_ratio = jnp.exp(logp - old_logp)
    return -jnp.clip(prob_ratio, clip_low, clip_high) * advantages * resp_mask.astype(jnp.float32)


def local(
    residual,
    norm_gain,
    head_weight,
    token_ids,
    old_logp,
    advantages,
    resp_mask,
    routes,
    combine_weights,
    expert_acts,
    down_weight,
):
    model_width = residual.shape[1]
    vocab_dev = head_weight.shape[1]
    per_expert = expert_acts.shape[0]
    capacity = expert_acts.shape[2]
    mp_count = lax.axis_size("mp")
    mp_index = lax.axis_index("mp")
    experts_all = per_expert * mp_count
    stream = residual.astype(jnp.float32)
    inv_rms = lax.rsqrt(jnp.mean(stream * stream, axis=1, keepdims=True) + norm_eps)
    normed = (stream * inv_rms * norm_gain[None, :]).astype(jnp.bfloat16)
    full_head = lax.all_gather(head_weight, "dp", axis=0, tiled=True)
    logits = jnp.dot(normed, full_head, preferred_element_type=jnp.float32)
    local_ids = token_ids - mp_index * vocab_dev
    column = jnp.arange(vocab_dev, dtype=jnp.int32)
    onehot = column[None, :] == local_ids[:, None]
    picked_local = jnp.sum(jnp.where(onehot, logits, 0.0), axis=1)
    local_top = jnp.max(logits, axis=1)
    row_top = lax.pmax(local_top, "mp")
    local_total = jnp.sum(jnp.exp(logits - row_top[:, None]), axis=1)
    row_total, picked = lax.psum((local_total, picked_local), "mp")
    shifted = jnp.exp(logits - row_top[:, None])
    weight_row = token_coef(picked, row_top, row_total, old_logp, advantages, resp_mask)
    logit_grad = (
        weight_row[:, None] * (onehot.astype(jnp.float32) - shifted / row_total[:, None])
    ).astype(jnp.bfloat16)
    partial_hidden = lax.dot_general(
        logit_grad, full_head, (((1,), (1,)), ((), ())), preferred_element_type=jnp.float32
    )
    expert_ids = jnp.arange(experts_all, dtype=jnp.int32)
    hit_routes = routes[:, :, None] == expert_ids[None, None, :]
    hit_token = jnp.sum(hit_routes.astype(jnp.int32), axis=1)
    before = jnp.cumsum(hit_token, axis=0) - hit_token
    slot_ids = jnp.arange(capacity, dtype=jnp.int32)
    matches = (hit_token.T[:, None, :] == 1) & (before.T[:, None, :] == slot_ids[None, :, None])
    weight_token = jnp.sum(
        jnp.where(hit_routes, combine_weights[:, :, None].astype(jnp.float32), 0.0), axis=1
    )
    first_expert = mp_index * per_expert
    own_matches = lax.dynamic_slice_in_dim(matches, first_expert, per_expert, 0)
    own_hits = lax.dynamic_slice_in_dim(hit_routes, first_expert, per_expert, 2)
    own_weights = lax.dynamic_slice_in_dim(weight_token, first_expert, per_expert, 1)
    hidden_grad = lax.psum(partial_hidden, "mp")
    scaled_grad = norm_gain[None, :] * hidden_grad
    unit = stream * inv_rms
    inner = jnp.sum(unit * scaled_grad, axis=1, keepdims=True) / model_width
    full_grad = inv_rms * (scaled_grad - unit * inner)
    block_width = model_width // mp_count
    resid_grad = lax.dynamic_slice_in_dim(full_grad, mp_index * block_width, block_width, 1)
    stream_grad = full_grad.astype(jnp.bfloat16)
    own_rows = jnp.einsum(
        "est,td->esd",
        own_matches.astype(jnp.bfloat16),
        stream_grad,
        preferred_element_type=jnp.float32,
    ).astype(jnp.bfloat16)
    slot_rows = lax.all_to_all(own_rows[:, None], "dp", split_axis=3, concat_axis=1, tiled=True)
    slot_weight = jnp.einsum(
        "est,te->es", own_matches.astype(jnp.float32), own_weights, precision=lax.Precision.HIGHEST
    ).astype(jnp.bfloat16)
    acts_all, weight_all = (
        lax.all_gather(expert_acts, "dp", axis=1, tiled=True),
        lax.all_gather(slot_weight[:, None, :], "dp", axis=1, tiled=True),
    )
    proj = jnp.einsum("egsf,efd->egsd", acts_all, down_weight, preferred_element_type=jnp.float32)
    rows_wide = slot_rows.astype(jnp.float32)
    slot_gate = jnp.sum(rows_wide * proj, axis=3)
    weighted = (weight_all.astype(jnp.float32)[:, :, :, None] * rows_wide).astype(jnp.bfloat16)
    down_grad = jnp.einsum(
        "egsf,egsd->efd", acts_all, weighted, preferred_element_type=jnp.float32
    ).astype(jnp.bfloat16)
    group_gate = lax.psum_scatter(slot_gate, "dp", scatter_dimension=1, tiled=True)[:, 0, :]
    per_token = jnp.einsum(
        "est,es->te", own_matches.astype(jnp.float32), group_gate, precision=lax.Precision.HIGHEST
    )
    gate_part = jnp.sum(jnp.where(own_hits, per_token[:, None, :], 0.0), axis=2)
    gate_grad = lax.psum(gate_part, "mp")
    return (resid_grad, down_grad, gate_grad)


def solution(mesh):
    placed = (
        P("dp", None),
        P(),
        P("dp", "mp"),
        P("dp"),
        P("dp"),
        P("dp"),
        P("dp"),
        P("dp", None),
        P("dp", None),
        P("mp", "dp", None, None),
        P("mp", None, "dp"),
    )
    return jax.shard_map(
        local,
        mesh=mesh,
        in_specs=placed,
        out_specs=(P("dp", "mp"), P("mp", None, "dp"), P("dp", None)),
        check_vma=False,
    )
```

profile of v0, /device:TPU:1, one launch (start us, length us, event | category | flops | bytes accessed | tf_op | source)
XLA Modules:
  0.0 515.3 jit_solution(3754663580079249718)
XLA Ops:
  8.0 1.7 fusion.11
  9.7 114.6 %all-gather.5.cloned.1.call-done = bf16[4096,2432]{1,0:T(8,128)(2,1)} async-done(((bf16[256,2432]{1,0:T(8,128)(2,1)}), bf16[4096,2432]{1,0:T(8,128)(2,1)}) %all-gather.5.cloned.1.call-update) | async-done | bytes 19922960 | tf_op jit(solution)/shard_map/all_gather | solution.py:40
  124.4 11.0 %fusion.42 = (f32[128]{0:T(128)S(1)}, f32[128,2432]{1,0:T(8,128)}) fusion(bf16[4096,2432]{1,0:T(8,128)(2,1)} %all-gather.5.cloned.1.call-done, bf16[128,4096]{1,0:T(8,128)(2,1)} %param.11, f32[4096]{0:T(1024)S(1)} %copy-done.4, f32[128]{0:T(128)S(1)} %add_rsqrt_fusion), kind=kOutput, calls=%fused_computation.63 | convolution fusion | flops 2552545280 | bytes 22234112 | tf_op jit(solution)/shard_map/dot_general | solution.py:41
  135.4 33.2 %pmax.7 = f32[128]{0:T(128)S(1)} all-reduce(f32[128]{0:T(128)S(1)} %get-tuple-element.25), channel_id=1, replica_groups=mesh['dp'=16,'mp'=16] {'mp'}, use_global_device_ids=true, to_apply=%region_4.5 | all-reduce | flops 128 | bytes 1024 | tf_op jit(solution)/shard_map/pmax | solution.py:47
  168.6 1.8 select_reduce_fusion
  170.3 28.5 %all-reduce.1 = (f32[128]{0:T(128)S(1)}, f32[128]{0:T(128)S(1)}) all-reduce(f32[128]{0:T(128)S(1)} %get-tuple-element.22, f32[128]{0:T(128)S(1)} %get-tuple-element.21), channel_id=1, replica_groups=mesh['dp'=16,'mp'=16] {'mp'}, use_global_device_ids=true, to_apply=%region_6.7 | all-reduce | flops 256 | bytes 2048 | tf_op jit(solution)/shard_map/psum | solution.py:49
  198.9 11.8 %fusion.25 = f32[128,4096]{1,0:T(8,128)} fusion(bf16[4096,2432]{1,0:T(8,128)(2,1)} %all-gather.5.cloned.1.call-done, f32[128,2432]{1,0:T(8,128)} %get-tuple-element.26, f32[128]{0:T(128)S(1)} %get-tuple-element.23, f32[128]{0:T(128)S(1)} %convert_multiply_fusion.2, f32[128]{0:T(128)S(1)} %pmax.7, s32[128]{0:T(128)S(1)} %broadcast_subtract_fusion), kind=kOutput, calls=%fused_computation.31 | convolution fusion | flops 2552315904 | bytes 23267328 | tf_op jit(solution)/shard_map/dot_general | solution.py:55
  212.0 106.9 %all-reduce.4.cloned.1.call-done = f32[128,4096]{1,0:T(8,128)} async-done(((f32[128,4096]{1,0:T(8,128)}), f32[128,4096]{1,0:T(8,128)}) %all-reduce.4.cloned.1.call-update) | async-done | bytes 2097168 | tf_op jit(solution)/shard_map/psum | solution.py:71
  318.9 2.5 fusion.8
  322.2 1.3 copy-done.2
  323.6 1.4 fusion
  325.0 6.2 %copy.62 = bf16[4,1,32,4096]{2,0,1,3:T(4,128)(2,1)} copy(bf16[4,1,32,4096]{3,2,0,1:T(8,128)(2,1)} %fusion) | data formatting | bytes 2097152 | tf_op jit(solution)/shard_map/broadcast_in_dim | solution.py:85
  331.1 7.7 %reshape.50 = bf16[16,2,16384]{2,1,0:T(2,128)(2,1)} reshape(bf16[4096,1,4,32]{3,2,1,0:T(4,128)(2,1)} %bitcast.69) | data formatting | bytes 2097152
  338.8 9.0 %all-to-all-start = ((bf16[16,2,16384]{2,1,0:T(2,128)(2,1)}), bf16[16,2,16384]{2,1,0:T(2,128)(2,1)}, u32[]{:S(2)}, u32[]{:S(2)}) async-start(bf16[16,2,16384]{2,1,0:T(2,128)(2,1)} %reshape.50), calls=%async_computation | async-start | bytes 2097152 | tf_op jit(solution)/shard_map/all_to_all | solution.py:85
  348.1 48.0 %all-gather.1 = bf16[16,32,4]{1,2,0:T(4,128)(2,1)S(1)} all-gather(bf16[1,32,4]{1,2,0:T(4,128)(2,1)S(1)} %convert_bitcast_fusion), channel_id=2, replica_groups=mesh['dp'=16,'mp'=16] {'dp'}, dimensions={0}, use_global_device_ids=true | all-gather | bytes 4352 | tf_op jit(solution)/shard_map/all_gather | solution.py:91
  396.9 1.6 constant_dynamic-slice_fusion.3
  398.4 7.4 %reshape.51 = bf16[4096,1,4,32]{3,2,1,0:T(4,128)(2,1)} reshape(bf16[16,2,16384]{2,1,0:T(2,128)(2,1)} %all-to-all-done) | data formatting | bytes 2097152
  405.8 6.3 %copy.63 = bf16[4,1,32,4096]{3,2,1,0:T(8,128)(2,1)} copy(bf16[4,1,32,4096]{2,0,1,3:T(4,128)(2,1)} %bitcast.70) | data formatting | bytes 2097152 | tf_op jit(solution)/shard_map/all_to_all | solution.py:85
  412.1 2.8 copy.76
  414.9 7.9 %fusion.1 = bf16[4,1536,256]{1,2,0:T(8,128)(2,1)} fusion(bf16[4,16,32,1536]{3,2,1,0:T(8,128)(2,1)} %all-gather.7.cloned.1.call-done, f32[4,1,32,16,256]{4,3,2,0,1:T(8,128)} %bitcast.72, f32[4,16,32]{2,1,0:T(8,128)S(1)} %reshape.38), kind=kOutput, calls=%fused_computation.3 | convolution fusion | flops 1613234176 | bytes 11542528 | tf_op jit(solution)/shard_map/egsf,egsd->efd/dot_general | solution.py:97
  422.9 4.6 copy.66
  427.5 6.1 %fusion.13 = f32[4,16,32]{2,1,0:T(8,128)S(1)} fusion(f32[4,1,32,16,256]{4,3,2,0,1:T(8,128)} %bitcast.73, bf16[4,16,32,1536]{3,2,1,0:T(8,128)(2,1)} %all-gather.7.cloned.1.call-done, bf16[4,1536,256]{2,1,0:T(8,128)(2,1)S(1)} %copy-done), kind=kOutput, calls=%fused_computation.19 | convolution fusion | flops 1611659264 | bytes 11542528 | tf_op jit(solution)/shard_map/egsf,efd->egsd/dot_general | solution.py:93
  433.6 42.5 %all-reduce = f32[4,16,32]{2,0,1:T(4,128)S(1)} all-reduce(f32[4,16,32]{2,0,1:T(4,128)S(1)} %copy.65), channel_id=3, replica_groups=mesh['dp'=16,'mp'=16] {'dp'}, use_global_device_ids=true, to_apply=%region_13.14.clone | all-reduce | flops 2048 | bytes 16384
  477.0 31.8 %psum.31 = f32[128,8]{0,1:T(8,128)} all-reduce(f32[128,8]{0,1:T(8,128)S(1)} %select_reduce_fusion.2), channel_id=1, replica_groups=mesh['dp'=16,'mp'=16] {'mp'}, use_global_device_ids=true, to_apply=%region_15.16 | all-reduce | flops 1024 | bytes 8192 | tf_op jit(solution)/shard_map/psum | solution.py:105
  (58 shorter events, 4.8 us)
Async XLA Ops:
  7.2 420.3 %copy-start = (bf16[4,1536,256]{2,1,0:T(8,128)(2,1)S(1)}, bf16[4,1536,256]{2,1,0:T(8,128)(2,1)}, u32[]{:S(2)}) copy-start(bf16[4,1536,256]{2,1,0:T(8,128)(2,1)} %param.21) | copy-start | bytes 9437188
  7.2 2.5 copy-start.10
  7.2 117.2 %copy-start.4 = (f32[4096]{0:T(1024)S(1)}, f32[4096]{0:T(1024)}, u32[]{:S(2)}) copy-start(f32[4096]{0:T(1024)} %param.12) | copy-start | bytes 49156
  7.2 117.2 %all-gather.5.cloned.1.call-start = ((), (), s32[]{:S(2)}) async-start(), calls=%async_computation.1 | async-start | bytes 21168128 | tf_op jit(solution)/shard_map/all_gather | solution.py:40
  7.9 310.9 %all-reduce.4.cloned.1.call-start = ((), (), s32[]{:S(2)}) async-start(), calls=%async_computation.2 | async-start | bytes 4194304 | tf_op jit(solution)/shard_map/psum | solution.py:71
  9.7 189.1 %copy-start.7 = (s32[128]{0:T(128)S(1)}, s32[128]{0:T(128)}, u32[]{:S(2)}) copy-start(s32[128]{0:T(128)} %param.17) | copy-start | bytes 1540
  9.7 189.1 %copy-start.8 = (f32[128]{0:T(128)S(1)}, f32[128]{0:T(128)}, u32[]{:S(2)}) copy-start(f32[128]{0:T(128)} %param.16) | copy-start | bytes 1540
  9.7 189.1 %copy-start.9 = (f32[128]{0:T(128)S(1)}, f32[128]{0:T(128)}, u32[]{:S(2)}) copy-start(f32[128]{0:T(128)} %param.15) | copy-start | bytes 1540
  210.7 0.8 copy-start.5
  210.7 204.2 %all-gather.7.cloned.1.call-start = ((), (), s32[]{:S(2)}) async-start(), calls=%async_computation.3 | async-start | bytes 6684672 | tf_op jit(solution)/shard_map/all_gather | solution.py:90
  318.9 2.6 copy-start.1
  318.9 2.9 copy-start.3
  322.2 1.3 copy-start.2
  338.8 9.0 %copy-start.6 = (bf16[128,8]{0,1:T(8,128)(2,1)S(1)}, bf16[128,8]{0,1:T(8,128)(2,1)}, u32[]{:S(2)}) copy-start(bf16[128,8]{0,1:T(8,128)(2,1)} %param.19) | copy-start | bytes 6148
  338.8 57.4 %copy-start.11 = (u32[256]{0:T(256)S(1)}, u32[256]{0:T(256)}, u32[]{:S(2)}) copy-start(u32[256]{0:T(256)} %constant.39) | copy-start | bytes 3076
  338.8 59.6 %all-to-all-start = ((bf16[16,2,16384]{2,1,0:T(2,128)(2,1)}), bf16[16,2,16384]{2,1,0:T(2,128)(2,1)}, u32[]{:S(2)}, u32[]{:S(2)}) async-start(bf16[16,2,16384]{2,1,0:T(2,128)(2,1)} %reshape.50), calls=%async_computation | async-start | bytes 2097152 | tf_op jit(solution)/shard_map/all_to_all | solution.py:85
Sparse Core Ops, SparseCore 0:
  9.9 114.4 all-gather.4
  210.8 107.9 all-reduce.3
  320.9 69.4 all-gather.6
where the time goes:
time: 524 us; the launch traced here: 515 us
  waiting for transfers between devices  223 us (43%)
  blocking collectives  184 us (35%)
  local copies, waits for them, and re-layouts  39.8 us (8%)
  matrix products  38.5 us (7%)
  between operations  14 us (3%)
  starting transfers between devices  9.12 us (2%)
  other arithmetic  6.95 us (1%)
    all_gather x1, waiting for transfers between devices, local(): full_head = lax.all_gather(head_weight, 'dp', axis=0, tiled=True)  115 us
    psum x1, waiting for transfers between devices, local(): hidden_grad = lax.psum(partial_hidden, 'mp')  107 us
    all_gather x1, blocking collectives, local(): lax.all_gather(slot_weight[:, None, :], 'dp', axis=1, tiled=True)  48 us
    unnamed x1, blocking collectives  42.5 us
    pmax x1, blocking collectives, local(): row_top = lax.pmax(local_top, 'mp')  33.2 us
    psum x1, blocking collectives, local(): gate_grad = lax.psum(gate_part, 'mp')  31.8 us
    psum x1, blocking collectives, local(): row_total, picked = lax.psum((local_total, picked_local), 'mp')  28.5 us
    unnamed x30, local copies, waits for them, and re-layouts  25.4 us
  transfers between devices with their start and end apart: 4, of which 2 were waited for; matrix products, arithmetic and copies ran while one was open for 8% of the time, Pallas kernels for 0%

commit v1 on v0

v1 whole, which is shorter than its diff:
```python
import functools

import jax
import jax.numpy as jnp
from jax import lax
from jax.experimental import pallas as pl
from jax.experimental.pallas import tpu as pltpu
from jax.sharding import PartitionSpec as P

clip_low = 0.8
clip_high = 1.2
norm_eps = 1e-06
f32 = jnp.float32
bf16 = jnp.bfloat16
lanes = 128


def z_shift(step, nz):
    return [(2 * z + c, 2 * ((z + step) % nz) + c) for z in range(nz) for c in range(2)]


def core_swap(nz):
    return [(2 * z + c, 2 * z + 1 - c) for z in range(nz) for c in range(2)]


def z_ring(block, nz):
    ahead = back = block
    pieces = [(0, 0, block)]
    for step in range(1, nz // 2):
        ahead = lax.ppermute(ahead, "dp", z_shift(1, nz))
        back = lax.ppermute(back, "dp", z_shift(-1, nz))
        pieces += [(nz - step, 0, ahead), (step, 0, back)]
    half = block.shape[0] // 2
    pieces += [
        (nz // 2, 0, lax.ppermute(ahead[:half], "dp", z_shift(1, nz))),
        (nz // 2, half, lax.ppermute(back[half:], "dp", z_shift(-1, nz))),
    ]
    return pieces


def proj_kernel(acts_ref, down_ref, proj_ref):
    groups, _, slots, wide = acts_ref.shape
    width = down_ref.shape[1]
    acts = acts_ref[:, 0, :, :width].reshape(groups * slots, width)
    out = jnp.dot(acts, down_ref[0], preferred_element_type=f32)
    proj_ref[...] = out.reshape(proj_ref.shape)


def slot_kernel(place_ref, group_ref, side_ref, rows_ref, proj_ref, weighted_ref, gate_ref):
    per_expert, slots, _ = side_ref.shape[1:]
    side = side_ref[0].reshape(per_expert * slots, lanes).astype(f32)
    weight = side[:, 0:1]
    token = side[:, 1:2]
    tokens = rows_ref.shape[1]
    column = lax.broadcasted_iota(jnp.int32, (per_expert * slots, tokens), 1).astype(f32)
    match = jnp.where(column == token, 1.0, 0.0).astype(bf16)
    rows = jnp.dot(match, rows_ref[0], preferred_element_type=f32)
    proj = proj_ref[:, 0].reshape(rows.shape)
    ones = jnp.ones((8, rows.shape[1]), f32)
    gate_ref[0] = lax.dot_general(
        ones, rows * proj, (((1,), (1,)), ((), ())),
        precision=lax.Precision.HIGHEST, preferred_element_type=f32,
    )
    weighted_ref[:, 0] = (weight * rows).astype(bf16).reshape(per_expert, slots, rows.shape[1])


def down_kernel(acts_ref, weighted_ref, out_ref):
    groups, _, slots, wide = acts_ref.shape
    width = out_ref.shape[1]
    acts = acts_ref[:, 0, :, :width].reshape(groups * slots, width)
    weighted = weighted_ref[0].reshape(groups * slots, weighted_ref.shape[3])
    out_ref[0] = lax.dot_general(
        acts, weighted, (((0,), (0,)), ((), ())), preferred_element_type=f32
    ).astype(bf16)


def local(
    residual,
    norm_gain,
    head_weight,
    token_ids,
    old_logp,
    advantages,
    resp_mask,
    routes,
    combine_weights,
    expert_acts,
    down_weight,
):
    tokens, model_width = residual.shape
    block, vocab_dev = head_weight.shape
    per_expert, _, capacity, hidden_width = expert_acts.shape
    dp_count = lax.axis_size("dp")
    mp_count = lax.axis_size("mp")
    nz = dp_count // 2
    dp_index = lax.axis_index("dp")
    mp_index = lax.axis_index("mp")
    z_index, core = dp_index // 2, dp_index % 2
    experts_all = per_expert * mp_count
    swap = functools.partial(lax.ppermute, axis_name="dp", perm=core_swap(nz))

    head_pieces = z_ring(head_weight, nz)

    stream = residual.astype(f32)
    inv_rms = lax.rsqrt(jnp.mean(stream * stream, axis=1, keepdims=True) + norm_eps)
    normed = (stream * inv_rms * norm_gain[None, :]).astype(bf16)
    by_block = normed.reshape(tokens, nz, 2, block).transpose(2, 1, 0, 3)
    mine = lax.dynamic_index_in_dim(by_block, core, 0, keepdims=False)
    theirs = lax.dynamic_index_in_dim(by_block, 1 - core, 0, keepdims=False)
    chip_normed = jnp.concatenate([mine, swap(theirs)], axis=1)

    expert_ids = jnp.arange(experts_all, dtype=jnp.int32)
    hit_routes = routes[:, :, None] == expert_ids[None, None, :]
    hit_token = jnp.sum(hit_routes.astype(jnp.int32), axis=1)
    before = jnp.cumsum(hit_token, axis=0) - hit_token
    slot_ids = jnp.arange(capacity, dtype=jnp.int32)
    matches = (hit_token.T[:, None, :] == 1) & (before.T[:, None, :] == slot_ids[None, :, None])
    weight_token = jnp.sum(
        jnp.where(hit_routes, combine_weights[:, :, None].astype(f32), 0.0), axis=1
    )
    first_expert = mp_index * per_expert
    own_matches = lax.dynamic_slice_in_dim(matches, first_expert, per_expert, 0)
    own_weights = lax.dynamic_slice_in_dim(weight_token, first_expert, per_expert, 1)
    slot_weight = jnp.sum(jnp.where(own_matches, own_weights.T[:, None, :], 0.0), axis=2)
    token_numbers = jnp.arange(tokens, dtype=jnp.int32)
    slot_token = jnp.sum(jnp.where(own_matches, token_numbers[None, None, :] + 1, 0), axis=2) - 1
    lane = jnp.arange(lanes, dtype=jnp.int32)
    side = jnp.where(
        lane == 0,
        slot_weight[:, :, None],
        jnp.where(lane == 1, slot_token.astype(f32)[:, :, None], 0.0),
    ).astype(bf16)
    acts_block = jnp.concatenate([expert_acts[:, 0], side], axis=2)

    partial = jnp.zeros((2 * tokens, vocab_dev), f32)
    for offset, first, piece in head_pieces:
        features = lax.dynamic_index_in_dim(
            chip_normed, lax.rem(z_index + offset, nz), 0, keepdims=False
        )[:, first : first + piece.shape[0]]
        partial = partial + jnp.dot(features, piece, preferred_element_type=f32)
    logits = partial[:tokens] + swap(partial[tokens:])

    local_ids = token_ids - mp_index * vocab_dev
    column = jnp.arange(vocab_dev, dtype=jnp.int32)
    onehot = column[None, :] == local_ids[:, None]
    local_top = jnp.max(logits, axis=1)
    local_exp = jnp.exp(logits - local_top[:, None])
    local_total = jnp.sum(local_exp, axis=1)
    local_mean = jnp.sum(local_exp * logits, axis=1)
    local_picked = jnp.sum(jnp.where(onehot, logits, 0.0), axis=1)
    stats = jnp.stack([local_top, local_total, local_mean, local_picked])
    stats = lax.all_to_all(
        jnp.broadcast_to(stats[None], (mp_count, 4, tokens)), "mp", 0, 0, tiled=True
    )
    row_top = jnp.max(stats[:, 0], axis=0)
    rescale = jnp.exp(stats[:, 0] - row_top[None])
    row_total = jnp.sum(stats[:, 1] * rescale, axis=0)
    mean_logit = jnp.sum(stats[:, 2] * rescale, axis=0) / row_total
    picked = jnp.sum(stats[:, 3], axis=0)

    logp = picked - row_top - jnp.log(row_total)
    prob_ratio = jnp.exp(logp - old_logp)
    weight_row = -jnp.clip(prob_ratio, clip_low, clip_high) * advantages * resp_mask.astype(f32)
    inner = weight_row * (picked - mean_logit) / model_width
    logit_grad = (
        weight_row[:, None]
        * (onehot.astype(f32) - jnp.exp(logits - row_top[:, None]) / row_total[:, None])
    ).astype(bf16)
    chip_grad = jnp.concatenate([logit_grad, swap(logit_grad)], axis=0)

    parts = []
    for offset, first, piece in head_pieces:
        parts.append(
            lax.dot_general(
                chip_grad, piece, (((1,), (1,)), ((), ())), preferred_element_type=f32
            )
        )
    parts = parts[:1] + parts[2:-2:2] + [jnp.concatenate(parts[-2:], axis=1)] + parts[-4:0:-2]
    by_offset = jnp.stack(parts)
    hidden = jnp.roll(by_offset, z_index, axis=0)
    own_part, other_part = hidden[:, :tokens], swap(hidden[:, tokens:])
    hidden = jnp.where(
        core == 0,
        jnp.stack([own_part, other_part], axis=1),
        jnp.stack([other_part, own_part], axis=1),
    ).reshape(mp_count, tokens, block)
    hidden_grad = jnp.sum(lax.all_to_all(hidden, "mp", 0, 0, tiled=True), axis=0)

    my_stream = lax.dynamic_slice_in_dim(stream, mp_index * block, block, 1)
    my_gain = lax.dynamic_slice_in_dim(norm_gain, mp_index * block, block, 0)
    scaled_grad = my_gain[None, :] * hidden_grad
    resid_grad = inv_rms * (scaled_grad - my_stream * inv_rms * inner[:, None])
    stream_grad = resid_grad.astype(bf16)

    turned = lax.ppermute(
        stream_grad,
        ("dp", "mp"),
        [(p * mp_count + q, q * mp_count + p) for p in range(dp_count) for q in range(mp_count)],
    )
    all_rows = lax.all_to_all(
        jnp.broadcast_to(turned[None], (mp_count, tokens, block)), "mp", 0, 0, tiled=True
    )

    pieces = z_ring(acts_block, nz)
    acts_list = [p for _, _, p in pieces[:-2]] + [jnp.concatenate([pieces[-2][2], pieces[-1][2]], axis=0)]
    offsets = [o for o, _, _ in pieces[:-1]]
    acts_own = jnp.stack(acts_list)
    acts_all = jnp.concatenate([acts_own, swap(acts_own)], axis=0)
    offsets = jnp.array(offsets, jnp.int32)
    z_of = lax.rem(z_index + offsets, nz)
    group_of = jnp.concatenate([2 * z_of + core, 2 * z_of + 1 - core]).astype(jnp.int32)

    wide = hidden_width + lanes
    proj = pl.pallas_call(
        proj_kernel,
        grid=(per_expert,),
        in_specs=[
            pl.BlockSpec((dp_count, 1, capacity, wide), lambda e: (0, e, 0, 0)),
            pl.BlockSpec((1, hidden_width, block), lambda e: (e, 0, 0)),
        ],
        out_specs=pl.BlockSpec((1, dp_count, capacity, block), lambda e: (e, 0, 0, 0)),
        out_shape=jax.ShapeDtypeStruct((per_expert, dp_count, capacity, block), f32),
        compiler_params=pltpu.CompilerParams(vmem_limit_bytes=32 * 1024 * 1024),
    )(acts_all, down_weight)
    weighted, gate = pl.pallas_call(
        slot_kernel,
        grid_spec=pltpu.PrefetchScalarGridSpec(
            num_scalar_prefetch=2,
            grid=(dp_count,),
            in_specs=[
                pl.BlockSpec(
                    (1, per_expert, capacity, lanes),
                    lambda n, place, group: (n, 0, 0, hidden_width // lanes),
                ),
                pl.BlockSpec((1, tokens, block), lambda n, place, group: (place[n], 0, 0)),
                pl.BlockSpec((per_expert, 1, capacity, block), lambda n, place, group: (0, n, 0, 0)),
            ],
            out_specs=[
                pl.BlockSpec((per_expert, 1, capacity, block), lambda n, place, group: (0, n, 0, 0)),
                pl.BlockSpec((1, 8, per_expert * capacity), lambda n, place, group: (group[n], 0, 0)),
            ],
        ),
        out_shape=[
            jax.ShapeDtypeStruct((per_expert, dp_count, capacity, block), bf16),
            jax.ShapeDtypeStruct((dp_count, 8, per_expert * capacity), f32),
        ],
    )(group_of, group_of, acts_all, all_rows, proj)
    down_grad = pl.pallas_call(
        down_kernel,
        grid=(per_expert,),
        in_specs=[
            pl.BlockSpec((dp_count, 1, capacity, wide), lambda e: (0, e, 0, 0)),
            pl.BlockSpec((1, dp_count, capacity, block), lambda e: (e, 0, 0, 0)),
        ],
        out_specs=pl.BlockSpec((1, hidden_width, block), lambda e: (e, 0, 0)),
        out_shape=jax.ShapeDtypeStruct((per_expert, hidden_width, block), bf16),
        compiler_params=pltpu.CompilerParams(vmem_limit_bytes=32 * 1024 * 1024),
    )(acts_all, weighted)

    group_gate = jnp.sum(
        lax.all_to_all(gate[:, :1, :], "dp", 0, 0, tiled=True), axis=0, keepdims=True
    )
    slot_gate = lax.all_to_all(
        jnp.broadcast_to(group_gate, (mp_count, 1, per_expert * capacity)), "mp", 0, 0, tiled=True
    ).reshape(experts_all, capacity)
    per_token = jnp.sum(jnp.where(matches, slot_gate[:, :, None], 0.0), axis=1)
    gate_grad = jnp.sum(jnp.where(hit_routes, per_token.T[:, None, :], 0.0), axis=2)
    return (resid_grad, down_grad, gate_grad)


def solution(mesh):
    placed = (
        P("dp", None),
        P(),
        P("dp", "mp"),
        P("dp"),
        P("dp"),
        P("dp"),
        P("dp"),
        P("dp", None),
        P("dp", None),
        P("mp", "dp", None, None),
        P("mp", None, "dp"),
    )
    return jax.shard_map(
        local,
        mesh=mesh,
        in_specs=placed,
        out_specs=(P("dp", "mp"), P("mp", None, "dp"), P("dp", None)),
        check_vma=False,
    )
```

time: 524 us -> 301 us (0.57); the launches traced: 515 us -> 300 us
  blocking collectives: 184 us -> 13.6 us
  waiting for transfers between devices: 223 us -> 132 us
  starting transfers between devices: 9.12 us -> 62.2 us
  Pallas kernels: 0 us -> 24.4 us
  matrix products: 38.5 us -> 20.2 us
  between operations: 14 us -> 1.4 us
  local copies, waits for them, and re-layouts: 39.8 us -> 29.6 us
  other arithmetic: 6.95 us -> 16.1 us
    all_gather x2 -> x0, waiting for transfers between devices: 115 us -> none  [the longest x1 115 us: local(): full_head = lax.all_gather(head_weight, 'dp', axis=0, tiled=True)]
    psum x1 -> x0, waiting for transfers between devices: 107 us -> none  [local(): hidden_grad = lax.psum(partial_hidden, 'mp')]
    ppermute x0 -> x22, waiting for transfers between devices: none -> 91.9 us  [the longest x6 68.1 us: z_ring(): back = lax.ppermute(back, 'dp', z_shift(-1, nz))]
    psum x2 -> x0, blocking collectives: 60.3 us -> none  [the longest x1 31.8 us: local(): gate_grad = lax.psum(gate_part, 'mp')]
    all_gather x1 -> x0, blocking collectives: 48 us -> none  [local(): lax.all_gather(slot_weight[:, None, :], 'dp', axis=1, tiled=True)]
    unnamed x1 -> x0, blocking collectives: 42.5 us -> none
    all_to_all x1 -> x4, waiting for transfers between devices: 0.01 us -> 40.2 us  [the longest x1 31.6 us: local(): lax.all_to_all(hidden, 'mp', 0, 0, tiled=True)]
    ppermute x0 -> x22, starting transfers between devices: none -> 37.7 us  [the longest x6 21.3 us: z_ring(): back = lax.ppermute(back, 'dp', z_shift(-1, nz))]
  transfers between devices with their start and end apart: 4 -> 26, of which waited for: 2 -> 10; matrix products, arithmetic and copies ran while one was open for 8% -> 18% of each run, Pallas kernels for 0% -> 4%
where the time goes in v1:
time: 301 us; the launch traced here: 300 us
  waiting for transfers between devices  132 us (44%)
  starting transfers between devices  62.2 us (21%)
  local copies, waits for them, and re-layouts  29.6 us (10%)
  Pallas kernels  24.4 us (8%)
  matrix products  20.2 us (7%)
  other arithmetic  16.1 us (5%)
  blocking collectives  13.6 us (5%)
    ppermute x6, waiting for transfers between devices, z_ring(): back = lax.ppermute(back, 'dp', z_shift(-1, nz))  68.1 us
    all_to_all x1, waiting for transfers between devices, local(): lax.all_to_all(hidden, 'mp', 0, 0, tiled=True)  31.6 us
    ppermute x6, starting transfers between devices, z_ring(): back = lax.ppermute(back, 'dp', z_shift(-1, nz))  21.3 us
    unnamed x68, local copies, waits for them, and re-layouts  17 us
    all_to_all x1, blocking collectives, local(): lax.all_to_all(gate[:, :1, :], 'dp', 0, 0, tiled=True)  13.6 us
    pallas_call x1, Pallas kernels, local(): pl.pallas_call(slot_kernel, grid_spec=pltpu.PrefetchScalarGridSpec(num_sc...  13.3 us
    all_to_all x1, starting transfers between devices, local(): lax.all_to_all(jnp.broadcast_to(turned[None], (mp_count, tokens, block)),...  10.5 us
    dot_general x9, matrix products, local(): partial = partial + jnp.dot(features, piece, preferred_element_type=f32)  10.2 us
  transfers between devices with their start and end apart: 26, of which 10 were waited for; matrix products, arithmetic and copies ran while one was open for 18% of the time, Pallas kernels for 4%

profile of v1, /device:TPU:1, one launch (start us, length us, event | category | flops | bytes accessed | tf_op | source)
XLA Modules:
  0.0 299.6 jit_solution(4309805725492072589)
XLA Ops:
  0.6 6.5 %collective-permute-start.2 = (bf16[256,2432]{1,0:T(8,128)(2,1)}, bf16[256,2432]{1,0:T(8,128)(2,1)}, u32[]{:S(2)}, u32[]{:S(2)}) collective-permute-start(bf16[256,2432]{1,0:T(8,128)(2,1)} %param.14), channel_id=1, source_target_pairs={{0,224},{16,240},{32,0},{48,16},{64,32},{80,48},{96,64},{112,80},{... | collective-permute-start | bytes 3735560 | tf_op jit(solution)/shard_map/ppermute | solution.py:31
  12.8 20.7 %collective-permute-done.2 = bf16[256,2432]{1,0:T(8,128)(2,1)} collective-permute-done((bf16[256,2432]{1,0:T(8,128)(2,1)}, bf16[256,2432]{1,0:T(8,128)(2,1)}, u32[]{:S(2)}, u32[]{:S(2)}) %collective-permute-start.2) | collective-permute-done | bytes 1245216 | tf_op jit(solution)/shard_map/ppermute | solution.py:31
  33.5 3.4 %collective-permute-start.4 = (bf16[256,2432]{1,0:T(8,128)(2,1)}, bf16[256,2432]{1,0:T(8,128)(2,1)}, u32[]{:S(2)}, u32[]{:S(2)}) collective-permute-start(bf16[256,2432]{1,0:T(8,128)(2,1)} %collective-permute-done.2), channel_id=1, source_target_pairs={{0,224},{16,240},{32,0},{48,16},{64,32},{80,48},{96,64},{112,80},{... | collective-permute-start | bytes 3735560 | tf_op jit(solution)/shard_map/ppermute | solution.py:31
  41.1 21.2 %collective-permute-done.4 = bf16[256,2432]{1,0:T(8,128)(2,1)} collective-permute-done((bf16[256,2432]{1,0:T(8,128)(2,1)}, bf16[256,2432]{1,0:T(8,128)(2,1)}, u32[]{:S(2)}, u32[]{:S(2)}) %collective-permute-start.4) | collective-permute-done | bytes 1245216 | tf_op jit(solution)/shard_map/ppermute | solution.py:31
  62.3 3.4 %collective-permute-start.6 = (bf16[256,2432]{1,0:T(8,128)(2,1)}, bf16[256,2432]{1,0:T(8,128)(2,1)S(1)}, u32[]{:S(2)}, u32[]{:S(2)}) collective-permute-start(bf16[256,2432]{1,0:T(8,128)(2,1)} %collective-permute-done.4), channel_id=1, source_target_pairs={{0,224},{16,240},{32,0},{48,16},{64,32},{80,48},{96,64},{112,80},{... | collective-permute-start | bytes 3735560 | tf_op jit(solution)/shard_map/ppermute | solution.py:31
  71.9 26.3 %collective-permute-done.6 = bf16[256,2432]{1,0:T(8,128)(2,1)S(1)} collective-permute-done((bf16[256,2432]{1,0:T(8,128)(2,1)}, bf16[256,2432]{1,0:T(8,128)(2,1)S(1)}, u32[]{:S(2)}, u32[]{:S(2)}) %collective-permute-start.6) | collective-permute-done | bytes 1245216 | tf_op jit(solution)/shard_map/ppermute | solution.py:31
  98.2 3.4 %collective-permute-start.8 = (bf16[128,2432]{1,0:T(8,128)(2,1)S(1)}, bf16[128,2432]{1,0:T(8,128)(2,1)S(1)}, u32[]{:S(2)}, u32[]{:S(2)}) collective-permute-start(bf16[128,2432]{1,0:T(8,128)(2,1)S(1)} %slice.64), channel_id=1, source_target_pairs={{0,224},{16,240},{32,0},{48,16},{64,32},{80,48},{96,64},{112,80},{... | collective-permute-start | bytes 1867784 | tf_op jit(solution)/shard_map/ppermute | solution.py:36
  104.4 8.0 %collective-permute-done.8 = bf16[128,2432]{1,0:T(8,128)(2,1)S(1)} collective-permute-done((bf16[128,2432]{1,0:T(8,128)(2,1)S(1)}, bf16[128,2432]{1,0:T(8,128)(2,1)S(1)}, u32[]{:S(2)}, u32[]{:S(2)}) %collective-permute-start.8) | collective-permute-done | bytes 622624 | tf_op jit(solution)/shard_map/ppermute | solution.py:36
  112.9 4.9 %collective-permute-done.7 = bf16[128,2432]{1,0:T(8,128)(2,1)S(1)} collective-permute-done((bf16[128,2432]{1,0:T(8,128)(2,1)S(1)}, bf16[128,2432]{1,0:T(8,128)(2,1)S(1)}, u32[]{:S(2)}, u32[]{:S(2)}) %collective-permute-start.7) | collective-permute-done | bytes 622624 | tf_op jit(solution)/shard_map/ppermute | solution.py:35
  122.5 3.7 %collective-permute-start.9 = (f32[128,2432]{1,0:T(8,128)}, f32[128,2432]{1,0:T(8,128)}, u32[]{:S(2)}, u32[]{:S(2)}) collective-permute-start(f32[128,2432]{1,0:T(8,128)} %slice.66), channel_id=1, source_target_pairs={{0,16},{16,0},{32,48},{48,32},{64,80},{80,64},{96,112},{112,96},{1... | collective-permute-start | bytes 3735560 | tf_op jit(solution)/shard_map/ppermute | solution.py:141
  133.9 6.3 %collective-permute-done.14 = bf16[4,32,1664]{2,1,0:T(8,128)(2,1)} collective-permute-done((bf16[4,32,1664]{2,1,0:T(8,128)(2,1)}, bf16[4,32,1664]{2,1,0:T(8,128)(2,1)}, u32[]{:S(2)}, u32[]{:S(2)}) %collective-permute-start.14) | collective-permute-done | bytes 426016 | tf_op jit(solution)/shard_map/ppermute | solution.py:30
  145.5 6.8 %all-to-all-start = ((f32[16,4,128]{2,1,0:T(4,128)}), f32[16,4,128]{2,1,0:T(4,128)S(1)}, u32[]{:S(2)}, u32[]{:S(2)}) async-start(f32[16,4,128]{2,1,0:T(4,128)} %broadcast_in_dim.131), calls=%async_computation | async-start | bytes 65536 | tf_op jit(solution)/shard_map/all_to_all | solution.py:152
  154.3 4.4 %all-to-all-done = f32[16,4,128]{2,1,0:T(4,128)S(1)} async-done(((f32[16,4,128]{2,1,0:T(4,128)}), f32[16,4,128]{2,1,0:T(4,128)S(1)}, u32[]{:S(2)}, u32[]{:S(2)}) %all-to-all-start) | async-done | bytes 32800 | tf_op jit(solution)/shard_map/all_to_all | solution.py:152
  184.2 3.8 %all-to-all-start.1 = ((f32[16,128,256]{2,1,0:T(8,128)}), f32[16,128,256]{2,1,0:T(8,128)S(1)}, u32[]{:S(2)}, u32[]{:S(2)}) async-start(f32[16,128,256]{2,1,0:T(8,128)} %bitcast.127), calls=%async_computation.1 | async-start | bytes 4194304 | tf_op jit(solution)/shard_map/all_to_all | solution.py:187
  190.3 31.6 %all-to-all-done.1 = f32[16,128,256]{2,1,0:T(8,128)S(1)} async-done(((f32[16,128,256]{2,1,0:T(8,128)}), f32[16,128,256]{2,1,0:T(8,128)S(1)}, u32[]{:S(2)}, u32[]{:S(2)}) %all-to-all-start.1) | async-done | bytes 2097184 | tf_op jit(solution)/shard_map/all_to_all | solution.py:187
  225.7 4.5 %collective-permute-done.21 = bf16[128,256]{1,0:T(8,128)(2,1)S(1)} collective-permute-done((bf16[128,256]{1,0:T(8,128)(2,1)S(1)}, bf16[128,256]{1,0:T(8,128)(2,1)S(1)}, u32[]{:S(2)}, u32[]{:S(2)}) %collective-permute-start.21) | collective-permute-done | bytes 65568 | tf_op jit(solution)/shard_map/ppermute | solution.py:195
  231.3 10.5 %all-to-all-start.2 = ((bf16[16,128,256]{2,1,0:T(8,128)(2,1)}), bf16[16,128,256]{2,1,0:T(8,128)(2,1)S(1)}, u32[]{:S(2)}, u32[]{:S(2)}) async-start(bf16[16,128,256]{2,1,0:T(8,128)(2,1)} %broadcast_in_dim.142), calls=%async_computation.2 | async-start | bytes 2097152 | tf_op jit(solution)/shard_map/all_to_all | solution.py:200
  242.4 4.2 %constant_dynamic-update-slice_fusion.14.acts_ref.side_ref = bf16[16,4,32,1664]{3,2,1,0:T(8,128)(2,1)} fusion(bf16[16,4,32,1664]{3,2,1,0:T(8,128)(2,1)} %get-tuple-element.28, bf16[8,4,32,1664]{3,2,1,0:T(8,128)(2,1)} %collective-permute-done.20), kind=kLoop, calls=%fused_computation.106 | loop fusion | bytes 6815744 | tf_op jit(solution)/shard_map/concatenate | solution.py:208
  246.6 4.8 %shard_map.139.proj_ref = f32[4,16,32,256]{3,2,1,0:T(8,128)S(1)} custom-call(bf16[16,4,32,1664]{3,2,1,0:T(8,128)(2,1)} %constant_dynamic-update-slice_fusion.14.acts_ref.side_ref, bf16[4,1536,256]{2,1,0:T(8,128)(2,1)S(1)} %copy-done.1), custom_call_target="tpu_custom_call" | custom-call | tf_op jit(solution)/shard_map/pallas_call | solution.py:214
  252.7 4.1 %all-to-all-done.2.rows_ref = bf16[16,128,256]{2,1,0:T(8,128)(2,1)S(1)} async-done(((bf16[16,128,256]{2,1,0:T(8,128)(2,1)}), bf16[16,128,256]{2,1,0:T(8,128)(2,1)S(1)}, u32[]{:S(2)}, u32[]{:S(2)}) %all-to-all-start.2) | async-done | bytes 1048608 | tf_op jit(solution)/shard_map/all_to_all | solution.py:200
  257.9 13.3 %shard_map.140 = (bf16[4,16,32,256]{3,2,1,0:T(8,128)(2,1)}, f32[16,8,128]{2,1,0:T(8,128)}) custom-call(s32[16]{0:T(128)} %pad_add_fusion.place_ref.group_ref, s32[16]{0:T(128)} %pad_add_fusion.place_ref.group_ref, bf16[16,4,32,1664]{3,2,1,0:T(8,128)(2,1)} %constant_dynamic-update-slice_fusion.14.acts_ref.side_ref, bf16[16,128,256]{2,1,0:T(8,128)(2,1)} %copy-done.6, ...), custom_call_target="tpu_custom_call" | custom-call | tf_op jit(solution)/shard_map/pallas_call | solution.py:225
  272.1 13.6 %all_to_all.25 = f32[16,1,128]{2,1,0:T(1,128)S(1)} all-to-all(f32[16,1,128]{2,1,0:T(1,128)S(1)} %slice.60), channel_id=1, replica_groups=mesh['dp'=16,'mp'=16] {'dp'}, dimensions={0} | all-to-all | bytes 16384 | tf_op jit(solution)/shard_map/all_to_all | solution.py:261
  286.3 3.4 %all-to-all-start.4 = ((f32[16,1,128]{2,1,0:T(1,128)}), f32[16,1,128]{2,1,0:T(1,128)S(1)}, u32[]{:S(2)}, u32[]{:S(2)}) async-start(f32[16,1,128]{2,1,0:T(1,128)} %broadcast_in_dim.143), calls=%async_computation.4 | async-start | bytes 16384 | tf_op jit(solution)/shard_map/all_to_all | solution.py:263
  291.0 6.3 %shard_map.141 = bf16[4,1536,256]{2,1,0:T(8,128)(2,1)} custom-call(bf16[16,4,32,1664]{3,2,1,0:T(8,128)(2,1)} %constant_dynamic-update-slice_fusion.14.acts_ref.side_ref, bf16[4,16,32,256]{3,2,1,0:T(8,128)(2,1)S(1)} %copy-done.2), custom_call_target="tpu_custom_call" | custom-call | tf_op jit(solution)/shard_map/pallas_call | solution.py:248
  (182 shorter events, 79.1 us)
Async XLA Ops:
  0.6 32.8 %collective-permute-start.2 = (bf16[256,2432]{1,0:T(8,128)(2,1)}, bf16[256,2432]{1,0:T(8,128)(2,1)}, u32[]{:S(2)}, u32[]{:S(2)}) collective-permute-start(bf16[256,2432]{1,0:T(8,128)(2,1)} %param.14), channel_id=1, source_target_pairs={{0,224},{16,240},{32,0},{48,16},{64,32},{80,48},{96,64},{112,80},{... | collective-permute-start | bytes 3735560 | tf_op jit(solution)/shard_map/ppermute | solution.py:31
  7.1 30.0 %collective-permute-start.1 = (bf16[256,2432]{1,0:T(8,128)(2,1)}, bf16[256,2432]{1,0:T(8,128)(2,1)}, u32[]{:S(2)}, u32[]{:S(2)}) collective-permute-start(bf16[256,2432]{1,0:T(8,128)(2,1)} %param.14), channel_id=1, source_target_pairs={{0,32},{16,48},{32,64},{48,80},{64,96},{80,112},{96,128},{112,144}... | collective-permute-start | bytes 3735560 | tf_op jit(solution)/shard_map/ppermute | solution.py:30
  11.1 29.9 %collective-permute-start = (bf16[8,128,256]{1,2,0:T(8,128)(2,1)S(1)}, bf16[8,128,256]{1,2,0:T(8,128)(2,1)S(1)}, u32[]{:S(2)}, u32[]{:S(2)}) collective-permute-start(bf16[8,128,256]{1,2,0:T(8,128)(2,1)S(1)} %get-tuple-element.25), channel_id=1, source_target_pairs={{0,16},{16,0},{32,48},{48,32},{64,80},{80,64},{96,112},{112,96},{1... | collective-permute-start | bytes 1572872 | tf_op jit(solution)/shard_map/ppermute | solution.py:110
  33.5 28.8 %collective-permute-start.4 = (bf16[256,2432]{1,0:T(8,128)(2,1)}, bf16[256,2432]{1,0:T(8,128)(2,1)}, u32[]{:S(2)}, u32[]{:S(2)}) collective-permute-start(bf16[256,2432]{1,0:T(8,128)(2,1)} %collective-permute-done.2), channel_id=1, source_target_pairs={{0,224},{16,240},{32,0},{48,16},{64,32},{80,48},{96,64},{112,80},{... | collective-permute-start | bytes 3735560 | tf_op jit(solution)/shard_map/ppermute | solution.py:31
  37.1 30.5 %collective-permute-start.3 = (bf16[256,2432]{1,0:T(8,128)(2,1)}, bf16[256,2432]{1,0:T(8,128)(2,1)}, u32[]{:S(2)}, u32[]{:S(2)}) collective-permute-start(bf16[256,2432]{1,0:T(8,128)(2,1)} %collective-permute-done.1), channel_id=1, source_target_pairs={{0,32},{16,48},{32,64},{48,80},{64,96},{80,112},{96,128},{112,144}... | collective-permute-start | bytes 3735560 | tf_op jit(solution)/shard_map/ppermute | solution.py:30
  38.2 89.0 %collective-permute-start.12 = (bf16[4,32,1664]{2,1,0:T(8,128)(2,1)}, bf16[4,32,1664]{2,1,0:T(8,128)(2,1)}, u32[]{:S(2)}, u32[]{:S(2)}) collective-permute-start(bf16[4,32,1664]{2,1,0:T(8,128)(2,1)} %pad_maximum_fusion.1), channel_id=1, source_target_pairs={{0,32},{16,48},{32,64},{48,80},{64,96},{80,112},{96,128},{112,144}... | collective-permute-start | bytes 1277960 | tf_op jit(solution)/shard_map/ppermute | solution.py:30
  38.3 89.0 %collective-permute-start.13 = (bf16[4,32,1664]{2,1,0:T(8,128)(2,1)}, bf16[4,32,1664]{2,1,0:T(8,128)(2,1)}, u32[]{:S(2)}, u32[]{:S(2)}) collective-permute-start(bf16[4,32,1664]{2,1,0:T(8,128)(2,1)} %pad_maximum_fusion.1), channel_id=1, source_target_pairs={{0,224},{16,240},{32,0},{48,16},{64,32},{80,48},{96,64},{112,80},{... | collective-permute-start | bytes 1277960 | tf_op jit(solution)/shard_map/ppermute | solution.py:31
  62.3 35.8 %collective-permute-start.6 = (bf16[256,2432]{1,0:T(8,128)(2,1)}, bf16[256,2432]{1,0:T(8,128)(2,1)S(1)}, u32[]{:S(2)}, u32[]{:S(2)}) collective-permute-start(bf16[256,2432]{1,0:T(8,128)(2,1)} %collective-permute-done.4), channel_id=1, source_target_pairs={{0,224},{16,240},{32,0},{48,16},{64,32},{80,48},{96,64},{112,80},{... | collective-permute-start | bytes 3735560 | tf_op jit(solution)/shard_map/ppermute | solution.py:31
  67.6 35.9 %collective-permute-start.5 = (bf16[256,2432]{1,0:T(8,128)(2,1)}, bf16[256,2432]{1,0:T(8,128)(2,1)S(1)}, u32[]{:S(2)}, u32[]{:S(2)}) collective-permute-start(bf16[256,2432]{1,0:T(8,128)(2,1)} %collective-permute-done.3), channel_id=1, source_target_pairs={{0,32},{16,48},{32,64},{48,80},{64,96},{80,112},{96,128},{112,144}... | collective-permute-start | bytes 3735560 | tf_op jit(solution)/shard_map/ppermute | solution.py:30
  98.2 14.2 %collective-permute-start.8 = (bf16[128,2432]{1,0:T(8,128)(2,1)S(1)}, bf16[128,2432]{1,0:T(8,128)(2,1)S(1)}, u32[]{:S(2)}, u32[]{:S(2)}) collective-permute-start(bf16[128,2432]{1,0:T(8,128)(2,1)S(1)} %slice.64), channel_id=1, source_target_pairs={{0,224},{16,240},{32,0},{48,16},{64,32},{80,48},{96,64},{112,80},{... | collective-permute-start | bytes 1867784 | tf_op jit(solution)/shard_map/ppermute | solution.py:36
  103.6 14.2 %collective-permute-start.7 = (bf16[128,2432]{1,0:T(8,128)(2,1)S(1)}, bf16[128,2432]{1,0:T(8,128)(2,1)S(1)}, u32[]{:S(2)}, u32[]{:S(2)}) collective-permute-start(bf16[128,2432]{1,0:T(8,128)(2,1)S(1)} %slice.62), channel_id=1, source_target_pairs={{0,32},{16,48},{32,64},{48,80},{64,96},{80,112},{96,128},{112,144}... | collective-permute-start | bytes 1867784 | tf_op jit(solution)/shard_map/ppermute | solution.py:35
  122.5 20.3 %collective-permute-start.9 = (f32[128,2432]{1,0:T(8,128)}, f32[128,2432]{1,0:T(8,128)}, u32[]{:S(2)}, u32[]{:S(2)}) collective-permute-start(f32[128,2432]{1,0:T(8,128)} %slice.66), channel_id=1, source_target_pairs={{0,16},{16,0},{32,48},{48,32},{64,80},{80,64},{96,112},{112,96},{1... | collective-permute-start | bytes 3735560 | tf_op jit(solution)/shard_map/ppermute | solution.py:141
  127.2 12.9 %collective-permute-start.14 = (bf16[4,32,1664]{2,1,0:T(8,128)(2,1)}, bf16[4,32,1664]{2,1,0:T(8,128)(2,1)}, u32[]{:S(2)}, u32[]{:S(2)}) collective-permute-start(bf16[4,32,1664]{2,1,0:T(8,128)(2,1)} %collective-permute-done.12), channel_id=1, source_target_pairs={{0,32},{16,48},{32,64},{48,80},{64,96},{80,112},{96,128},{112,144}... | collective-permute-start | bytes 1277960 | tf_op jit(solution)/shard_map/ppermute | solution.py:30
  127.2 12.9 %collective-permute-start.15 = (bf16[4,32,1664]{2,1,0:T(8,128)(2,1)}, bf16[4,32,1664]{2,1,0:T(8,128)(2,1)}, u32[]{:S(2)}, u32[]{:S(2)}) collective-permute-start(bf16[4,32,1664]{2,1,0:T(8,128)(2,1)} %collective-permute-done.13), channel_id=1, source_target_pairs={{0,224},{16,240},{32,0},{48,16},{64,32},{80,48},{96,64},{112,80},{... | collective-permute-start | bytes 1277960 | tf_op jit(solution)/shard_map/ppermute | solution.py:31
  140.2 24.9 %collective-permute-start.16 = (bf16[4,32,1664]{2,1,0:T(8,128)(2,1)}, bf16[4,32,1664]{2,1,0:T(8,128)(2,1)S(1)}, u32[]{:S(2)}, u32[]{:S(2)}) collective-permute-start(bf16[4,32,1664]{2,1,0:T(8,128)(2,1)} %collective-permute-done.14), channel_id=1, source_target_pairs={{0,32},{16,48},{32,64},{48,80},{64,96},{80,112},{96,128},{112,144}... | collective-permute-start | bytes 1277960 | tf_op jit(solution)/shard_map/ppermute | solution.py:30
  140.2 24.8 %collective-permute-start.17 = (bf16[4,32,1664]{2,1,0:T(8,128)(2,1)}, bf16[4,32,1664]{2,1,0:T(8,128)(2,1)S(1)}, u32[]{:S(2)}, u32[]{:S(2)}) collective-permute-start(bf16[4,32,1664]{2,1,0:T(8,128)(2,1)} %collective-permute-done.15), channel_id=1, source_target_pairs={{0,224},{16,240},{32,0},{48,16},{64,32},{80,48},{96,64},{112,80},{... | collective-permute-start | bytes 1277960 | tf_op jit(solution)/shard_map/ppermute | solution.py:31
  145.5 13.2 %all-to-all-start = ((f32[16,4,128]{2,1,0:T(4,128)}), f32[16,4,128]{2,1,0:T(4,128)S(1)}, u32[]{:S(2)}, u32[]{:S(2)}) async-start(f32[16,4,128]{2,1,0:T(4,128)} %broadcast_in_dim.131), calls=%async_computation | async-start | bytes 65536 | tf_op jit(solution)/shard_map/all_to_all | solution.py:152
  160.1 7.8 %collective-permute-start.10 = (bf16[128,2432]{1,0:T(8,128)(2,1)S(1)}, bf16[128,2432]{1,0:T(8,128)(2,1)S(1)}, u32[]{:S(2)}, u32[]{:S(2)}) collective-permute-start(bf16[128,2432]{1,0:T(8,128)(2,1)S(1)} %multiply_convert_fusion.1), channel_id=1, source_target_pairs={{0,16},{16,0},{32,48},{48,32},{64,80},{80,64},{96,112},{112,96},{1... | collective-permute-start | bytes 1867784 | tf_op jit(solution)/shard_map/ppermute | solution.py:169
  165.0 15.8 %collective-permute-start.19 = (bf16[2,32,1664]{2,1,0:T(8,128)(2,1)S(1)}, bf16[2,32,1664]{2,1,0:T(8,128)(2,1)S(1)}, u32[]{:S(2)}, u32[]{:S(2)}) collective-permute-start(bf16[2,32,1664]{2,1,0:T(8,128)(2,1)S(1)} %slice.72), channel_id=1, source_target_pairs={{0,224},{16,240},{32,0},{48,16},{64,32},{80,48},{96,64},{112,80},{... | collective-permute-start | bytes 638984 | tf_op jit(solution)/shard_map/ppermute | solution.py:36
  165.1 15.7 %collective-permute-start.18 = (bf16[2,32,1664]{2,1,0:T(8,128)(2,1)S(1)}, bf16[2,32,1664]{2,1,0:T(8,128)(2,1)S(1)}, u32[]{:S(2)}, u32[]{:S(2)}) collective-permute-start(bf16[2,32,1664]{2,1,0:T(8,128)(2,1)S(1)} %slice.71), channel_id=1, source_target_pairs={{0,32},{16,48},{32,64},{48,80},{64,96},{80,112},{96,128},{112,144}... | collective-permute-start | bytes 638984 | tf_op jit(solution)/shard_map/ppermute | solution.py:35
  181.8 60.6 %collective-permute-start.20 = (bf16[8,4,32,1664]{3,2,1,0:T(8,128)(2,1)}, bf16[8,4,32,1664]{3,2,1,0:T(8,128)(2,1)}, u32[]{:S(2)}, u32[]{:S(2)}) collective-permute-start(bf16[8,4,32,1664]{3,2,1,0:T(8,128)(2,1)} %get-tuple-element.27), channel_id=1, source_target_pairs={{0,16},{16,0},{32,48},{48,32},{64,80},{80,64},{96,112},{112,96},{1... | collective-permute-start | bytes 10223624 | tf_op jit(solution)/shard_map/ppermute | solution.py:208
  184.2 37.8 %all-to-all-start.1 = ((f32[16,128,256]{2,1,0:T(8,128)}), f32[16,128,256]{2,1,0:T(8,128)S(1)}, u32[]{:S(2)}, u32[]{:S(2)}) async-start(f32[16,128,256]{2,1,0:T(8,128)} %bitcast.127), calls=%async_computation.1 | async-start | bytes 4194304 | tf_op jit(solution)/shard_map/all_to_all | solution.py:187
  231.3 25.5 %all-to-all-start.2 = ((bf16[16,128,256]{2,1,0:T(8,128)(2,1)}), bf16[16,128,256]{2,1,0:T(8,128)(2,1)S(1)}, u32[]{:S(2)}, u32[]{:S(2)}) async-start(bf16[16,128,256]{2,1,0:T(8,128)(2,1)} %broadcast_in_dim.142), calls=%async_computation.2 | async-start | bytes 2097152 | tf_op jit(solution)/shard_map/all_to_all | solution.py:200
  286.3 10.9 %all-to-all-start.4 = ((f32[16,1,128]{2,1,0:T(1,128)}), f32[16,1,128]{2,1,0:T(1,128)S(1)}, u32[]{:S(2)}, u32[]{:S(2)}) async-start(f32[16,1,128]{2,1,0:T(1,128)} %broadcast_in_dim.143), calls=%async_computation.4 | async-start | bytes 16384 | tf_op jit(solution)/shard_map/all_to_all | solution.py:263
  (30 other events, 337.5 us)

commit v2 on v1

--- a/solution.py
+++ b/solution.py
@@ -38,6 +38,37 @@
     return pieces
 
 
+def x_shift(step):
+    return [(4 * y + x, 4 * y + (x + step) % 4) for y in range(4) for x in range(4)]
+
+
+def y_shift(step):
+    return [(4 * y + x, 4 * ((y + step) % 4) + x) for y in range(4) for x in range(4)]
+
+
+def x_stage(nz, flip, far):
+    pairs = []
+    for z in range(nz):
+        for core in range(2):
+            for y in range(4):
+                for high in range(2):
+                    for low in range(2):
+                        source = (2 * z + core) * 16 + 4 * y + 2 * high + low
+                        target = (2 * z + (low ^ flip)) * 16 + 4 * y + 2 * (high ^ far) + core
+                        pairs.append((source, target))
+    return pairs
+
+
+def y_stage(step):
+    pairs = []
+    for group in range(16):
+        for y in range(4):
+            for x in range(4):
+                target = (4 * ((y + step) % 4) + x) * 16 + group
+                pairs.append((group * 16 + 4 * y + x, target))
+    return pairs
+
+
 def proj_kernel(acts_ref, down_ref, proj_ref):
     groups, _, slots, wide = acts_ref.shape
     width = down_ref.shape[1]
@@ -46,22 +77,57 @@
     proj_ref[...] = out.reshape(proj_ref.shape)
 
 
-def slot_kernel(place_ref, group_ref, side_ref, rows_ref, proj_ref, weighted_ref, gate_ref):
-    per_expert, slots, _ = side_ref.shape[1:]
-    side = side_ref[0].reshape(per_expert * slots, lanes).astype(f32)
-    weight = side[:, 0:1]
-    token = side[:, 1:2]
-    tokens = rows_ref.shape[1]
-    column = lax.broadcasted_iota(jnp.int32, (per_expert * slots, tokens), 1).astype(f32)
-    match = jnp.where(column == token, 1.0, 0.0).astype(bf16)
-    rows = jnp.dot(match, rows_ref[0], preferred_element_type=f32)
-    proj = proj_ref[:, 0].reshape(rows.shape)
-    ones = jnp.ones((8, rows.shape[1]), f32)
-    gate_ref[0] = lax.dot_general(
-        ones, rows * proj, (((1,), (1,)), ((), ())),
-        precision=lax.Precision.HIGHEST, preferred_element_type=f32,
-    )
-    weighted_ref[:, 0] = (weight * rows).astype(bf16).reshape(per_expert, slots, rows.shape[1])
+def slot_kernel(group_ref, side_ref, rows0, rows1, rows2, rows3, proj_ref, weighted_ref, gate_ref):
+    groups, per_expert, slots, _ = side_ref.shape
+    tokens, width = rows0.shape[1:]
+    count = per_expert * slots
+    column = lax.broadcasted_iota(jnp.int32, (count, tokens), 1)
+    gates = jnp.zeros((count, lanes), f32)
+    for place in range(groups):
+        group = group_ref[place]
+        rows_ref = (rows0, rows1, rows2, rows3)[place // 4]
+        side = side_ref[group].reshape(count, lanes).astype(f32)
+        match = jnp.where(column.astype(f32) == side[:, 1:2], 1.0, 0.0).astype(bf16)
+        rows = jnp.dot(match, rows_ref[place % 4], preferred_element_type=f32)
+        proj = proj_ref[:, group].reshape(count, width)
+        gate = jnp.sum(rows * proj, axis=1, keepdims=True)
+        gates = jnp.where(column == group, gate, gates)
+        weighted = (side[:, 0:1] * rows).astype(bf16)
+        weighted_ref[:, group] = weighted.reshape(per_expert, slots, width)
+    gate_ref[...] = gates.T[:groups]
+
+
+def hidden_kernel(nz, place_ref, grad_ref, *refs):
+    count = nz + 1
+    pieces, out_ref, held, sems = refs[:count], refs[count], refs[count + 1], refs[count + 2]
+    z_index, core, x_high, x_low = [place_ref[i] for i in range(4)]
+    copies = []
+    half = pieces[0].shape[0] // 2
+    for number, piece in enumerate(pieces):
+        target = held.at[number]
+        if number >= nz - 1:
+            first = half * (number - nz + 1)
+            target = held.at[nz - 1, first : first + half]
+        copies.append(pltpu.make_async_copy(piece, target, sems.at[number]))
+        copies[-1].start()
+    tokens = grad_ref.shape[0] // 2
+    grad = grad_ref[...]
+    for number in range(nz):
+        copies[number].wait()
+        if number == nz - 1:
+            copies[nz].wait()
+        step = (number + 1) // 2
+        offset = step if number % 2 == 0 else nz - step
+        if number == nz - 1:
+            offset = nz // 2
+        part = lax.dot_general(
+            grad, held[number], (((1,), (1,)), ((), ())), preferred_element_type=f32
+        )
+        block = lax.rem(z_index + offset, nz)
+        far_x = lax.rem(block % 2 + x_high, 2)
+        own = lax.rem(core + x_low, 2)
+        out_ref[own, far_x, block // 2] = part[:tokens]
+        out_ref[1 - own, far_x, block // 2] = part[tokens:]
 
 
 def down_kernel(acts_ref, weighted_ref, out_ref):
@@ -96,6 +162,10 @@
     dp_index = lax.axis_index("dp")
     mp_index = lax.axis_index("mp")
     z_index, core = dp_index // 2, dp_index % 2
+    y_index, x_index = mp_index // 4, mp_index % 4
+    x_high, x_low = x_index // 2, x_index % 2
+    both = ("dp", "mp")
+    turn = [(p * mp_count + q, q * mp_count + p) for p in range(dp_count) for q in range(mp_count)]
     experts_all = per_expert * mp_count
     swap = functools.partial(lax.ppermute, axis_name="dp", perm=core_swap(nz))
 
@@ -108,6 +178,10 @@
     mine = lax.dynamic_index_in_dim(by_block, core, 0, keepdims=False)
     theirs = lax.dynamic_index_in_dim(by_block, 1 - core, 0, keepdims=False)
     chip_normed = jnp.concatenate([mine, swap(theirs)], axis=1)
+
+    turned_stream = lax.ppermute(
+        lax.dynamic_slice_in_dim(residual, mp_index * block, block, 1), both, turn
+    )
 
     expert_ids = jnp.arange(experts_all, dtype=jnp.int32)
     hit_routes = routes[:, :, None] == expert_ids[None, None, :]
@@ -132,13 +206,22 @@
     ).astype(bf16)
     acts_block = jnp.concatenate([expert_acts[:, 0], side], axis=2)
 
-    partial = jnp.zeros((2 * tokens, vocab_dev), f32)
-    for offset, first, piece in head_pieces:
-        features = lax.dynamic_index_in_dim(
+    def features_of(offset, first, piece):
+        return lax.dynamic_index_in_dim(
             chip_normed, lax.rem(z_index + offset, nz), 0, keepdims=False
         )[:, first : first + piece.shape[0]]
-        partial = partial + jnp.dot(features, piece, preferred_element_type=f32)
-    logits = partial[:tokens] + swap(partial[tokens:])
+
+    partial = jnp.zeros((2 * tokens, vocab_dev), f32)
+    for offset, first, piece in head_pieces[:-2]:
+        partial = partial + jnp.dot(
+            features_of(offset, first, piece), piece, preferred_element_type=f32
+        )
+    own_part, other_part = partial[:tokens], partial[tokens:]
+    for offset, first, piece in head_pieces[-2:]:
+        features = features_of(offset, first, piece)
+        other_part = other_part + jnp.dot(features[tokens:], piece, preferred_element_type=f32)
+        own_part = own_part + jnp.dot(features[:tokens], piece, preferred_element_type=f32)
+    logits = own_part + swap(other_part)
 
     local_ids = token_ids - mp_index * vocab_dev
     column = jnp.arange(vocab_dev, dtype=jnp.int32)
@@ -162,53 +245,59 @@
     prob_ratio = jnp.exp(logp - old_logp)
     weight_row = -jnp.clip(prob_ratio, clip_low, clip_high) * advantages * resp_mask.astype(f32)
     inner = weight_row * (picked - mean_logit) / model_width
+    turned_rows = lax.ppermute(jnp.stack([inv_rms[:, 0], inner]), both, turn)
     logit_grad = (
         weight_row[:, None]
         * (onehot.astype(f32) - jnp.exp(logits - row_top[:, None]) / row_total[:, None])
     ).astype(bf16)
     chip_grad = jnp.concatenate([logit_grad, swap(logit_grad)], axis=0)
 
-    parts = []
-    for offset, first, piece in head_pieces:
-        parts.append(
-            lax.dot_general(
-                chip_grad, piece, (((1,), (1,)), ((), ())), preferred_element_type=f32
-            )
-        )
-    parts = parts[:1] + parts[2:-2:2] + [jnp.concatenate(parts[-2:], axis=1)] + parts[-4:0:-2]
-    by_offset = jnp.stack(parts)
-    hidden = jnp.roll(by_offset, z_index, axis=0)
-    own_part, other_part = hidden[:, :tokens], swap(hidden[:, tokens:])
-    hidden = jnp.where(
-        core == 0,
-        jnp.stack([own_part, other_part], axis=1),
-        jnp.stack([other_part, own_part], axis=1),
-    ).reshape(mp_count, tokens, block)
-    hidden_grad = jnp.sum(lax.all_to_all(hidden, "mp", 0, 0, tiled=True), axis=0)
-
-    my_stream = lax.dynamic_slice_in_dim(stream, mp_index * block, block, 1)
-    my_gain = lax.dynamic_slice_in_dim(norm_gain, mp_index * block, block, 0)
+    place = jnp.stack([z_index, core, x_high, x_low]).astype(jnp.int32)
+    hidden = pl.pallas_call(
+        functools.partial(hidden_kernel, nz),
+        grid_spec=pltpu.PrefetchScalarGridSpec(
+            num_scalar_prefetch=1,
+            grid=(1,),
+            in_specs=[pl.BlockSpec((2 * tokens, vocab_dev), lambda n, place: (0, 0))]
+            + [pl.BlockSpec(memory_space=pl.ANY)] * (nz + 1),
+            out_specs=pl.BlockSpec((2, 2, 4, tokens, block), lambda n, place: (0, 0, 0, 0, 0)),
+            scratch_shapes=[
+                pltpu.VMEM((nz, block, vocab_dev), bf16),
+                pltpu.SemaphoreType.DMA((nz + 1,)),
+            ],
+        ),
+        out_shape=jax.ShapeDtypeStruct((2, 2, 4, tokens, block), f32),
+        compiler_params=pltpu.CompilerParams(vmem_limit_bytes=40 * 1024 * 1024),
+    )(place, chip_grad, *[piece for _, _, piece in head_pieces])
+
+    rows_sum = None
+    for flip in range(2):
+        for far in range(2):
+            moved = lax.ppermute(hidden[flip, far], both, x_stage(nz, flip, far))
+            rows_sum = moved if rows_sum is None else rows_sum + moved
+    hidden_grad = None
+    for step in range(4):
+        sent = lax.dynamic_index_in_dim(rows_sum, lax.rem(y_index + step, 4), 0, keepdims=False)
+        moved = lax.ppermute(sent, both, y_stage(step))
+        hidden_grad = moved if hidden_grad is None else hidden_grad + moved
+
+    my_gain = lax.dynamic_slice_in_dim(norm_gain, dp_index * block, block, 0)
+    turned_rms, turned_inner = turned_rows[0][:, None], turned_rows[1][:, None]
     scaled_grad = my_gain[None, :] * hidden_grad
-    resid_grad = inv_rms * (scaled_grad - my_stream * inv_rms * inner[:, None])
-    stream_grad = resid_grad.astype(bf16)
-
-    turned = lax.ppermute(
-        stream_grad,
-        ("dp", "mp"),
-        [(p * mp_count + q, q * mp_count + p) for p in range(dp_count) for q in range(mp_count)],
-    )
-    all_rows = lax.all_to_all(
-        jnp.broadcast_to(turned[None], (mp_count, tokens, block)), "mp", 0, 0, tiled=True
-    )
-
-    pieces = z_ring(acts_block, nz)
-    acts_list = [p for _, _, p in pieces[:-2]] + [jnp.concatenate([pieces[-2][2], pieces[-1][2]], axis=0)]
-    offsets = [o for o, _, _ in pieces[:-1]]
-    acts_own = jnp.stack(acts_list)
-    acts_all = jnp.concatenate([acts_own, swap(acts_own)], axis=0)
-    offsets = jnp.array(offsets, jnp.int32)
-    z_of = lax.rem(z_index + offsets, nz)
-    group_of = jnp.concatenate([2 * z_of + core, 2 * z_of + 1 - core]).astype(jnp.int32)
+    turned_resid = turned_rms * (
+        scaled_grad - turned_stream.astype(f32) * turned_rms * turned_inner
+    )
+    stream_grad = turned_resid.astype(bf16)
+    resid_grad = lax.ppermute(turned_resid, both, turn)
+
+    in_row = [stream_grad] + [lax.ppermute(stream_grad, "mp", x_shift(k)) for k in (1, 2, 3)]
+    in_row = jnp.stack(in_row)
+    all_rows = [in_row] + [lax.ppermute(in_row, "mp", y_shift(k)) for k in (1, 2, 3)]
+    steps = jnp.arange(16, dtype=jnp.int32)
+    group_of = 4 * lax.rem(y_index + 4 - steps // 4, 4) + lax.rem(x_index + 4 - steps % 4, 4)
+
+    acts_block, _ = lax.optimization_barrier((acts_block, (head_pieces[-1][2], head_pieces[-2][2])))
+    acts_all = lax.all_gather(acts_block, "dp", axis=0, tiled=False)
 
     wide = hidden_width + lanes
     proj = pl.pallas_call(
@@ -225,26 +314,27 @@
     weighted, gate = pl.pallas_call(
         slot_kernel,
         grid_spec=pltpu.PrefetchScalarGridSpec(
-            num_scalar_prefetch=2,
-            grid=(dp_count,),
+            num_scalar_prefetch=1,
+            grid=(1,),
             in_specs=[
                 pl.BlockSpec(
-                    (1, per_expert, capacity, lanes),
-                    lambda n, place, group: (n, 0, 0, hidden_width // lanes),
+                    (dp_count, per_expert, capacity, lanes),
+                    lambda n, group: (0, 0, 0, hidden_width // lanes),
                 ),
-                pl.BlockSpec((1, tokens, block), lambda n, place, group: (place[n], 0, 0)),
-                pl.BlockSpec((per_expert, 1, capacity, block), lambda n, place, group: (0, n, 0, 0)),
-            ],
+            ]
+            + [pl.BlockSpec((4, tokens, block), lambda n, group: (0, 0, 0))] * 4
+            + [pl.BlockSpec((per_expert, dp_count, capacity, block), lambda n, group: (0, 0, 0, 0))],
             out_specs=[
-                pl.BlockSpec((per_expert, 1, capacity, block), lambda n, place, group: (0, n, 0, 0)),
-                pl.BlockSpec((1, 8, per_expert * capacity), lambda n, place, group: (group[n], 0, 0)),
+                pl.BlockSpec((per_expert, dp_count, capacity, block), lambda n, group: (0, 0, 0, 0)),
+                pl.BlockSpec((dp_count, per_expert * capacity), lambda n, group: (0, 0)),
             ],
         ),
         out_shape=[
             jax.ShapeDtypeStruct((per_expert, dp_count, capacity, block), bf16),
-            jax.ShapeDtypeStruct((dp_count, 8, per_expert * capacity), f32),
+            jax.ShapeDtypeStruct((dp_count, per_expert * capacity), f32),
         ],
-    )(group_of, group_of, acts_all, all_rows, proj)
+        compiler_params=pltpu.CompilerParams(vmem_limit_bytes=32 * 1024 * 1024),
+    )(group_of.astype(jnp.int32), acts_all, *all_rows, proj)
     down_grad = pl.pallas_call(
         down_kernel,
         grid=(per_expert,),
@@ -258,7 +348,7 @@
     )(acts_all, weighted)
 
     group_gate = jnp.sum(
-        lax.all_to_all(gate[:, :1, :], "dp", 0, 0, tiled=True), axis=0, keepdims=True
+        lax.all_to_all(gate[:, None, :], "dp", 0, 0, tiled=True), axis=0, keepdims=True
     )
     slot_gate = lax.all_to_all(
         jnp.broadcast_to(group_gate, (mp_count, 1, per_expert * capacity)), "mp", 0, 0, tiled=True

time: 301 us -> 309 us (1.027)
  blocking collectives: 13.6 us -> 27.2 us
  between operations: 1.4 us -> 14.7 us
  waiting for transfers between devices: 132 us -> 119 us
  starting transfers between devices: 62.2 us -> 73.2 us
  local copies, waits for them, and re-layouts: 29.6 us -> 21.7 us
  Pallas kernels: 24.4 us -> 19.3 us
  matrix products: 20.2 us -> 16.6 us
    ppermute x4 -> x18, starting transfers between devices: 6.83 us -> 47 us  [the longest x3 18.7 us: local(): lax.ppermute(stream_grad, 'mp', x_shift(k))]
    all_to_all x3 -> x0, waiting for transfers between devices: 40.2 us -> none  [the longest x1 31.6 us: local(): lax.all_to_all(hidden, 'mp', 0, 0, tiled=True)]
    ppermute x4 -> x18, waiting for transfers between devices: 4.55 us -> 30.9 us  [the longest x4 21.1 us: local(): moved = lax.ppermute(hidden[flip, far], both, x_stage(nz, flip, far))]
    all_to_all x3 -> x0, starting transfers between devices: 21.1 us -> none  [the longest x1 10.5 us: local(): lax.all_to_all(jnp.broadcast_to(turned[None], (mp_count, tokens, block)),...]
    ppermute x6 -> x3, waiting for transfers between devices: 6.29 us -> 25.6 us  [z_ring(): ahead = lax.ppermute(ahead, 'dp', z_shift(1, nz))]
    ppermute x6 -> x3, waiting for transfers between devices: 68.1 us -> 50.4 us  [z_ring(): back = lax.ppermute(back, 'dp', z_shift(-1, nz))]
    all_to_all x1 -> x2, blocking collectives: 13.6 us -> 27.2 us  [the longest x1 14.1 us: local(): lax.all_to_all(gate[:, None, :], 'dp', 0, 0, tiled=True)]
    pallas_call x1, Pallas kernels: 13.3 us -> 3.07 us  [local(): pl.pallas_call(slot_kernel, grid_spec=pltpu.PrefetchScalarGridSpec(num_sc...]
  transfers between devices with their start and end apart: 26 -> 30, of which waited for: 10 -> 15; matrix products, arithmetic and copies ran while one was open for 18% -> 13% of each run, Pallas kernels for 4% -> 6%
where the time goes in v2:
time: 309 us; the launch traced here: 308 us
  waiting for transfers between devices  119 us (39%)
  starting transfers between devices  73.2 us (24%)
  blocking collectives  27.2 us (9%)
  local copies, waits for them, and re-layouts  21.7 us (7%)
  Pallas kernels  19.3 us (6%)
  matrix products  16.6 us (5%)
  other arithmetic  16 us (5%)
  between operations  14.7 us (5%)
    ppermute x3, waiting for transfers between devices, z_ring(): back = lax.ppermute(back, 'dp', z_shift(-1, nz))  50.4 us
    ppermute x3, waiting for transfers between devices, z_ring(): ahead = lax.ppermute(ahead, 'dp', z_shift(1, nz))  25.6 us
    ppermute x4, waiting for transfers between devices, local(): moved = lax.ppermute(hidden[flip, far], both, x_stage(nz, flip, far))  21.1 us
    ppermute x3, starting transfers between devices, local(): lax.ppermute(stream_grad, 'mp', x_shift(k))  18.7 us
    unnamed x50, local copies, waits for them, and re-layouts  15.2 us
    all_to_all x1, blocking collectives, local(): lax.all_to_all(gate[:, None, :], 'dp', 0, 0, tiled=True)  14.1 us
    ppermute x3, starting transfers between devices, z_ring(): back = lax.ppermute(back, 'dp', z_shift(-1, nz))  13.3 us
    all_to_all x1, blocking collectives, local(): lax.all_to_all(jnp.broadcast_to(stats[None], (mp_count, 4, tokens)), 'mp'...  13.1 us
  transfers between devices with their start and end apart: 30, of which 15 were waited for; matrix products, arithmetic and copies ran while one was open for 13% of the time, Pallas kernels for 6%

profile of v2, /device:TPU:1, one launch (start us, length us, event | category | flops | bytes accessed | tf_op | source)
XLA Modules:
  0.0 308.1 jit_solution(6081754891999504948)
XLA Ops:
  7.2 6.5 %collective-permute-start.2 = (bf16[256,2432]{1,0:T(8,128)(2,1)}, bf16[256,2432]{1,0:T(8,128)(2,1)S(1)}, u32[]{:S(2)}, u32[]{:S(2)}) collective-permute-start(bf16[256,2432]{1,0:T(8,128)(2,1)} %refs_0_.1), channel_id=1, source_target_pairs={{0,224},{16,240},{32,0},{48,16},{64,32},{80,48},{96,64},{112,80},{... | collective-permute-start | bytes 3735560 | tf_op jit(solution)/shard_map/ppermute | solution.py:31
  13.7 26.4 %collective-permute-done.2.refs_2_ = bf16[256,2432]{1,0:T(8,128)(2,1)S(1)} collective-permute-done((bf16[256,2432]{1,0:T(8,128)(2,1)}, bf16[256,2432]{1,0:T(8,128)(2,1)S(1)}, u32[]{:S(2)}, u32[]{:S(2)}) %collective-permute-start.2) | collective-permute-done | bytes 1245216 | tf_op jit(solution)/shard_map/ppermute | solution.py:31
  40.0 3.3 %collective-permute-start.4 = (bf16[256,2432]{1,0:T(8,128)(2,1)S(1)}, bf16[256,2432]{1,0:T(8,128)(2,1)}, u32[]{:S(2)}, u32[]{:S(2)}) collective-permute-start(bf16[256,2432]{1,0:T(8,128)(2,1)S(1)} %collective-permute-done.2.refs_2_), channel_id=1, source_target_pairs={{0,224},{16,240},{32,0},{48,16},{64,32},{80,48},{96,64},{112,80},{... | collective-permute-start | bytes 3735560 | tf_op jit(solution)/shard_map/ppermute | solution.py:31
  44.4 24.1 %collective-permute-done.4.refs_4_ = bf16[256,2432]{1,0:T(8,128)(2,1)} collective-permute-done((bf16[256,2432]{1,0:T(8,128)(2,1)S(1)}, bf16[256,2432]{1,0:T(8,128)(2,1)}, u32[]{:S(2)}, u32[]{:S(2)}) %collective-permute-start.4) | collective-permute-done | bytes 1245216 | tf_op jit(solution)/shard_map/ppermute | solution.py:31
  68.5 3.5 %collective-permute-start.6 = (bf16[256,2432]{1,0:T(8,128)(2,1)}, bf16[256,2432]{1,0:T(8,128)(2,1)S(1)}, u32[]{:S(2)}, u32[]{:S(2)}) collective-permute-start(bf16[256,2432]{1,0:T(8,128)(2,1)} %collective-permute-done.4.refs_4_), channel_id=1, source_target_pairs={{0,224},{16,240},{32,0},{48,16},{64,32},{80,48},{96,64},{112,80},{... | collective-permute-start | bytes 3735560 | tf_op jit(solution)/shard_map/ppermute | solution.py:31
  74.0 25.6 %collective-permute-done.5.refs_5_ = bf16[256,2432]{1,0:T(8,128)(2,1)S(1)} collective-permute-done((bf16[256,2432]{1,0:T(8,128)(2,1)}, bf16[256,2432]{1,0:T(8,128)(2,1)S(1)}, u32[]{:S(2)}, u32[]{:S(2)}) %collective-permute-start.5) | collective-permute-done | bytes 1245216 | tf_op jit(solution)/shard_map/ppermute | solution.py:30
  105.0 8.6 %collective-permute-done.7.refs_7_ = bf16[128,2432]{1,0:T(8,128)(2,1)S(1)} collective-permute-done((bf16[128,2432]{1,0:T(8,128)(2,1)}, bf16[128,2432]{1,0:T(8,128)(2,1)S(1)}, u32[]{:S(2)}, u32[]{:S(2)}) %collective-permute-start.7) | collective-permute-done | bytes 622624 | tf_op jit(solution)/shard_map/ppermute | solution.py:35
  119.7 4.9 %collective-permute-start = (bf16[8,128,256]{1,2,0:T(8,128)(2,1)}, bf16[8,128,256]{1,2,0:T(8,128)(2,1)}, u32[]{:S(2)}, u32[]{:S(2)}) collective-permute-start(bf16[8,128,256]{1,2,0:T(8,128)(2,1)} %get-tuple-element.24), channel_id=1, source_target_pairs={{0,16},{16,0},{32,48},{48,32},{64,80},{80,64},{96,112},{112,96},{1... | collective-permute-start | bytes 1572872 | tf_op jit(solution)/shard_map/ppermute | solution.py:180
  139.3 3.0 fusion.5
  149.1 13.1 %all_to_all.15 = f32[16,4,128]{2,1,0:T(4,128)S(1)} all-to-all(f32[16,4,128]{2,1,0:T(4,128)S(1)} %broadcast_in_dim.127), channel_id=1, replica_groups=mesh['dp'=16,'mp'=16] {'mp'}, dimensions={0} | all-to-all | bytes 65536 | tf_op jit(solution)/shard_map/all_to_all | solution.py:235
  171.6 9.3 %shard_map.130 = f32[2,2,4,128,256]{4,3,2,1,0:T(8,128)S(1)} custom-call(s32[4]{0:T(128)S(1)} %pad_add_fusion.place_ref, bf16[256,2432]{1,0:T(8,128)(2,1)S(1)} %pad_maximum_fusion.grad_ref, bf16[256,2432]{1,0:T(8,128)(2,1)S(1)} %copy-done.3, bf16[256,2432]{1,0:T(8,128)(2,1)S(1)} %copy-done.8, bf16[256,2432]{1,0:T(8,128)(2,1)S(1)} %copy-done.6, ...), custom_call_target="tpu_custom_call" | custom-call | tf_op jit(solution)/shard_map/pallas_call | solution.py:256
  190.9 12.8 %collective-permute-done.12 = f32[4,128,256]{2,1,0:T(8,128)S(1)} collective-permute-done((f32[4,128,256]{2,1,0:T(8,128)}, f32[4,128,256]{2,1,0:T(8,128)S(1)}, u32[]{:S(2)}, u32[]{:S(2)}) %collective-permute-start.12) | collective-permute-done | bytes 524320 | tf_op jit(solution)/shard_map/ppermute | solution.py:276
  205.6 6.2 %collective-permute-done.14 = f32[4,128,256]{2,1,0:T(8,128)S(1)} collective-permute-done((f32[4,128,256]{2,1,0:T(8,128)}, f32[4,128,256]{2,1,0:T(8,128)S(1)}, u32[]{:S(2)}, u32[]{:S(2)}) %collective-permute-start.14) | collective-permute-done | bytes 524320 | tf_op jit(solution)/shard_map/ppermute | solution.py:276
  214.1 3.9 %collective-permute-start.16 = (f32[128,256]{1,0:T(8,128)S(1)}, f32[128,256]{1,0:T(8,128)S(1)}, u32[]{:S(2)}, u32[]{:S(2)}) collective-permute-start(f32[128,256]{1,0:T(8,128)S(1)} %get-tuple-element.29), channel_id=1, source_target_pairs={{0,0},{1,16},{2,32},{3,48},{4,64},{5,80},{6,96},{7,112},{8,128},{9... | collective-permute-start | bytes 393224 | tf_op jit(solution)/shard_map/ppermute | solution.py:281
  220.6 3.8 %collective-permute-start.19 = (f32[128,256]{1,0:T(8,128)S(1)}, f32[128,256]{1,0:T(8,128)S(1)}, u32[]{:S(2)}, u32[]{:S(2)}) collective-permute-start(f32[128,256]{1,0:T(8,128)S(1)} %get-tuple-element.27), channel_id=1, source_target_pairs={{0,192},{1,208},{2,224},{3,240},{4,0},{5,16},{6,32},{7,48},{8,64},... | collective-permute-start | bytes 393224 | tf_op jit(solution)/shard_map/ppermute | solution.py:281
  224.5 3.8 %collective-permute-done.16 = f32[128,256]{1,0:T(8,128)S(1)} collective-permute-done((f32[128,256]{1,0:T(8,128)S(1)}, f32[128,256]{1,0:T(8,128)S(1)}, u32[]{:S(2)}, u32[]{:S(2)}) %collective-permute-start.16) | collective-permute-done | bytes 131104 | tf_op jit(solution)/shard_map/ppermute | solution.py:281
  228.5 18.6 %collective-permute-start.23 = (bf16[128,256]{1,0:T(8,128)(2,1)S(1)}, bf16[128,256]{1,0:T(8,128)(2,1)S(1)}, u32[]{:S(2)}, u32[]{:S(2)}) collective-permute-start(bf16[128,256]{1,0:T(8,128)(2,1)S(1)} %get-tuple-element.14), channel_id=1, source_target_pairs={{0,2},{1,3},{2,0},{3,1},{4,6},{5,7},{6,4},{7,5},{8,10},{9,11},{10,... | collective-permute-start | bytes 196616 | tf_op jit(solution)/shard_map/ppermute | solution.py:293
  254.1 4.4 %collective-permute-start.21 = (f32[128,256]{1,0:T(8,128)S(1)}, f32[128,256]{1,0:T(8,128)S(1)}, u32[]{:S(2)}, u32[]{:S(2)}) collective-permute-start(f32[128,256]{1,0:T(8,128)S(1)} %get-tuple-element.15), channel_id=1, source_target_pairs={{0,0},{1,16},{2,32},{3,48},{4,64},{5,80},{6,96},{7,112},{8,128},{9... | collective-permute-start | bytes 393224 | tf_op jit(solution)/shard_map/ppermute | solution.py:291
  258.5 2.9 copy-done
  267.7 3.1 shard_map.132
  271.8 14.1 %all_to_all.16 = f32[16,1,128]{2,1,0:T(1,128)S(1)} all-to-all(f32[16,1,128]{2,1,0:T(1,128)S(1)} %bitcast.108), channel_id=1, replica_groups=mesh['dp'=16,'mp'=16] {'dp'}, dimensions={0} | all-to-all | bytes 16384 | tf_op jit(solution)/shard_map/all_to_all | solution.py:351
  286.5 3.5 %all-to-all-start.2 = ((f32[16,1,128]{2,1,0:T(1,128)}), f32[16,1,128]{2,1,0:T(1,128)S(1)}, u32[]{:S(2)}, u32[]{:S(2)}) async-start(f32[16,1,128]{2,1,0:T(1,128)} %broadcast_in_dim.139), calls=%async_computation.2 | async-start | bytes 16384 | tf_op jit(solution)/shard_map/all_to_all | solution.py:353
  290.0 2.9 copy-done.1
  294.2 4.0 %shard_map.133 = bf16[4,1536,256]{2,1,0:T(8,128)(2,1)} custom-call(bf16[16,4,32,1664]{3,2,1,0:T(8,128)(2,1)S(1)} %bitcast.107, bf16[4,16,32,256]{3,2,1,0:T(8,128)(2,1)S(1)} %copy-done.11), custom_call_target="tpu_custom_call" | custom-call | tf_op jit(solution)/shard_map/pallas_call | solution.py:338
  (158 shorter events, 81.2 us)
Async XLA Ops:
  7.2 251.3 %all-gather.3.cloned.1.call-start = ((), (), s32[]{:S(2)}) async-start(), calls=%async_computation.3 | async-start | bytes 7241728 | tf_op jit(solution)/shard_map/all_gather | solution.py:300
  7.2 32.8 %collective-permute-start.2 = (bf16[256,2432]{1,0:T(8,128)(2,1)}, bf16[256,2432]{1,0:T(8,128)(2,1)S(1)}, u32[]{:S(2)}, u32[]{:S(2)}) collective-permute-start(bf16[256,2432]{1,0:T(8,128)(2,1)} %refs_0_.1), channel_id=1, source_target_pairs={{0,224},{16,240},{32,0},{48,16},{64,32},{80,48},{96,64},{112,80},{... | collective-permute-start | bytes 3735560 | tf_op jit(solution)/shard_map/ppermute | solution.py:31
  13.7 29.7 %collective-permute-start.1 = (bf16[256,2432]{1,0:T(8,128)(2,1)}, bf16[256,2432]{1,0:T(8,128)(2,1)S(1)}, u32[]{:S(2)}, u32[]{:S(2)}) collective-permute-start(bf16[256,2432]{1,0:T(8,128)(2,1)} %refs_0_.1), channel_id=1, source_target_pairs={{0,32},{16,48},{32,64},{48,80},{64,96},{80,112},{96,128},{112,144}... | collective-permute-start | bytes 3735560 | tf_op jit(solution)/shard_map/ppermute | solution.py:30
  40.0 28.4 %collective-permute-start.4 = (bf16[256,2432]{1,0:T(8,128)(2,1)S(1)}, bf16[256,2432]{1,0:T(8,128)(2,1)}, u32[]{:S(2)}, u32[]{:S(2)}) collective-permute-start(bf16[256,2432]{1,0:T(8,128)(2,1)S(1)} %collective-permute-done.2.refs_2_), channel_id=1, source_target_pairs={{0,224},{16,240},{32,0},{48,16},{64,32},{80,48},{96,64},{112,80},{... | collective-permute-start | bytes 3735560 | tf_op jit(solution)/shard_map/ppermute | solution.py:31
  43.4 28.6 %collective-permute-start.3 = (bf16[256,2432]{1,0:T(8,128)(2,1)S(1)}, bf16[256,2432]{1,0:T(8,128)(2,1)}, u32[]{:S(2)}, u32[]{:S(2)}) collective-permute-start(bf16[256,2432]{1,0:T(8,128)(2,1)S(1)} %collective-permute-done.1.refs_1_), channel_id=1, source_target_pairs={{0,32},{16,48},{32,64},{48,80},{64,96},{80,112},{96,128},{112,144}... | collective-permute-start | bytes 3735560 | tf_op jit(solution)/shard_map/ppermute | solution.py:30
  68.5 31.9 %collective-permute-start.6 = (bf16[256,2432]{1,0:T(8,128)(2,1)}, bf16[256,2432]{1,0:T(8,128)(2,1)S(1)}, u32[]{:S(2)}, u32[]{:S(2)}) collective-permute-start(bf16[256,2432]{1,0:T(8,128)(2,1)} %collective-permute-done.4.refs_4_), channel_id=1, source_target_pairs={{0,224},{16,240},{32,0},{48,16},{64,32},{80,48},{96,64},{112,80},{... | collective-permute-start | bytes 3735560 | tf_op jit(solution)/shard_map/ppermute | solution.py:31
  72.0 27.5 %collective-permute-start.5 = (bf16[256,2432]{1,0:T(8,128)(2,1)}, bf16[256,2432]{1,0:T(8,128)(2,1)S(1)}, u32[]{:S(2)}, u32[]{:S(2)}) collective-permute-start(bf16[256,2432]{1,0:T(8,128)(2,1)} %collective-permute-done.3.refs_3_), channel_id=1, source_target_pairs={{0,32},{16,48},{32,64},{48,80},{64,96},{80,112},{96,128},{112,144}... | collective-permute-start | bytes 3735560 | tf_op jit(solution)/shard_map/ppermute | solution.py:30
  100.4 13.3 %collective-permute-start.7 = (bf16[128,2432]{1,0:T(8,128)(2,1)}, bf16[128,2432]{1,0:T(8,128)(2,1)S(1)}, u32[]{:S(2)}, u32[]{:S(2)}) collective-permute-start(bf16[128,2432]{1,0:T(8,128)(2,1)} %slice.81), channel_id=1, source_target_pairs={{0,32},{16,48},{32,64},{48,80},{64,96},{80,112},{96,128},{112,144}... | collective-permute-start | bytes 1867784 | tf_op jit(solution)/shard_map/ppermute | solution.py:35
  101.3 12.4 %collective-permute-start.8 = (bf16[128,2432]{1,0:T(8,128)(2,1)}, bf16[128,2432]{1,0:T(8,128)(2,1)}, u32[]{:S(2)}, u32[]{:S(2)}) collective-permute-start(bf16[128,2432]{1,0:T(8,128)(2,1)} %slice.83), channel_id=1, source_target_pairs={{0,224},{16,240},{32,0},{48,16},{64,32},{80,48},{96,64},{112,80},{... | collective-permute-start | bytes 1867784 | tf_op jit(solution)/shard_map/ppermute | solution.py:36
  182.1 21.6 %collective-permute-start.12 = (f32[4,128,256]{2,1,0:T(8,128)}, f32[4,128,256]{2,1,0:T(8,128)S(1)}, u32[]{:S(2)}, u32[]{:S(2)}) collective-permute-start(f32[4,128,256]{2,1,0:T(8,128)} %get-tuple-element.23), channel_id=1, source_target_pairs={{0,0},{1,16},{2,2},{3,18},{4,4},{5,20},{6,6},{7,22},{8,8},{9,24},{... | collective-permute-start | bytes 1572872 | tf_op jit(solution)/shard_map/ppermute | solution.py:276
  184.6 21.0 %collective-permute-start.13 = (f32[4,128,256]{2,1,0:T(8,128)}, f32[4,128,256]{2,1,0:T(8,128)S(1)}, u32[]{:S(2)}, u32[]{:S(2)}) collective-permute-start(f32[4,128,256]{2,1,0:T(8,128)} %get-tuple-element.20), channel_id=1, source_target_pairs={{0,2},{1,18},{2,0},{3,16},{4,6},{5,22},{6,4},{7,20},{8,10},{9,26},... | collective-permute-start | bytes 1572872 | tf_op jit(solution)/shard_map/ppermute | solution.py:276
  185.7 26.2 %collective-permute-start.14 = (f32[4,128,256]{2,1,0:T(8,128)}, f32[4,128,256]{2,1,0:T(8,128)S(1)}, u32[]{:S(2)}, u32[]{:S(2)}) collective-permute-start(f32[4,128,256]{2,1,0:T(8,128)} %get-tuple-element.22), channel_id=1, source_target_pairs={{0,16},{1,0},{2,18},{3,2},{4,20},{5,4},{6,22},{7,6},{8,24},{9,8},{... | collective-permute-start | bytes 1572872 | tf_op jit(solution)/shard_map/ppermute | solution.py:276
  185.7 28.3 %collective-permute-start.15 = (f32[4,128,256]{2,1,0:T(8,128)S(1)}, f32[4,128,256]{2,1,0:T(8,128)S(1)}, u32[]{:S(2)}, u32[]{:S(2)}) collective-permute-start(f32[4,128,256]{2,1,0:T(8,128)S(1)} %get-tuple-element.21), channel_id=1, source_target_pairs={{0,18},{1,2},{2,16},{3,0},{4,22},{5,6},{6,20},{7,4},{8,26},{9,10},... | collective-permute-start | bytes 1572872 | tf_op jit(solution)/shard_map/ppermute | solution.py:276
  188.6 35.8 %collective-permute-start.20 = (bf16[128,256]{1,0:T(8,128)(2,1)S(1)}, bf16[128,256]{1,0:T(8,128)(2,1)S(1)}, u32[]{:S(2)}, u32[]{:S(2)}) collective-permute-start(bf16[128,256]{1,0:T(8,128)(2,1)S(1)} %constant_dynamic-slice_fusion.2), channel_id=1, source_target_pairs={{0,0},{1,16},{2,32},{3,48},{4,64},{5,80},{6,96},{7,112},{8,128},{9... | collective-permute-start | bytes 196616 | tf_op jit(solution)/shard_map/ppermute | solution.py:182
  203.7 16.9 %collective-permute-start.10 = (f32[2,128]{1,0:T(2,128)S(1)}, f32[2,128]{1,0:T(2,128)S(1)}, u32[]{:S(2)}, u32[]{:S(2)}) collective-permute-start(f32[2,128]{1,0:T(2,128)S(1)} %pad_maximum_fusion.4), channel_id=1, source_target_pairs={{0,0},{1,16},{2,32},{3,48},{4,64},{5,80},{6,96},{7,112},{8,128},{9... | collective-permute-start | bytes 3080 | tf_op jit(solution)/shard_map/ppermute | solution.py:248
  214.1 14.1 %collective-permute-start.16 = (f32[128,256]{1,0:T(8,128)S(1)}, f32[128,256]{1,0:T(8,128)S(1)}, u32[]{:S(2)}, u32[]{:S(2)}) collective-permute-start(f32[128,256]{1,0:T(8,128)S(1)} %get-tuple-element.29), channel_id=1, source_target_pairs={{0,0},{1,16},{2,32},{3,48},{4,64},{5,80},{6,96},{7,112},{8,128},{9... | collective-permute-start | bytes 393224 | tf_op jit(solution)/shard_map/ppermute | solution.py:281
  218.0 10.2 %collective-permute-start.17 = (f32[128,256]{1,0:T(8,128)S(1)}, f32[128,256]{1,0:T(8,128)S(1)}, u32[]{:S(2)}, u32[]{:S(2)}) collective-permute-start(f32[128,256]{1,0:T(8,128)S(1)} %get-tuple-element.26), channel_id=1, source_target_pairs={{0,64},{1,80},{2,96},{3,112},{4,128},{5,144},{6,160},{7,176},{8,19... | collective-permute-start | bytes 393224 | tf_op jit(solution)/shard_map/ppermute | solution.py:281
  228.4 19.2 %collective-permute-start.22 = (bf16[128,256]{1,0:T(8,128)(2,1)S(1)}, bf16[128,256]{1,0:T(8,128)(2,1)S(1)}, u32[]{:S(2)}, u32[]{:S(2)}) collective-permute-start(bf16[128,256]{1,0:T(8,128)(2,1)S(1)} %get-tuple-element.14), channel_id=1, source_target_pairs={{0,1},{1,2},{2,3},{3,0},{4,5},{5,6},{6,7},{7,4},{8,9},{9,10},{10,1... | collective-permute-start | bytes 196616 | tf_op jit(solution)/shard_map/ppermute | solution.py:293
  228.5 21.2 %collective-permute-start.23 = (bf16[128,256]{1,0:T(8,128)(2,1)S(1)}, bf16[128,256]{1,0:T(8,128)(2,1)S(1)}, u32[]{:S(2)}, u32[]{:S(2)}) collective-permute-start(bf16[128,256]{1,0:T(8,128)(2,1)S(1)} %get-tuple-element.14), channel_id=1, source_target_pairs={{0,2},{1,3},{2,0},{3,1},{4,6},{5,7},{6,4},{7,5},{8,10},{9,11},{10,... | collective-permute-start | bytes 196616 | tf_op jit(solution)/shard_map/ppermute | solution.py:293
  250.4 15.8 %collective-permute-start.25 = (bf16[4,128,256]{2,1,0:T(8,128)(2,1)S(1)}, bf16[4,128,256]{2,1,0:T(8,128)(2,1)S(1)}, u32[]{:S(2)}, u32[]{:S(2)}) collective-permute-start(bf16[4,128,256]{2,1,0:T(8,128)(2,1)S(1)} %pad_maximum_fusion.2.rows0), channel_id=1, source_target_pairs={{0,4},{1,5},{2,6},{3,7},{4,8},{5,9},{6,10},{7,11},{8,12},{9,13},{1... | collective-permute-start | bytes 786440 | tf_op jit(solution)/shard_map/ppermute | solution.py:295
  250.5 15.7 %collective-permute-start.26 = (bf16[4,128,256]{2,1,0:T(8,128)(2,1)S(1)}, bf16[4,128,256]{2,1,0:T(8,128)(2,1)S(1)}, u32[]{:S(2)}, u32[]{:S(2)}) collective-permute-start(bf16[4,128,256]{2,1,0:T(8,128)(2,1)S(1)} %pad_maximum_fusion.2.rows0), channel_id=1, source_target_pairs={{0,8},{1,9},{2,10},{3,11},{4,12},{5,13},{6,14},{7,15},{8,0},{9,1},... | collective-permute-start | bytes 786440 | tf_op jit(solution)/shard_map/ppermute | solution.py:295
  252.1 15.6 %collective-permute-start.27 = (bf16[4,128,256]{2,1,0:T(8,128)(2,1)S(1)}, bf16[4,128,256]{2,1,0:T(8,128)(2,1)S(1)}, u32[]{:S(2)}, u32[]{:S(2)}) collective-permute-start(bf16[4,128,256]{2,1,0:T(8,128)(2,1)S(1)} %pad_maximum_fusion.2.rows0), channel_id=1, source_target_pairs={{0,12},{1,13},{2,14},{3,15},{4,0},{5,1},{6,2},{7,3},{8,4},{9,5},{1... | collective-permute-start | bytes 786440 | tf_op jit(solution)/shard_map/ppermute | solution.py:295
  254.1 35.9 %collective-permute-start.21 = (f32[128,256]{1,0:T(8,128)S(1)}, f32[128,256]{1,0:T(8,128)S(1)}, u32[]{:S(2)}, u32[]{:S(2)}) collective-permute-start(f32[128,256]{1,0:T(8,128)S(1)} %get-tuple-element.15), channel_id=1, source_target_pairs={{0,0},{1,16},{2,32},{3,48},{4,64},{5,80},{6,96},{7,112},{8,128},{9... | collective-permute-start | bytes 393224 | tf_op jit(solution)/shard_map/ppermute | solution.py:291
  286.5 11.7 %all-to-all-start.2 = ((f32[16,1,128]{2,1,0:T(1,128)}), f32[16,1,128]{2,1,0:T(1,128)S(1)}, u32[]{:S(2)}, u32[]{:S(2)}) async-start(f32[16,1,128]{2,1,0:T(1,128)} %broadcast_in_dim.139), calls=%async_computation.2 | async-start | bytes 16384 | tf_op jit(solution)/shard_map/all_to_all | solution.py:353
  (30 other events, 188.7 us)
Sparse Core Ops, SparseCore 0:
  113.8 52.5 all-gather.2

commit v3 on v2

v3 whole, which is shorter than its diff:
```python
import functools

import jax
import jax.numpy as jnp
from jax import lax
from jax.experimental import pallas as pl
from jax.experimental.pallas import tpu as pltpu
from jax.sharding import PartitionSpec as P

clip_low = 0.8
clip_high = 1.2
norm_eps = 1e-06
f32 = jnp.float32
bf16 = jnp.bfloat16
lanes = 128


def z_shift(step, nz):
    return [(2 * z + c, 2 * ((z + step) % nz) + c) for z in range(nz) for c in range(2)]


def core_swap(nz):
    return [(2 * z + c, 2 * z + 1 - c) for z in range(nz) for c in range(2)]


def sum_turn(nz):
    return [
        ((2 * z + c) * 16 + 2 * b + low, (2 * b + c) * 16 + 2 * z + low)
        for z in range(nz) for c in range(2) for b in range(nz) for low in range(2)
    ]


def proj_kernel(acts_ref, down_ref, proj_ref):
    groups, _, slots, wide = acts_ref.shape
    acts = acts_ref[:, 0].reshape(groups * slots, wide)
    out = jnp.dot(acts, down_ref[0], preferred_element_type=f32)
    proj_ref[...] = out.reshape(proj_ref.shape)


def gate_kernel(slot_token_ref, rows_ref, proj_ref, gate_ref):
    shards, count, width = proj_ref.shape
    tokens = rows_ref.shape[0]
    column = lax.broadcasted_iota(jnp.int32, (count, tokens), 1)
    slot_token = slot_token_ref[...]
    stream_rows = rows_ref[...]
    gates = jnp.zeros((count, lanes), f32)
    for shard in range(shards):
        match = jnp.where(column == slot_token[:, shard : shard + 1], 1.0, 0.0).astype(bf16)
        rows = jnp.dot(match, stream_rows, preferred_element_type=f32)
        gate = jnp.sum(rows * proj_ref[shard], axis=1, keepdims=True)
        gates = jnp.where(column == shard, gate, gates)
    gate_ref[...] = gates.T[:shards]


def hidden_kernel(nz, place_ref, grad_ref, *refs):
    count = nz + 1
    pieces, out_ref, held, sems = refs[:count], refs[count], refs[count + 1], refs[count + 2]
    z_index, core = place_ref[0], place_ref[1]
    copies = []
    half = pieces[0].shape[0] // 2
    for number, piece in enumerate(pieces):
        target = held.at[number]
        if number >= nz - 1:
            first = half * (number - nz + 1)
            target = held.at[nz - 1, first : first + half]
        copies.append(pltpu.make_async_copy(piece, target, sems.at[number]))
        copies[-1].start()
    tokens = grad_ref.shape[0] // 2
    grad = grad_ref[...]
    for number in range(nz):
        copies[number].wait()
        if number == nz - 1:
            copies[nz].wait()
        step = (number + 1) // 2
        offset = step if number % 2 == 0 else nz - step
        if number == nz - 1:
            offset = nz // 2
        part = lax.dot_general(
            grad, held[number], (((1,), (1,)), ((), ())), preferred_element_type=f32
        )
        block = lax.rem(z_index + offset, nz)
        out_ref[2 * block + core] = part[:tokens]
        out_ref[2 * block + 1 - core] = part[tokens:]


def down_kernel(side_ref, rows_ref, acts_ref, out_ref, weighted):
    groups, per_expert, slots, _ = side_ref.shape
    tokens, width = rows_ref.shape[1:]
    count = per_expert * slots
    expert = pl.program_id(0)

    @pl.when(expert == 0)
    def _():
        column = lax.broadcasted_iota(jnp.int32, (count, tokens), 1).astype(f32)
        for group in range(groups):
            side = side_ref[group].reshape(count, lanes).astype(f32)
            match = jnp.where(column == side[:, 1:2], 1.0, 0.0).astype(bf16)
            rows = jnp.dot(match, rows_ref[group], preferred_element_type=f32)
            made = (side[:, 0:1] * rows).astype(bf16)
            weighted[:, group] = made.reshape(per_expert, slots, width)

    acts = acts_ref[:, 0].reshape(groups * slots, acts_ref.shape[3])
    out_ref[0] = lax.dot_general(
        acts,
        weighted[expert].reshape(groups * slots, width),
        (((0,), (0,)), ((), ())),
        preferred_element_type=f32,
    ).astype(bf16)


def local(
    residual,
    norm_gain,
    head_weight,
    token_ids,
    old_logp,
    advantages,
    resp_mask,
    routes,
    combine_weights,
    expert_acts,
    down_weight,
):
    tokens, model_width = residual.shape
    block, vocab_dev = head_weight.shape
    per_expert, _, capacity, hidden_width = expert_acts.shape
    dp_count = lax.axis_size("dp")
    mp_count = lax.axis_size("mp")
    nz = dp_count // 2
    dp_index = lax.axis_index("dp")
    mp_index = lax.axis_index("mp")
    z_index, core = dp_index // 2, dp_index % 2
    both = ("dp", "mp")
    turn = [(p * mp_count + q, q * mp_count + p) for p in range(dp_count) for q in range(mp_count)]
    experts_all = per_expert * mp_count
    swap = functools.partial(lax.ppermute, axis_name="dp", perm=core_swap(nz))

    stream = residual.astype(f32)
    inv_rms = lax.rsqrt(jnp.mean(stream * stream, axis=1, keepdims=True) + norm_eps)
    normed = (stream * inv_rms * norm_gain[None, :]).astype(bf16)
    by_block = normed.reshape(tokens, nz, 2, block).transpose(2, 1, 0, 3)
    mine = lax.dynamic_index_in_dim(by_block, core, 0, keepdims=False)
    theirs = lax.dynamic_index_in_dim(by_block, 1 - core, 0, keepdims=False)
    chip_normed = jnp.concatenate([mine, swap(theirs)], axis=1)

    turned_stream = lax.ppermute(
        lax.dynamic_slice_in_dim(residual, mp_index * block, block, 1), both, turn
    )

    expert_ids = jnp.arange(experts_all, dtype=jnp.int32)
    hit_routes = routes[:, :, None] == expert_ids[None, None, :]
    hit_token = jnp.sum(hit_routes.astype(jnp.int32), axis=1)
    before = jnp.cumsum(hit_token, axis=0) - hit_token
    slot_ids = jnp.arange(capacity, dtype=jnp.int32)
    matches = (hit_token.T[:, None, :] == 1) & (before.T[:, None, :] == slot_ids[None, :, None])
    weight_token = jnp.sum(
        jnp.where(hit_routes, combine_weights[:, :, None].astype(f32), 0.0), axis=1
    )
    first_expert = mp_index * per_expert
    token_numbers = jnp.arange(tokens, dtype=jnp.int32)
    slot_token = jnp.sum(jnp.where(matches, token_numbers[None, None, :] + 1, 0), axis=2) - 1
    own_matches = lax.dynamic_slice_in_dim(matches, first_expert, per_expert, 0)
    own_weights = lax.dynamic_slice_in_dim(weight_token, first_expert, per_expert, 1)
    own_slot_token = lax.dynamic_slice_in_dim(slot_token, first_expert, per_expert, 0)
    slot_weight = jnp.sum(jnp.where(own_matches, own_weights.T[:, None, :], 0.0), axis=2)
    turned_slots = lax.ppermute(
        slot_token.reshape(mp_count, per_expert * capacity).T, both, turn
    )
    lane = jnp.arange(lanes, dtype=jnp.int32)
    side = jnp.where(
        lane == 0,
        slot_weight[:, :, None],
        jnp.where(lane == 1, own_slot_token.astype(f32)[:, :, None], 0.0),
    ).astype(bf16)
    acts_block = jnp.concatenate([expert_acts[:, 0], side], axis=2)

    acts_all = lax.all_gather(acts_block, "dp", axis=0, tiled=False)
    proj = pl.pallas_call(
        proj_kernel,
        grid=(per_expert,),
        in_specs=[
            pl.BlockSpec((dp_count, 1, capacity, hidden_width), lambda e: (0, e, 0, 0)),
            pl.BlockSpec((1, hidden_width, block), lambda e: (e, 0, 0)),
        ],
        out_specs=pl.BlockSpec((dp_count, 1, capacity, block), lambda e: (0, e, 0, 0)),
        out_shape=jax.ShapeDtypeStruct((dp_count, per_expert, capacity, block), f32),
        compiler_params=pltpu.CompilerParams(vmem_limit_bytes=32 * 1024 * 1024),
    )(acts_all, down_weight)

    def logits_of(rows, offset, first, piece):
        features = lax.dynamic_index_in_dim(
            chip_normed, lax.rem(z_index + offset, nz), 0, keepdims=False
        )[rows, first : first + piece.shape[0]]
        return jnp.dot(features, piece, preferred_element_type=f32)

    everything = slice(0, 2 * tokens)
    ahead = back = head_weight
    head_pieces = [(0, 0, head_weight)]
    partial = None
    for step in range(1, nz // 2):
        if step == 2:
            ahead, back, chip_normed = lax.optimization_barrier((ahead, back, chip_normed))
        if step > 2:
            ahead, back, partial = lax.optimization_barrier((ahead, back, partial))
        if step >= 2:
            done = head_pieces[-2:] if step > 2 else head_pieces
            for offset, first, piece in done:
                added = logits_of(everything, offset, first, piece)
                partial = added if partial is None else partial + added
        ahead = lax.ppermute(ahead, "dp", z_shift(1, nz))
        back = lax.ppermute(back, "dp", z_shift(-1, nz))
        head_pieces += [(nz - step, 0, ahead), (step, 0, back)]
    ahead, back, partial, proj = lax.optimization_barrier((ahead, back, partial, proj))
    half = block // 2
    last_pieces = [
        (nz // 2, 0, lax.ppermute(ahead[:half], "dp", z_shift(1, nz))),
        (nz // 2, half, lax.ppermute(back[half:], "dp", z_shift(-1, nz))),
    ]
    turned_proj = lax.all_to_all(
        proj.reshape(dp_count, per_expert * capacity, block), "mp", 0, 0, tiled=True
    )
    for offset, first, piece in head_pieces[-2:]:
        partial = partial + logits_of(everything, offset, first, piece)
    own_part, other_part = partial[:tokens], partial[tokens:]
    for offset, first, piece in last_pieces:
        other_part = other_part + logits_of(slice(tokens, None), offset, first, piece)
        own_part = own_part + logits_of(slice(0, tokens), offset, first, piece)
    head_pieces += last_pieces
    logits = own_part + swap(other_part)

    local_ids = token_ids - mp_index * vocab_dev
    column = jnp.arange(vocab_dev, dtype=jnp.int32)
    onehot = column[None, :] == local_ids[:, None]
    local_top = jnp.max(logits, axis=1)
    local_exp = jnp.exp(logits - local_top[:, None])
    local_total = jnp.sum(local_exp, axis=1)
    local_mean = jnp.sum(local_exp * logits, axis=1)
    local_picked = jnp.sum(jnp.where(onehot, logits, 0.0), axis=1)
    stats = jnp.stack([local_top, local_total, local_mean, local_picked])
    stats = lax.all_to_all(
        jnp.broadcast_to(stats[None], (mp_count, 4, tokens)), "mp", 0, 0, tiled=True
    )
    row_top = jnp.max(stats[:, 0], axis=0)
    rescale = jnp.exp(stats[:, 0] - row_top[None])
    row_total = jnp.sum(stats[:, 1] * rescale, axis=0)
    mean_logit = jnp.sum(stats[:, 2] * rescale, axis=0) / row_total
    picked = jnp.sum(stats[:, 3], axis=0)

    logp = picked - row_top - jnp.log(row_total)
    prob_ratio = jnp.exp(logp - old_logp)
    weight_row = -jnp.clip(prob_ratio, clip_low, clip_high) * advantages * resp_mask.astype(f32)
    inner = weight_row * (picked - mean_logit) / model_width
    turned_rows = lax.ppermute(jnp.stack([inv_rms[:, 0], inner]), both, turn)
    logit_grad = (
        weight_row[:, None]
        * (onehot.astype(f32) - jnp.exp(logits - row_top[:, None]) / row_total[:, None])
    ).astype(bf16)
    chip_grad = jnp.concatenate([logit_grad, swap(logit_grad)], axis=0)

    place = jnp.stack([z_index, core]).astype(jnp.int32)
    hidden = pl.pallas_call(
        functools.partial(hidden_kernel, nz),
        grid_spec=pltpu.PrefetchScalarGridSpec(
            num_scalar_prefetch=1,
            grid=(1,),
            in_specs=[pl.BlockSpec((2 * tokens, vocab_dev), lambda n, place: (0, 0))]
            + [pl.BlockSpec(memory_space=pl.ANY)] * (nz + 1),
            out_specs=pl.BlockSpec((mp_count, tokens, block), lambda n, place: (0, 0, 0)),
            scratch_shapes=[
                pltpu.VMEM((nz, block, vocab_dev), bf16),
                pltpu.SemaphoreType.DMA((nz + 1,)),
            ],
        ),
        out_shape=jax.ShapeDtypeStruct((mp_count, tokens, block), f32),
        compiler_params=pltpu.CompilerParams(vmem_limit_bytes=40 * 1024 * 1024),
    )(place, chip_grad, *[piece for _, _, piece in head_pieces])

    hidden, turned_proj = lax.optimization_barrier((hidden, turned_proj))
    hidden_grad = jnp.sum(lax.all_to_all(hidden, "mp", 0, 0, tiled=True), axis=0)
    hidden_grad = lax.ppermute(hidden_grad, both, sum_turn(nz))

    my_gain = lax.dynamic_slice_in_dim(norm_gain, dp_index * block, block, 0)
    turned_rms, turned_inner = turned_rows[0][:, None], turned_rows[1][:, None]
    scaled_grad = my_gain[None, :] * hidden_grad
    turned_resid = turned_rms * (
        scaled_grad - turned_stream.astype(f32) * turned_rms * turned_inner
    )
    stream_grad = turned_resid.astype(bf16)
    resid_grad = lax.ppermute(turned_resid, both, turn)

    all_rows = lax.all_to_all(
        jnp.broadcast_to(stream_grad[None], (mp_count, tokens, block)), "mp", 0, 0, tiled=True
    )
    gate = pl.pallas_call(
        gate_kernel,
        out_shape=jax.ShapeDtypeStruct((mp_count, per_expert * capacity), f32),
        compiler_params=pltpu.CompilerParams(vmem_limit_bytes=32 * 1024 * 1024),
    )(turned_slots, stream_grad, turned_proj)
    down_grad = pl.pallas_call(
        down_kernel,
        grid=(per_expert,),
        in_specs=[
            pl.BlockSpec(
                (dp_count, per_expert, capacity, lanes), lambda e: (0, 0, 0, hidden_width // lanes)
            ),
            pl.BlockSpec((dp_count, tokens, block), lambda e: (0, 0, 0)),
            pl.BlockSpec((dp_count, 1, capacity, hidden_width), lambda e: (0, e, 0, 0)),
        ],
        out_specs=pl.BlockSpec((1, hidden_width, block), lambda e: (e, 0, 0)),
        out_shape=jax.ShapeDtypeStruct((per_expert, hidden_width, block), bf16),
        scratch_shapes=[pltpu.VMEM((per_expert, dp_count, capacity, block), bf16)],
        compiler_params=pltpu.CompilerParams(vmem_limit_bytes=40 * 1024 * 1024),
    )(acts_all, all_rows, acts_all)

    gate = lax.ppermute(gate, both, turn)
    slot_gate = jnp.sum(
        lax.all_to_all(
            jnp.broadcast_to(gate[None], (mp_count,) + gate.shape), "mp", 0, 0, tiled=True
        ),
        axis=0,
    ).reshape(experts_all, capacity)
    per_token = jnp.sum(jnp.where(matches, slot_gate[:, :, None], 0.0), axis=1)
    gate_grad = jnp.sum(jnp.where(hit_routes, per_token.T[:, None, :], 0.0), axis=2)
    return (resid_grad, down_grad, gate_grad)


def solution(mesh):
    placed = (
        P("dp", None),
        P(),
        P("dp", "mp"),
        P("dp"),
        P("dp"),
        P("dp"),
        P("dp"),
        P("dp", None),
        P("dp", None),
        P("mp", "dp", None, None),
        P("mp", None, "dp"),
    )
    return jax.shard_map(
        local,
        mesh=mesh,
        in_specs=placed,
        out_specs=(P("dp", "mp"), P("mp", None, "dp"), P("dp", None)),
        check_vma=False,
    )
```

time: 309 us -> 336 us (1.087)
  waiting for transfers between devices: 119 us -> 146 us
  blocking collectives: 27.2 us -> 45.4 us
  starting transfers between devices: 73.2 us -> 58.5 us
    ppermute x22 -> x11, starting transfers between devices: 54.2 us -> 23 us  [the longest x3 10.1 us: local(): back = lax.ppermute(back, 'dp', z_shift(-1, nz))]
    all_to_all x1 -> x3, waiting for transfers between devices: 0.01 us -> 29.3 us  [the longest x1 19.3 us: local(): lax.all_to_all(hidden, 'mp', 0, 0, tiled=True)]
    ppermute x22 -> x11, waiting for transfers between devices: 114 us -> 92.7 us  [the longest x3 77.9 us: local(): ahead = lax.ppermute(ahead, 'dp', z_shift(1, nz))]
    all_to_all x1, blocking collectives: 14.1 us -> 32.4 us  [local(): lax.all_to_all(jnp.broadcast_to(gate[None], (mp_count,) + gate.shape), 'm...]
    ppermute x1, waiting for transfers between devices: 0.01 us -> 17.9 us  [local(): resid_grad = lax.ppermute(turned_resid, both, turn)]
    all_to_all x1 -> x3, starting transfers between devices: 3.47 us -> 13.6 us  [the longest x1 5.99 us: local(): lax.all_to_all(hidden, 'mp', 0, 0, tiled=True)]
    ppermute x1, starting transfers between devices: 4.86 us -> 1.04 us  [local(): chip_normed = jnp.concatenate([mine, swap(theirs)], axis=1)]
    ppermute x1, starting transfers between devices: 0.39 us -> 4.07 us  [local(): logits = own_part + swap(other_part)]
  transfers between devices with their start and end apart: 30 -> 21, of which waited for: 15 -> 16; matrix products, arithmetic and copies ran while one was open for 13% -> 9% of each run, Pallas kernels for 6% -> 4%
where the time goes in v3:
time: 336 us; the launch traced here: 334 us
  waiting for transfers between devices  146 us (43%)
  starting transfers between devices  58.5 us (17%)
  blocking collectives  45.4 us (14%)
  Pallas kernels  20.6 us (6%)
  local copies, waits for them, and re-layouts  19.4 us (6%)
  matrix products  16.2 us (5%)
  between operations  14.6 us (4%)
  other arithmetic  13.8 us (4%)
    ppermute x3, waiting for transfers between devices, local(): ahead = lax.ppermute(ahead, 'dp', z_shift(1, nz))  77.9 us
    all_to_all x1, blocking collectives, local(): lax.all_to_all(jnp.broadcast_to(gate[None], (mp_count,) + gate.shape), 'm...  32.4 us
    all_to_all x1, waiting for transfers between devices, local(): lax.all_to_all(hidden, 'mp', 0, 0, tiled=True)  19.3 us
    ppermute x1, waiting for transfers between devices, local(): resid_grad = lax.ppermute(turned_resid, both, turn)  17.9 us
    dot_general x11, matrix products, logits_of(): return jnp.dot(features, piece, preferred_element_type=f32)  16.2 us
    all_to_all x1, blocking collectives, local(): lax.all_to_all(jnp.broadcast_to(stats[None], (mp_count, 4, tokens)), 'mp'...  13 us
    unnamed x66, local copies, waits for them, and re-layouts  12.6 us
    pallas_call x1, Pallas kernels, local(): pl.pallas_call(functools.partial(hidden_kernel, nz), grid_spec=pltpu.Pref...  10.5 us
  transfers between devices with their start and end apart: 21, of which 16 were waited for; matrix products, arithmetic and copies ran while one was open for 9% of the time, Pallas kernels for 4%

profile of v3, /device:TPU:1, one launch (start us, length us, event | category | flops | bytes accessed | tf_op | source)
XLA Modules:
  0.0 334.4 jit_solution(4637985137557707807)
XLA Ops:
  14.9 4.0 %collective-permute-start.1 = (bf16[256,2432]{1,0:T(8,128)(2,1)}, bf16[256,2432]{1,0:T(8,128)(2,1)S(1)}, u32[]{:S(2)}, u32[]{:S(2)}) collective-permute-start(bf16[256,2432]{1,0:T(8,128)(2,1)} %refs_0_.1), channel_id=1, source_target_pairs={{0,224},{16,240},{32,0},{48,16},{64,32},{80,48},{96,64},{112,80},{... | collective-permute-start | bytes 3735560 | tf_op jit(solution)/shard_map/ppermute | solution.py:211
  27.3 33.5 %collective-permute-done.refs_1_ = bf16[256,2432]{1,0:T(8,128)(2,1)S(1)} collective-permute-done((bf16[256,2432]{1,0:T(8,128)(2,1)}, bf16[256,2432]{1,0:T(8,128)(2,1)S(1)}, u32[]{:S(2)}, u32[]{:S(2)}) %collective-permute-start) | collective-permute-done | bytes 1245216 | tf_op jit(solution)/shard_map/ppermute | solution.py:210
  62.7 3.4 %collective-permute-start.4 = (bf16[256,2432]{1,0:T(8,128)(2,1)S(1)}, bf16[256,2432]{1,0:T(8,128)(2,1)}, u32[]{:S(2)}, u32[]{:S(2)}) collective-permute-start(bf16[256,2432]{1,0:T(8,128)(2,1)S(1)} %collective-permute-done.1.refs_2_), channel_id=1, source_target_pairs={{0,224},{16,240},{32,0},{48,16},{64,32},{80,48},{96,64},{112,80},{... | collective-permute-start | bytes 3735560 | tf_op jit(solution)/shard_map/ppermute | solution.py:211
  70.5 33.9 %collective-permute-done.3.refs_3_ = bf16[256,2432]{1,0:T(8,128)(2,1)} collective-permute-done((bf16[256,2432]{1,0:T(8,128)(2,1)S(1)}, bf16[256,2432]{1,0:T(8,128)(2,1)}, u32[]{:S(2)}, u32[]{:S(2)}) %collective-permute-start.3) | collective-permute-done | bytes 1245216 | tf_op jit(solution)/shard_map/ppermute | solution.py:210
  111.5 3.3 add_add_fusion.1
  114.8 2.9 copy-done
  122.5 10.5 %collective-permute-done.5.refs_5_ = bf16[256,2432]{1,0:T(8,128)(2,1)S(1)} collective-permute-done((bf16[256,2432]{1,0:T(8,128)(2,1)}, bf16[256,2432]{1,0:T(8,128)(2,1)S(1)}, u32[]{:S(2)}, u32[]{:S(2)}) %collective-permute-start.5) | collective-permute-done | bytes 1245216 | tf_op jit(solution)/shard_map/ppermute | solution.py:210
  139.2 8.2 %collective-permute-done.7.refs_7_ = bf16[128,2432]{1,0:T(8,128)(2,1)S(1)} collective-permute-done((bf16[128,2432]{1,0:T(8,128)(2,1)S(1)}, bf16[128,2432]{1,0:T(8,128)(2,1)S(1)}, u32[]{:S(2)}, u32[]{:S(2)}) %collective-permute-start.7) | collective-permute-done | bytes 622624 | tf_op jit(solution)/shard_map/ppermute | solution.py:216
  150.5 4.1 %collective-permute-start.9 = (f32[128,2432]{1,0:T(8,128)}, f32[128,2432]{1,0:T(8,128)S(1)}, u32[]{:S(2)}, u32[]{:S(2)}) collective-permute-start(f32[128,2432]{1,0:T(8,128)} %fusion.3), channel_id=1, source_target_pairs={{0,16},{16,0},{32,48},{48,32},{64,80},{80,64},{96,112},{112,96},{1... | collective-permute-start | bytes 3735560 | tf_op jit(solution)/shard_map/ppermute | solution.py:229
  159.4 13.0 %all_to_all.25 = f32[16,4,128]{2,1,0:T(4,128)S(1)} all-to-all(f32[16,4,128]{2,1,0:T(4,128)S(1)} %broadcast_in_dim.140), channel_id=1, replica_groups=mesh['dp'=16,'mp'=16] {'mp'}, dimensions={0} | all-to-all | bytes 65536 | tf_op jit(solution)/shard_map/all_to_all | solution.py:240
  172.4 3.8 %all-to-all-start.1 = ((f32[16,128,256]{2,1,0:T(8,128)}), f32[16,128,256]{2,1,0:T(8,128)S(1)}, u32[]{:S(2)}, u32[]{:S(2)}) async-start(f32[16,128,256]{2,1,0:T(8,128)} %bitcast.89), calls=%async_computation.1 | async-start | bytes 4194304 | tf_op jit(solution)/shard_map/all_to_all | solution.py:219
  183.4 10.5 %shard_map.131 = f32[16,128,256]{2,1,0:T(8,128)} custom-call(s32[2]{0:T(128)S(1)} %pad_add_fusion.place_ref, bf16[256,2432]{1,0:T(8,128)(2,1)S(1)} %pad_maximum_fusion.grad_ref, bf16[256,2432]{1,0:T(8,128)(2,1)} %refs_0_.1, bf16[256,2432]{1,0:T(8,128)(2,1)S(1)} %copy-done.10, bf16[256,2432]{1,0:T(8,128)(2,1)S(1)} %copy-done.12, ...), custom_call_target="tpu_custom_call" | custom-call | tf_op jit(solution)/shard_map/pallas_call | solution.py:261
  193.9 10.1 %all-to-all-done.1.proj_ref = f32[16,128,256]{2,1,0:T(8,128)S(1)} async-done(((f32[16,128,256]{2,1,0:T(8,128)}), f32[16,128,256]{2,1,0:T(8,128)S(1)}, u32[]{:S(2)}, u32[]{:S(2)}) %all-to-all-start.1) | async-done | bytes 2097184 | tf_op jit(solution)/shard_map/all_to_all | solution.py:219
  204.0 6.0 %all-to-all-start.2 = ((f32[16,128,256]{2,1,0:T(8,128)}), f32[16,128,256]{2,1,0:T(8,128)}, u32[]{:S(2)}, u32[]{:S(2)}) async-start(f32[16,128,256]{2,1,0:T(8,128)} %shard_map.131), calls=%async_computation.2 | async-start | bytes 4194304 | tf_op jit(solution)/shard_map/all_to_all | solution.py:279
  210.0 5.6 %collective-permute-start.10 = (f32[2,128]{1,0:T(2,128)S(1)}, f32[2,128]{1,0:T(2,128)S(1)}, u32[]{:S(2)}, u32[]{:S(2)}) collective-permute-start(f32[2,128]{1,0:T(2,128)S(1)} %pad_maximum_fusion.4), channel_id=1, source_target_pairs={{0,0},{1,16},{2,32},{3,48},{4,64},{5,80},{6,96},{7,112},{8,128},{9... | collective-permute-start | bytes 3080 | tf_op jit(solution)/shard_map/ppermute | solution.py:253
  218.6 3.6 %collective-permute-start.15 = (s32[128,16]{1,0:T(8,128)S(1)}, s32[128,16]{1,0:T(8,128)S(1)}, u32[]{:S(2)}, u32[]{:S(2)}) collective-permute-start(s32[128,16]{1,0:T(8,128)S(1)} %bitcast.99), channel_id=1, source_target_pairs={{0,0},{1,16},{2,32},{3,48},{4,64},{5,80},{6,96},{7,112},{8,128},{9... | collective-permute-start | bytes 24584 | tf_op jit(solution)/shard_map/ppermute | solution.py:166
  223.0 19.3 %all-to-all-done.2 = f32[16,128,256]{2,1,0:T(8,128)} async-done(((f32[16,128,256]{2,1,0:T(8,128)}), f32[16,128,256]{2,1,0:T(8,128)}, u32[]{:S(2)}, u32[]{:S(2)}) %all-to-all-start.2) | async-done | bytes 2097184 | tf_op jit(solution)/shard_map/all_to_all | solution.py:279
  249.9 3.0 collective-permute-start.16
  255.6 32.4 %all_to_all.26 = f32[16,16,128]{2,1,0:T(8,128)S(1)} all-to-all(f32[16,16,128]{2,1,0:T(8,128)S(1)} %broadcast_in_dim.142), channel_id=1, replica_groups=mesh['dp'=16,'mp'=16] {'mp'}, dimensions={0} | all-to-all | bytes 262144 | tf_op jit(solution)/shard_map/all_to_all | solution.py:317
  289.1 3.8 %all-to-all-start.3 = ((bf16[16,128,256]{2,1,0:T(8,128)(2,1)}), bf16[16,128,256]{2,1,0:T(8,128)(2,1)S(1)}, u32[]{:S(2)}, u32[]{:S(2)}) async-start(bf16[16,128,256]{2,1,0:T(8,128)(2,1)} %broadcast_in_dim.141), calls=%async_computation.3 | async-start | bytes 2097152 | tf_op jit(solution)/shard_map/all_to_all | solution.py:291
  292.9 7.4 %collective-permute-start.14 = (f32[128,256]{1,0:T(8,128)S(1)}, f32[128,256]{1,0:T(8,128)S(1)}, u32[]{:S(2)}, u32[]{:S(2)}) collective-permute-start(f32[128,256]{1,0:T(8,128)S(1)} %get-tuple-element.33), channel_id=1, source_target_pairs={{0,0},{1,16},{2,32},{3,48},{4,64},{5,80},{6,96},{7,112},{8,128},{9... | collective-permute-start | bytes 393224 | tf_op jit(solution)/shard_map/ppermute | solution.py:289
  300.4 17.9 %collective-permute-done.14 = f32[128,256]{1,0:T(8,128)S(1)} collective-permute-done((f32[128,256]{1,0:T(8,128)S(1)}, f32[128,256]{1,0:T(8,128)S(1)}, u32[]{:S(2)}, u32[]{:S(2)}) %collective-permute-start.14) | collective-permute-done | bytes 131104 | tf_op jit(solution)/shard_map/ppermute | solution.py:289
  319.3 2.9 copy-done.1
  322.3 4.6 %shard_map.132 = bf16[4,1536,256]{2,1,0:T(8,128)(2,1)} custom-call(bf16[16,4,32,1664]{3,2,1,0:T(8,128)(2,1)S(1)} %bitcast.87, bf16[16,128,256]{2,1,0:T(8,128)(2,1)S(1)} %all-to-all-done.3.rows_ref, bf16[16,4,32,1664]{3,2,1,0:T(8,128)(2,1)S(1)} %bitcast.88), custom_call_target="tpu_custom_call" | custom-call | tf_op jit(solution)/shard_map/pallas_call | solution.py:299
  (155 shorter events, 72.1 us)
Async XLA Ops:
  7.2 107.6 %all-gather.3.cloned.1.call-start = ((), (), s32[]{:S(2)}) async-start(), calls=%async_computation.5 | async-start | bytes 7241728 | tf_op jit(solution)/shard_map/all_gather | solution.py:177
  12.4 48.5 %collective-permute-start = (bf16[256,2432]{1,0:T(8,128)(2,1)}, bf16[256,2432]{1,0:T(8,128)(2,1)S(1)}, u32[]{:S(2)}, u32[]{:S(2)}) collective-permute-start(bf16[256,2432]{1,0:T(8,128)(2,1)} %refs_0_.1), channel_id=1, source_target_pairs={{0,32},{16,48},{32,64},{48,80},{64,96},{80,112},{96,128},{112,144}... | collective-permute-start | bytes 3735560 | tf_op jit(solution)/shard_map/ppermute | solution.py:210
  14.9 47.8 %collective-permute-start.1 = (bf16[256,2432]{1,0:T(8,128)(2,1)}, bf16[256,2432]{1,0:T(8,128)(2,1)S(1)}, u32[]{:S(2)}, u32[]{:S(2)}) collective-permute-start(bf16[256,2432]{1,0:T(8,128)(2,1)} %refs_0_.1), channel_id=1, source_target_pairs={{0,224},{16,240},{32,0},{48,16},{64,32},{80,48},{96,64},{112,80},{... | collective-permute-start | bytes 3735560 | tf_op jit(solution)/shard_map/ppermute | solution.py:211
  24.6 2.6 collective-permute-start.2
  27.3 84.1 %copy-start.19 = (bf16[8,256,256]{1,2,0:T(8,128)(2,1)}, bf16[8,256,256]{1,2,0:T(8,128)(2,1)S(1)}, u32[]{:S(2)}) copy-start(bf16[8,256,256]{1,2,0:T(8,128)(2,1)S(1)} %pad_maximum_fusion.1) | copy-start | bytes 3145732
  62.7 41.7 %collective-permute-start.3 = (bf16[256,2432]{1,0:T(8,128)(2,1)S(1)}, bf16[256,2432]{1,0:T(8,128)(2,1)}, u32[]{:S(2)}, u32[]{:S(2)}) collective-permute-start(bf16[256,2432]{1,0:T(8,128)(2,1)S(1)} %collective-permute-done.refs_1_), channel_id=1, source_target_pairs={{0,32},{16,48},{32,64},{48,80},{64,96},{80,112},{96,128},{112,144}... | collective-permute-start | bytes 3735560 | tf_op jit(solution)/shard_map/ppermute | solution.py:210
  62.7 41.7 %collective-permute-start.4 = (bf16[256,2432]{1,0:T(8,128)(2,1)S(1)}, bf16[256,2432]{1,0:T(8,128)(2,1)}, u32[]{:S(2)}, u32[]{:S(2)}) collective-permute-start(bf16[256,2432]{1,0:T(8,128)(2,1)S(1)} %collective-permute-done.1.refs_2_), channel_id=1, source_target_pairs={{0,224},{16,240},{32,0},{48,16},{64,32},{80,48},{96,64},{112,80},{... | collective-permute-start | bytes 3735560 | tf_op jit(solution)/shard_map/ppermute | solution.py:211
  104.4 28.6 %collective-permute-start.5 = (bf16[256,2432]{1,0:T(8,128)(2,1)}, bf16[256,2432]{1,0:T(8,128)(2,1)S(1)}, u32[]{:S(2)}, u32[]{:S(2)}) collective-permute-start(bf16[256,2432]{1,0:T(8,128)(2,1)} %collective-permute-done.3.refs_3_), channel_id=1, source_target_pairs={{0,32},{16,48},{32,64},{48,80},{64,96},{80,112},{96,128},{112,144}... | collective-permute-start | bytes 3735560 | tf_op jit(solution)/shard_map/ppermute | solution.py:210
  104.4 28.6 %collective-permute-start.6 = (bf16[256,2432]{1,0:T(8,128)(2,1)}, bf16[256,2432]{1,0:T(8,128)(2,1)S(1)}, u32[]{:S(2)}, u32[]{:S(2)}) collective-permute-start(bf16[256,2432]{1,0:T(8,128)(2,1)} %collective-permute-done.4.refs_4_), channel_id=1, source_target_pairs={{0,224},{16,240},{32,0},{48,16},{64,32},{80,48},{96,64},{112,80},{... | collective-permute-start | bytes 3735560 | tf_op jit(solution)/shard_map/ppermute | solution.py:211
  133.0 14.4 %collective-permute-start.7 = (bf16[128,2432]{1,0:T(8,128)(2,1)S(1)}, bf16[128,2432]{1,0:T(8,128)(2,1)S(1)}, u32[]{:S(2)}, u32[]{:S(2)}) collective-permute-start(bf16[128,2432]{1,0:T(8,128)(2,1)S(1)} %slice.45), channel_id=1, source_target_pairs={{0,32},{16,48},{32,64},{48,80},{64,96},{80,112},{96,128},{112,144}... | collective-permute-start | bytes 1867784 | tf_op jit(solution)/shard_map/ppermute | solution.py:216
  136.7 12.5 %collective-permute-start.8 = (bf16[128,2432]{1,0:T(8,128)(2,1)S(1)}, bf16[128,2432]{1,0:T(8,128)(2,1)S(1)}, u32[]{:S(2)}, u32[]{:S(2)}) collective-permute-start(bf16[128,2432]{1,0:T(8,128)(2,1)S(1)} %slice.47), channel_id=1, source_target_pairs={{0,224},{16,240},{32,0},{48,16},{64,32},{80,48},{96,64},{112,80},{... | collective-permute-start | bytes 1867784 | tf_op jit(solution)/shard_map/ppermute | solution.py:217
  150.5 6.8 %collective-permute-start.9 = (f32[128,2432]{1,0:T(8,128)}, f32[128,2432]{1,0:T(8,128)S(1)}, u32[]{:S(2)}, u32[]{:S(2)}) collective-permute-start(f32[128,2432]{1,0:T(8,128)} %fusion.3), channel_id=1, source_target_pairs={{0,16},{16,0},{32,48},{48,32},{64,80},{80,64},{96,112},{112,96},{1... | collective-permute-start | bytes 3735560 | tf_op jit(solution)/shard_map/ppermute | solution.py:229
  172.4 31.6 %all-to-all-start.1 = ((f32[16,128,256]{2,1,0:T(8,128)}), f32[16,128,256]{2,1,0:T(8,128)S(1)}, u32[]{:S(2)}, u32[]{:S(2)}) async-start(f32[16,128,256]{2,1,0:T(8,128)} %bitcast.89), calls=%async_computation.1 | async-start | bytes 4194304 | tf_op jit(solution)/shard_map/all_to_all | solution.py:219
  178.4 3.6 %collective-permute-start.11 = (bf16[128,2432]{1,0:T(8,128)(2,1)S(1)}, bf16[128,2432]{1,0:T(8,128)(2,1)S(1)}, u32[]{:S(2)}, u32[]{:S(2)}) collective-permute-start(bf16[128,2432]{1,0:T(8,128)(2,1)S(1)} %multiply_convert_fusion), channel_id=1, source_target_pairs={{0,16},{16,0},{32,48},{48,32},{64,80},{80,64},{96,112},{112,96},{1... | collective-permute-start | bytes 1867784 | tf_op jit(solution)/shard_map/ppermute | solution.py:258
  204.0 38.2 %all-to-all-start.2 = ((f32[16,128,256]{2,1,0:T(8,128)}), f32[16,128,256]{2,1,0:T(8,128)}, u32[]{:S(2)}, u32[]{:S(2)}) async-start(f32[16,128,256]{2,1,0:T(8,128)} %shard_map.131), calls=%async_computation.2 | async-start | bytes 4194304 | tf_op jit(solution)/shard_map/all_to_all | solution.py:279
  210.0 35.8 %collective-permute-start.10 = (f32[2,128]{1,0:T(2,128)S(1)}, f32[2,128]{1,0:T(2,128)S(1)}, u32[]{:S(2)}, u32[]{:S(2)}) collective-permute-start(f32[2,128]{1,0:T(2,128)S(1)} %pad_maximum_fusion.4), channel_id=1, source_target_pairs={{0,0},{1,16},{2,32},{3,48},{4,64},{5,80},{6,96},{7,112},{8,128},{9... | collective-permute-start | bytes 3080 | tf_op jit(solution)/shard_map/ppermute | solution.py:253
  216.5 30.1 %collective-permute-start.13 = (bf16[128,256]{1,0:T(8,128)(2,1)S(1)}, bf16[128,256]{1,0:T(8,128)(2,1)S(1)}, u32[]{:S(2)}, u32[]{:S(2)}) collective-permute-start(bf16[128,256]{1,0:T(8,128)(2,1)S(1)} %constant_dynamic-slice_fusion), channel_id=1, source_target_pairs={{0,0},{1,16},{2,32},{3,48},{4,64},{5,80},{6,96},{7,112},{8,128},{9... | collective-permute-start | bytes 196616 | tf_op jit(solution)/shard_map/ppermute | solution.py:146
  218.6 28.7 %collective-permute-start.15 = (s32[128,16]{1,0:T(8,128)S(1)}, s32[128,16]{1,0:T(8,128)S(1)}, u32[]{:S(2)}, u32[]{:S(2)}) collective-permute-start(s32[128,16]{1,0:T(8,128)S(1)} %bitcast.99), channel_id=1, source_target_pairs={{0,0},{1,16},{2,32},{3,48},{4,64},{5,80},{6,96},{7,112},{8,128},{9... | collective-permute-start | bytes 24584 | tf_op jit(solution)/shard_map/ppermute | solution.py:166
  244.0 2.6 collective-permute-start.12
  249.9 5.8 %collective-permute-start.16 = (f32[16,128]{1,0:T(8,128)S(1)}, f32[16,128]{1,0:T(8,128)S(1)}, u32[]{:S(2)}, u32[]{:S(2)}) collective-permute-start(f32[16,128]{1,0:T(8,128)S(1)} %shard_map.133), channel_id=1, source_target_pairs={{0,0},{1,16},{2,32},{3,48},{4,64},{5,80},{6,96},{7,112},{8,128},{9... | collective-permute-start | bytes 24584 | tf_op jit(solution)/shard_map/ppermute | solution.py:315
  289.1 29.1 %copy-start.21 = (s32[64,128]{1,0:T(8,128)S(1)}, s32[64,128]{1,0:T(8,128)}, u32[]{:S(2)}) copy-start(s32[64,128]{1,0:T(8,128)} %copy-done.20) | copy-start | bytes 98308
  289.1 29.6 %copy-start.27 = (s32[128,8]{0,1:T(8,128)S(1)}, s32[128,8]{0,1:T(8,128)}, u32[]{:S(2)}) copy-start(s32[128,8]{0,1:T(8,128)} %param.18) | copy-start | bytes 12292
  289.1 30.2 %all-to-all-start.3 = ((bf16[16,128,256]{2,1,0:T(8,128)(2,1)}), bf16[16,128,256]{2,1,0:T(8,128)(2,1)S(1)}, u32[]{:S(2)}, u32[]{:S(2)}) async-start(bf16[16,128,256]{2,1,0:T(8,128)(2,1)} %broadcast_in_dim.141), calls=%async_computation.3 | async-start | bytes 2097152 | tf_op jit(solution)/shard_map/all_to_all | solution.py:291
  292.9 25.3 %collective-permute-start.14 = (f32[128,256]{1,0:T(8,128)S(1)}, f32[128,256]{1,0:T(8,128)S(1)}, u32[]{:S(2)}, u32[]{:S(2)}) collective-permute-start(f32[128,256]{1,0:T(8,128)S(1)} %get-tuple-element.33), channel_id=1, source_target_pairs={{0,0},{1,16},{2,32},{3,48},{4,64},{5,80},{6,96},{7,112},{8,128},{9... | collective-permute-start | bytes 393224 | tf_op jit(solution)/shard_map/ppermute | solution.py:289
  (29 other events, 153.5 us)
Sparse Core Ops, SparseCore 0:
  12.5 78.5 all-gather.2

commit v4 on v3

--- a/solution.py
+++ b/solution.py
@@ -30,11 +30,23 @@
     ]
 
 
-def proj_kernel(acts_ref, down_ref, proj_ref):
-    groups, _, slots, wide = acts_ref.shape
-    acts = acts_ref[:, 0].reshape(groups * slots, wide)
+def acts_of(refs, expert, wide):
+    parts = []
+    for core in range(2):
+        mine = refs[core * len(refs) // 2 : (core + 1) * len(refs) // 2]
+        parts += [ref[0, :, :wide] for ref in mine[:-2]]
+        first = mine[-2][0, :, :wide]
+        parts.append(jnp.where(expert < 2, first, mine[-1][0, :, :wide]))
+    return jnp.concatenate(parts, axis=0)
+
+
+def proj_kernel(group_ref, down_ref, *refs):
+    acts_refs, proj_ref = refs[:-1], refs[-1]
+    acts = acts_of(acts_refs, pl.program_id(0), down_ref.shape[1])
     out = jnp.dot(acts, down_ref[0], preferred_element_type=f32)
-    proj_ref[...] = out.reshape(proj_ref.shape)
+    slots = proj_ref.shape[2]
+    for place in range(proj_ref.shape[0]):
+        proj_ref[group_ref[place], 0] = out[place * slots : (place + 1) * slots]
 
 
 def gate_kernel(slot_token_ref, rows_ref, proj_ref, gate_ref):
@@ -53,56 +65,53 @@
 
 
 def hidden_kernel(nz, place_ref, grad_ref, *refs):
-    count = nz + 1
-    pieces, out_ref, held, sems = refs[:count], refs[count], refs[count + 1], refs[count + 2]
+    pieces, out_ref = refs[: nz + 1], refs[nz + 1]
     z_index, core = place_ref[0], place_ref[1]
-    copies = []
+    tokens = grad_ref.shape[0] // 2
     half = pieces[0].shape[0] // 2
-    for number, piece in enumerate(pieces):
-        target = held.at[number]
-        if number >= nz - 1:
-            first = half * (number - nz + 1)
-            target = held.at[nz - 1, first : first + half]
-        copies.append(pltpu.make_async_copy(piece, target, sems.at[number]))
-        copies[-1].start()
-    tokens = grad_ref.shape[0] // 2
     grad = grad_ref[...]
-    for number in range(nz):
-        copies[number].wait()
-        if number == nz - 1:
-            copies[nz].wait()
+    for number in range(nz + 1):
         step = (number + 1) // 2
         offset = step if number % 2 == 0 else nz - step
-        if number == nz - 1:
-            offset = nz // 2
+        first = 0
+        if number >= nz - 1:
+            offset, first = nz // 2, half * (number - nz + 1)
         part = lax.dot_general(
-            grad, held[number], (((1,), (1,)), ((), ())), preferred_element_type=f32
-        )
+            pieces[number][...], grad, (((1,), (1,)), ((), ())), preferred_element_type=f32
+        ).astype(out_ref.dtype)
+        rows = slice(first, first + part.shape[0])
         block = lax.rem(z_index + offset, nz)
-        out_ref[2 * block + core] = part[:tokens]
-        out_ref[2 * block + 1 - core] = part[tokens:]
-
-
-def down_kernel(side_ref, rows_ref, acts_ref, out_ref, weighted):
-    groups, per_expert, slots, _ = side_ref.shape
+        out_ref[2 * block + core, rows] = part[:, :tokens]
+        out_ref[2 * block + 1 - core, rows] = part[:, tokens:]
+
+
+def down_kernel(group_ref, rows_ref, *refs):
+    count = (len(refs) - 2) // 2
+    side_refs, acts_refs, out_ref, weighted = refs[:count], refs[count:-2], refs[-2], refs[-1]
+    per_expert, places, slots, _ = weighted.shape
+    sides = []
+    for core in range(2):
+        mine = side_refs[core * count // 2 : (core + 1) * count // 2]
+        sides += [(ref,) for ref in mine[:-2]] + [mine[-2:]]
     tokens, width = rows_ref.shape[1:]
-    count = per_expert * slots
+    rows_out = per_expert * slots
     expert = pl.program_id(0)
 
     @pl.when(expert == 0)
     def _():
-        column = lax.broadcasted_iota(jnp.int32, (count, tokens), 1).astype(f32)
-        for group in range(groups):
-            side = side_ref[group].reshape(count, lanes).astype(f32)
+        column = lax.broadcasted_iota(jnp.int32, (rows_out, tokens), 1).astype(f32)
+        for place in range(places):
+            side = jnp.concatenate([ref[...] for ref in sides[place]], axis=0)
+            side = side.reshape(rows_out, lanes).astype(f32)
             match = jnp.where(column == side[:, 1:2], 1.0, 0.0).astype(bf16)
-            rows = jnp.dot(match, rows_ref[group], preferred_element_type=f32)
+            rows = jnp.dot(match, rows_ref[group_ref[place]], preferred_element_type=f32)
             made = (side[:, 0:1] * rows).astype(bf16)
-            weighted[:, group] = made.reshape(per_expert, slots, width)
-
-    acts = acts_ref[:, 0].reshape(groups * slots, acts_ref.shape[3])
+            weighted[:, place] = made.reshape(per_expert, slots, width)
+
+    acts = acts_of(acts_refs, expert, out_ref.shape[1])
     out_ref[0] = lax.dot_general(
         acts,
-        weighted[expert].reshape(groups * slots, width),
+        weighted[expert].reshape(places * slots, width),
         (((0,), (0,)), ((), ())),
         preferred_element_type=f32,
     ).astype(bf16)
@@ -174,19 +183,6 @@
     ).astype(bf16)
     acts_block = jnp.concatenate([expert_acts[:, 0], side], axis=2)
 
-    acts_all = lax.all_gather(acts_block, "dp", axis=0, tiled=False)
-    proj = pl.pallas_call(
-        proj_kernel,
-        grid=(per_expert,),
-        in_specs=[
-            pl.BlockSpec((dp_count, 1, capacity, hidden_width), lambda e: (0, e, 0, 0)),
-            pl.BlockSpec((1, hidden_width, block), lambda e: (e, 0, 0)),
-        ],
-        out_specs=pl.BlockSpec((dp_count, 1, capacity, block), lambda e: (0, e, 0, 0)),
-        out_shape=jax.ShapeDtypeStruct((dp_count, per_expert, capacity, block), f32),
-        compiler_params=pltpu.CompilerParams(vmem_limit_bytes=32 * 1024 * 1024),
-    )(acts_all, down_weight)
-
     def logits_of(rows, offset, first, piece):
         features = lax.dynamic_index_in_dim(
             chip_normed, lax.rem(z_index + offset, nz), 0, keepdims=False
@@ -194,37 +190,86 @@
         return jnp.dot(features, piece, preferred_element_type=f32)
 
     everything = slice(0, 2 * tokens)
-    ahead = back = head_weight
-    head_pieces = [(0, 0, head_weight)]
-    partial = None
+    ahead = lax.ppermute(head_weight, "dp", z_shift(1, nz))
+    back = lax.ppermute(head_weight, "dp", z_shift(-1, nz))
+    head_pieces = [(0, 0, head_weight), (nz - 1, 0, ahead), (1, 0, back)]
+
+    acts_ahead = acts_back = acts_block
+    acts_pieces = [acts_block]
     for step in range(1, nz // 2):
-        if step == 2:
-            ahead, back, chip_normed = lax.optimization_barrier((ahead, back, chip_normed))
-        if step > 2:
-            ahead, back, partial = lax.optimization_barrier((ahead, back, partial))
-        if step >= 2:
-            done = head_pieces[-2:] if step > 2 else head_pieces
-            for offset, first, piece in done:
-                added = logits_of(everything, offset, first, piece)
-                partial = added if partial is None else partial + added
+        acts_ahead = lax.ppermute(acts_ahead, "dp", z_shift(1, nz))
+        acts_back = lax.ppermute(acts_back, "dp", z_shift(-1, nz))
+        acts_pieces += [acts_ahead, acts_back]
+    ahead, back, chip_normed, acts_ahead, acts_back = lax.optimization_barrier(
+        (ahead, back, chip_normed, acts_ahead, acts_back)
+    )
+    ahead = lax.ppermute(ahead, "dp", z_shift(1, nz))
+    back = lax.ppermute(back, "dp", z_shift(-1, nz))
+    acts_half = per_expert // 2
+    acts_pieces += [
+        lax.ppermute(acts_ahead[:acts_half], "dp", z_shift(1, nz)),
+        lax.ppermute(acts_back[acts_half:], "dp", z_shift(-1, nz)),
+    ]
+    acts_pieces += [swap(piece) for piece in acts_pieces]
+    partial = logits_of(everything, *head_pieces[0])
+    for piece in head_pieces[1:]:
+        partial = partial + logits_of(everything, *piece)
+    head_pieces += [(nz - 2, 0, ahead), (2, 0, back)]
+
+    offsets = [0]
+    for step in range(1, nz // 2):
+        offsets += [nz - step, step]
+    z_of = lax.rem(z_index + jnp.array(offsets + [nz // 2], jnp.int32), nz)
+    group_of = jnp.concatenate([2 * z_of + core, 2 * z_of + 1 - core]).astype(jnp.int32)
+
+    def acts_spec(at):
+        at = at % (nz + 1)
+        if at < nz - 1:
+            return pl.BlockSpec((1, capacity, hidden_width), lambda e, group: (e, 0, 0))
+        if at == nz - 1:
+            return pl.BlockSpec(
+                (1, capacity, hidden_width), lambda e, group: (jnp.minimum(e, acts_half - 1), 0, 0)
+            )
+        return pl.BlockSpec(
+            (1, capacity, hidden_width), lambda e, group: (jnp.maximum(e - acts_half, 0), 0, 0)
+        )
+
+    acts_specs = [acts_spec(at) for at in range(2 * nz + 2)]
+    proj = pl.pallas_call(
+        proj_kernel,
+        grid_spec=pltpu.PrefetchScalarGridSpec(
+            num_scalar_prefetch=1,
+            grid=(per_expert,),
+            in_specs=[pl.BlockSpec((1, hidden_width, block), lambda e, group: (e, 0, 0))]
+            + acts_specs,
+            out_specs=pl.BlockSpec((dp_count, 1, capacity, block), lambda e, group: (0, e, 0, 0)),
+        ),
+        out_shape=jax.ShapeDtypeStruct((dp_count, per_expert, capacity, block), f32),
+        compiler_params=pltpu.CompilerParams(vmem_limit_bytes=58 * 1024 * 1024),
+    )(group_of, down_weight, *acts_pieces)
+    for step in range(3, nz // 2):
+        ahead, back, partial, proj = lax.optimization_barrier((ahead, back, partial, proj))
         ahead = lax.ppermute(ahead, "dp", z_shift(1, nz))
         back = lax.ppermute(back, "dp", z_shift(-1, nz))
+        for piece in head_pieces[-2:]:
+            partial = partial + logits_of(everything, *piece)
         head_pieces += [(nz - step, 0, ahead), (step, 0, back)]
-    ahead, back, partial, proj = lax.optimization_barrier((ahead, back, partial, proj))
+    turned_proj = lax.all_to_all(
+        proj.reshape(dp_count, per_expert * capacity, block), "mp", 0, 0, tiled=True
+    )
+
+    ahead, back, partial = lax.optimization_barrier((ahead, back, partial))
     half = block // 2
     last_pieces = [
         (nz // 2, 0, lax.ppermute(ahead[:half], "dp", z_shift(1, nz))),
         (nz // 2, half, lax.ppermute(back[half:], "dp", z_shift(-1, nz))),
     ]
-    turned_proj = lax.all_to_all(
-        proj.reshape(dp_count, per_expert * capacity, block), "mp", 0, 0, tiled=True
-    )
-    for offset, first, piece in head_pieces[-2:]:
-        partial = partial + logits_of(everything, offset, first, piece)
+    for piece in head_pieces[-2:]:
+        partial = partial + logits_of(everything, *piece)
     own_part, other_part = partial[:tokens], partial[tokens:]
-    for offset, first, piece in last_pieces:
-        other_part = other_part + logits_of(slice(tokens, None), offset, first, piece)
-        own_part = own_part + logits_of(slice(0, tokens), offset, first, piece)
+    for piece in last_pieces:
+        other_part = other_part + logits_of(slice(tokens, None), *piece)
+        own_part = own_part + logits_of(slice(0, tokens), *piece)
     head_pieces += last_pieces
     logits = own_part + swap(other_part)
 
@@ -237,6 +282,7 @@
     local_mean = jnp.sum(local_exp * logits, axis=1)
     local_picked = jnp.sum(jnp.where(onehot, logits, 0.0), axis=1)
     stats = jnp.stack([local_top, local_total, local_mean, local_picked])
+    stats, turned_proj = lax.optimization_barrier((stats, turned_proj))
     stats = lax.all_to_all(
         jnp.broadcast_to(stats[None], (mp_count, 4, tokens)), "mp", 0, 0, tiled=True
     )
@@ -260,24 +306,17 @@
     place = jnp.stack([z_index, core]).astype(jnp.int32)
     hidden = pl.pallas_call(
         functools.partial(hidden_kernel, nz),
-        grid_spec=pltpu.PrefetchScalarGridSpec(
-            num_scalar_prefetch=1,
-            grid=(1,),
-            in_specs=[pl.BlockSpec((2 * tokens, vocab_dev), lambda n, place: (0, 0))]
-            + [pl.BlockSpec(memory_space=pl.ANY)] * (nz + 1),
-            out_specs=pl.BlockSpec((mp_count, tokens, block), lambda n, place: (0, 0, 0)),
-            scratch_shapes=[
-                pltpu.VMEM((nz, block, vocab_dev), bf16),
-                pltpu.SemaphoreType.DMA((nz + 1,)),
-            ],
-        ),
-        out_shape=jax.ShapeDtypeStruct((mp_count, tokens, block), f32),
+        in_specs=[pl.BlockSpec(memory_space=pltpu.SMEM)]
+        + [pl.BlockSpec(memory_space=pltpu.VMEM)] * (nz + 2),
+        out_specs=pl.BlockSpec(memory_space=pltpu.VMEM),
+        out_shape=jax.ShapeDtypeStruct((mp_count, block, tokens), bf16),
         compiler_params=pltpu.CompilerParams(vmem_limit_bytes=40 * 1024 * 1024),
     )(place, chip_grad, *[piece for _, _, piece in head_pieces])
 
-    hidden, turned_proj = lax.optimization_barrier((hidden, turned_proj))
-    hidden_grad = jnp.sum(lax.all_to_all(hidden, "mp", 0, 0, tiled=True), axis=0)
-    hidden_grad = lax.ppermute(hidden_grad, both, sum_turn(nz))
+    hidden_grad = jnp.sum(
+        lax.all_to_all(hidden, "mp", 0, 0, tiled=True).astype(f32), axis=0
+    )
+    hidden_grad = lax.ppermute(hidden_grad.T, both, sum_turn(nz))
 
     my_gain = lax.dynamic_slice_in_dim(norm_gain, dp_index * block, block, 0)
     turned_rms, turned_inner = turned_rows[0][:, None], turned_rows[1][:, None]
@@ -296,23 +335,31 @@
         out_shape=jax.ShapeDtypeStruct((mp_count, per_expert * capacity), f32),
         compiler_params=pltpu.CompilerParams(vmem_limit_bytes=32 * 1024 * 1024),
     )(turned_slots, stream_grad, turned_proj)
+    gate = lax.ppermute(gate, both, turn)
+    gate, all_rows, resid_grad = lax.optimization_barrier((gate, all_rows, resid_grad))
     down_grad = pl.pallas_call(
         down_kernel,
-        grid=(per_expert,),
-        in_specs=[
-            pl.BlockSpec(
-                (dp_count, per_expert, capacity, lanes), lambda e: (0, 0, 0, hidden_width // lanes)
-            ),
-            pl.BlockSpec((dp_count, tokens, block), lambda e: (0, 0, 0)),
-            pl.BlockSpec((dp_count, 1, capacity, hidden_width), lambda e: (0, e, 0, 0)),
-        ],
-        out_specs=pl.BlockSpec((1, hidden_width, block), lambda e: (e, 0, 0)),
+        grid_spec=pltpu.PrefetchScalarGridSpec(
+            num_scalar_prefetch=1,
+            grid=(per_expert,),
+            in_specs=[
+                pl.BlockSpec((dp_count, tokens, block), lambda e, group: (0, 0, 0)),
+            ]
+            + [
+                pl.BlockSpec(
+                    (piece.shape[0], capacity, lanes),
+                    lambda e, group: (0, 0, hidden_width // lanes),
+                )
+                for piece in acts_pieces
+            ]
+            + acts_specs,
+            out_specs=pl.BlockSpec((1, hidden_width, block), lambda e, group: (e, 0, 0)),
+            scratch_shapes=[pltpu.VMEM((per_expert, dp_count, capacity, block), bf16)],
+        ),
         out_shape=jax.ShapeDtypeStruct((per_expert, hidden_width, block), bf16),
-        scratch_shapes=[pltpu.VMEM((per_expert, dp_count, capacity, block), bf16)],
-        compiler_params=pltpu.CompilerParams(vmem_limit_bytes=40 * 1024 * 1024),
-    )(acts_all, all_rows, acts_all)
-
-    gate = lax.ppermute(gate, both, turn)
+        compiler_params=pltpu.CompilerParams(vmem_limit_bytes=58 * 1024 * 1024),
+    )(group_of, all_rows, *acts_pieces, *acts_pieces)
+
     slot_gate = jnp.sum(
         lax.all_to_all(
             jnp.broadcast_to(gate[None], (mp_count,) + gate.shape), "mp", 0, 0, tiled=True

time: 336 us -> 316 us (0.940)
  starting transfers between devices: 58.5 us -> 99.8 us
  blocking collectives: 45.4 us -> 13 us
  waiting for transfers between devices: 146 us -> 126 us
  between operations: 14.6 us -> 1.42 us
  local copies, waits for them, and re-layouts: 19.4 us -> 15.9 us
    ppermute x3 -> x2, waiting for transfers between devices: 77.9 us -> 15.7 us  [local(): ahead = lax.ppermute(ahead, 'dp', z_shift(1, nz))]
    ppermute x1 -> x20, waiting for transfers between devices: 0.01 us -> 58.3 us  [the longest x3 31 us: local(): acts_ahead = lax.ppermute(acts_ahead, 'dp', z_shift(1, nz))]
    all_to_all x1 -> x0, blocking collectives: 32.4 us -> none  [local(): lax.all_to_all(jnp.broadcast_to(gate[None], (mp_count,) + gate.shape), 'm...]
    ppermute x1 -> x20, starting transfers between devices: 0.67 us -> 29 us  [the longest x9 9.7 us: local(): acts_pieces += [swap(piece) for piece in acts_pieces]]
    ppermute x1, waiting for transfers between devices: 0.59 us -> 27 us  [local(): lax.ppermute(slot_token.reshape(mp_count, per_expert * capacity).T, both,...]
    all_to_all x1, starting transfers between devices: 3.79 us -> 24.2 us  [local(): lax.all_to_all(jnp.broadcast_to(stream_grad[None], (mp_count, tokens, blo...]
    ppermute x1, waiting for transfers between devices: 17.9 us -> 0.01 us  [local(): resid_grad = lax.ppermute(turned_resid, both, turn)]
    all_to_all x1, waiting for transfers between devices: 10.1 us -> 0.01 us  [local(): lax.all_to_all(proj.reshape(dp_count, per_expert * capacity, block), 'mp'...]
  transfers between devices with their start and end apart: 21 -> 38, of which waited for: 16 -> 15; matrix products, arithmetic and copies ran while one was open for 9% -> 12% of each run, Pallas kernels for 4% -> 6%
where the time goes in v4:
time: 316 us; the launch traced here: 313 us
  waiting for transfers between devices  126 us (40%)
  starting transfers between devices  99.8 us (32%)
  Pallas kernels  23.2 us (7%)
  matrix products  17.1 us (5%)
  other arithmetic  16.3 us (5%)
  local copies, waits for them, and re-layouts  15.9 us (5%)
  blocking collectives  13 us (4%)
    ppermute x3, waiting for transfers between devices, local(): acts_ahead = lax.ppermute(acts_ahead, 'dp', z_shift(1, nz))  31 us
    ppermute x1, waiting for transfers between devices, local(): lax.ppermute(slot_token.reshape(mp_count, per_expert * capacity).T, both,...  27 us
    all_to_all x1, starting transfers between devices, local(): lax.all_to_all(jnp.broadcast_to(stream_grad[None], (mp_count, tokens, blo...  24.2 us
    ppermute x1, waiting for transfers between devices, local(): lax.ppermute(acts_ahead[:acts_half], 'dp', z_shift(1, nz))  22.8 us
    dot_general x11, matrix products, logits_of(): return jnp.dot(features, piece, preferred_element_type=f32)  17.1 us
    ppermute x2, waiting for transfers between devices, local(): ahead = lax.ppermute(ahead, 'dp', z_shift(1, nz))  15.7 us
    all_to_all x1, blocking collectives, local(): lax.all_to_all(jnp.broadcast_to(stats[None], (mp_count, 4, tokens)), 'mp'...  13 us
    all_to_all x1, waiting for transfers between devices, local(): lax.all_to_all(hidden, 'mp', 0, 0, tiled=True).astype(f32)  10.3 us
  transfers between devices with their start and end apart: 38, of which 15 were waited for; matrix products, arithmetic and copies ran while one was open for 12% of the time, Pallas kernels for 6%

profile of v4, /device:TPU:1, one launch (start us, length us, event | category | flops | bytes accessed | tf_op | source)
XLA Modules:
  0.0 312.5 jit_solution(6839062443642689383)
XLA Ops:
  3.2 4.0 %collective-permute-start.2 = (bf16[256,2432]{1,0:T(8,128)(2,1)}, bf16[256,2432]{1,0:T(8,128)(2,1)S(1)}, u32[]{:S(2)}, u32[]{:S(2)}) collective-permute-start(bf16[256,2432]{1,0:T(8,128)(2,1)} %refs_0_.1), channel_id=1, source_target_pairs={{0,224},{16,240},{32,0},{48,16},{64,32},{80,48},{96,64},{112,80},{... | collective-permute-start | bytes 3735560 | tf_op jit(solution)/shard_map/ppermute | solution.py:194
  19.2 24.4 %collective-permute-done.4.refs_1_.refs_19_ = bf16[4,32,1664]{2,1,0:T(8,128)(2,1)} collective-permute-done((bf16[4,32,1664]{2,1,0:T(8,128)(2,1)}, bf16[4,32,1664]{2,1,0:T(8,128)(2,1)}, u32[]{:S(2)}, u32[]{:S(2)}) %collective-permute-start.4) | collective-permute-done | bytes 426016 | tf_op jit(solution)/shard_map/ppermute | solution.py:200
  47.0 3.0 collective-permute-start.8
  49.9 5.3 %collective-permute-done.5.refs_3_.refs_21_ = bf16[4,32,1664]{2,1,0:T(8,128)(2,1)} collective-permute-done((bf16[4,32,1664]{2,1,0:T(8,128)(2,1)}, bf16[4,32,1664]{2,1,0:T(8,128)(2,1)}, u32[]{:S(2)}, u32[]{:S(2)}) %collective-permute-start.5) | collective-permute-done | bytes 426016 | tf_op jit(solution)/shard_map/ppermute | solution.py:200
  55.3 4.2 %collective-permute-done.8.refs_4_.refs_22_ = bf16[4,32,1664]{2,1,0:T(8,128)(2,1)} collective-permute-done((bf16[4,32,1664]{2,1,0:T(8,128)(2,1)}, bf16[4,32,1664]{2,1,0:T(8,128)(2,1)}, u32[]{:S(2)}, u32[]{:S(2)}) %collective-permute-start.8) | collective-permute-done | bytes 426016 | tf_op jit(solution)/shard_map/ppermute | solution.py:201
  59.5 3.4 %collective-permute-start.9 = (bf16[4,32,1664]{2,1,0:T(8,128)(2,1)}, bf16[4,32,1664]{2,1,0:T(8,128)(2,1)S(1)}, u32[]{:S(2)}, u32[]{:S(2)}) collective-permute-start(bf16[4,32,1664]{2,1,0:T(8,128)(2,1)} %collective-permute-done.8.refs_4_.refs_22_), channel_id=1, source_target_pairs={{0,224},{16,240},{32,0},{48,16},{64,32},{80,48},{96,64},{112,80},{... | collective-permute-start | bytes 1277960 | tf_op jit(solution)/shard_map/ppermute | solution.py:201
  65.9 3.1 collective-permute-start.17
  79.8 2.9 collective-permute-start.13
  82.7 22.8 %collective-permute-done.12.refs_7_.refs_25_ = bf16[2,32,1664]{2,1,0:T(8,128)(2,1)S(1)} collective-permute-done((bf16[2,32,1664]{2,1,0:T(8,128)(2,1)S(1)}, bf16[2,32,1664]{2,1,0:T(8,128)(2,1)S(1)}, u32[]{:S(2)}, u32[]{:S(2)}) %collective-permute-start.12) | collective-permute-done | bytes 213024 | tf_op jit(solution)/shard_map/ppermute | solution.py:210
  114.3 7.2 %shard_map.139 = f32[16,4,32,256]{3,2,1,0:T(8,128)} custom-call(s32[16]{0:T(128)} %pad_add_fusion.group_ref, bf16[4,1536,256]{2,1,0:T(8,128)(2,1)} %down_ref.1, bf16[4,32,1664]{2,1,0:T(8,128)(2,1)} %pad_maximum_fusion.2.refs_0_.refs_18_, bf16[4,32,1664]{2,1,0:T(8,128)(2,1)} %collective-permute-done.4.refs_1_.refs_19_, ...), custom_call_target="tpu_custom_call" | custom-call | tf_op jit(solution)/shard_map/pallas_call | solution.py:238
  125.3 6.8 %all-to-all-start = ((f32[16,128,256]{2,1,0:T(8,128)}), f32[16,128,256]{2,1,0:T(8,128)S(1)}, u32[]{:S(2)}, u32[]{:S(2)}) async-start(f32[16,128,256]{2,1,0:T(8,128)} %bitcast.86), calls=%async_computation | async-start | bytes 4194304 | tf_op jit(solution)/shard_map/all_to_all | solution.py:257
  136.2 15.7 %collective-permute-done.23.refs_5_ = bf16[256,2432]{1,0:T(8,128)(2,1)S(1)} collective-permute-done((bf16[256,2432]{1,0:T(8,128)(2,1)}, bf16[256,2432]{1,0:T(8,128)(2,1)S(1)}, u32[]{:S(2)}, u32[]{:S(2)}) %collective-permute-start.23) | collective-permute-done | bytes 1245216 | tf_op jit(solution)/shard_map/ppermute | solution.py:252
  159.5 8.3 %collective-permute-done.25.refs_7_ = bf16[128,2432]{1,0:T(8,128)(2,1)S(1)} collective-permute-done((bf16[128,2432]{1,0:T(8,128)(2,1)S(1)}, bf16[128,2432]{1,0:T(8,128)(2,1)S(1)}, u32[]{:S(2)}, u32[]{:S(2)}) %collective-permute-start.25) | collective-permute-done | bytes 622624 | tf_op jit(solution)/shard_map/ppermute | solution.py:264
  178.2 13.0 %all_to_all.25 = f32[16,4,128]{2,1,0:T(4,128)S(1)} all-to-all(f32[16,4,128]{2,1,0:T(4,128)S(1)} %broadcast_in_dim.140), channel_id=1, replica_groups=mesh['dp'=16,'mp'=16] {'mp'}, dimensions={0} | all-to-all | bytes 65536 | tf_op jit(solution)/shard_map/all_to_all | solution.py:286
  198.3 5.3 %shard_map.140 = bf16[16,256,128]{2,1,0:T(8,128)(2,1)S(1)} custom-call(s32[2]{0:T(128)S(1)} %pad_add_fusion.1.place_ref, bf16[256,2432]{1,0:T(8,128)(2,1)S(1)} %pad_maximum_fusion.grad_ref, bf16[256,2432]{1,0:T(8,128)(2,1)S(1)} %copy-done.9, bf16[256,2432]{1,0:T(8,128)(2,1)S(1)} %copy-done.6, bf16[256,2432]{1,0:T(8,128)(2,1)S(1)} %copy-done.8, ...), custom_call_target="tpu_custom_call" | custom-call | tf_op jit(solution)/shard_map/pallas_call | solution.py:307
  204.7 3.8 %all-to-all-start.2 = ((bf16[16,256,128]{2,1,0:T(8,128)(2,1)}), bf16[16,256,128]{2,1,0:T(8,128)(2,1)S(1)}, u32[]{:S(2)}, u32[]{:S(2)}) async-start(bf16[16,256,128]{2,1,0:T(8,128)(2,1)} %copy-done.10), calls=%async_computation.2 | async-start | bytes 2097152 | tf_op jit(solution)/shard_map/all_to_all | solution.py:317
  209.3 3.7 %collective-permute-start.31 = (bf16[128,256]{1,0:T(8,128)(2,1)S(1)}, bf16[128,256]{1,0:T(8,128)(2,1)S(1)}, u32[]{:S(2)}, u32[]{:S(2)}) collective-permute-start(bf16[128,256]{1,0:T(8,128)(2,1)S(1)} %constant_dynamic-slice_fusion), channel_id=1, source_target_pairs={{0,0},{1,16},{2,32},{3,48},{4,64},{5,80},{6,96},{7,112},{8,128},{9... | collective-permute-start | bytes 196616 | tf_op jit(solution)/shard_map/ppermute | solution.py:155
  215.7 10.3 %all-to-all-done.2 = bf16[16,256,128]{2,1,0:T(8,128)(2,1)S(1)} async-done(((bf16[16,256,128]{2,1,0:T(8,128)(2,1)}), bf16[16,256,128]{2,1,0:T(8,128)(2,1)S(1)}, u32[]{:S(2)}, u32[]{:S(2)}) %all-to-all-start.2) | async-done | bytes 1048608 | tf_op jit(solution)/shard_map/all_to_all | solution.py:317
  229.7 24.2 %all-to-all-start.3 = ((bf16[16,128,256]{2,1,0:T(8,128)(2,1)}), bf16[16,128,256]{2,1,0:T(8,128)(2,1)S(1)}, u32[]{:S(2)}, u32[]{:S(2)}) async-start(bf16[16,128,256]{2,1,0:T(8,128)(2,1)} %broadcast_in_dim.141), calls=%async_computation.3 | async-start | bytes 2097152 | tf_op jit(solution)/shard_map/all_to_all | solution.py:330
  253.9 4.2 %collective-permute-start.33 = (f32[128,256]{1,0:T(8,128)S(1)}, f32[128,256]{1,0:T(8,128)}, u32[]{:S(2)}, u32[]{:S(2)}) collective-permute-start(f32[128,256]{1,0:T(8,128)S(1)} %get-tuple-element.43), channel_id=1, source_target_pairs={{0,0},{1,16},{2,32},{3,48},{4,64},{5,80},{6,96},{7,112},{8,128},{9... | collective-permute-start | bytes 393224 | tf_op jit(solution)/shard_map/ppermute | solution.py:328
  260.2 27.0 %collective-permute-done.slot_token_ref = s32[128,16]{1,0:T(8,128)S(1)} collective-permute-done((s32[128,16]{1,0:T(8,128)S(1)}, s32[128,16]{1,0:T(8,128)S(1)}, u32[]{:S(2)}, u32[]{:S(2)}) %collective-permute-start) | collective-permute-done | bytes 8224 | tf_op jit(solution)/shard_map/ppermute | solution.py:175
  289.8 4.3 %collective-permute-start.32 = (f32[16,128]{1,0:T(8,128)S(1)}, f32[16,128]{1,0:T(8,128)S(1)}, u32[]{:S(2)}, u32[]{:S(2)}) collective-permute-start(f32[16,128]{1,0:T(8,128)S(1)} %shard_map.141), channel_id=1, source_target_pairs={{0,0},{1,16},{2,32},{3,48},{4,64},{5,80},{6,96},{7,112},{8,128},{9... | collective-permute-start | bytes 24584 | tf_op jit(solution)/shard_map/ppermute | solution.py:338
  296.2 5.4 %all-to-all-start.4 = ((f32[16,16,128]{2,1,0:T(8,128)}), f32[16,16,128]{2,1,0:T(8,128)S(1)}, u32[]{:S(2)}, u32[]{:S(2)}) async-start(f32[16,16,128]{2,1,0:T(8,128)} %broadcast_in_dim.142), calls=%async_computation.4 | async-start | bytes 262144 | tf_op jit(solution)/shard_map/all_to_all | solution.py:364
  301.7 8.1 %shard_map.142 = bf16[4,1536,256]{2,1,0:T(8,128)(2,1)} custom-call(s32[16]{0:T(128)} %pad_add_fusion.group_ref, bf16[16,128,256]{2,1,0:T(8,128)(2,1)} %copy-done.17, bf16[4,32,1664]{2,1,0:T(8,128)(2,1)} %pad_maximum_fusion.2.refs_0_.refs_18_, bf16[4,32,1664]{2,1,0:T(8,128)(2,1)} %collective-permute-done.4.refs_1_.refs_19_, ...), custom_call_target="tpu_custom_call" | custom-call | tf_op jit(solution)/shard_map/pallas_call | solution.py:340
  (209 shorter events, 90.8 us)
Async XLA Ops:
  0.6 63.3 %collective-permute-start.1 = (bf16[256,2432]{1,0:T(8,128)(2,1)}, bf16[256,2432]{1,0:T(8,128)(2,1)S(1)}, u32[]{:S(2)}, u32[]{:S(2)}) collective-permute-start(bf16[256,2432]{1,0:T(8,128)(2,1)} %refs_0_.1), channel_id=1, source_target_pairs={{0,32},{16,48},{32,64},{48,80},{64,96},{80,112},{96,128},{112,144}... | collective-permute-start | bytes 3735560 | tf_op jit(solution)/shard_map/ppermute | solution.py:193
  3.2 60.9 %collective-permute-start.2 = (bf16[256,2432]{1,0:T(8,128)(2,1)}, bf16[256,2432]{1,0:T(8,128)(2,1)S(1)}, u32[]{:S(2)}, u32[]{:S(2)}) collective-permute-start(bf16[256,2432]{1,0:T(8,128)(2,1)} %refs_0_.1), channel_id=1, source_target_pairs={{0,224},{16,240},{32,0},{48,16},{64,32},{80,48},{96,64},{112,80},{... | collective-permute-start | bytes 3735560 | tf_op jit(solution)/shard_map/ppermute | solution.py:194
  12.3 31.4 %collective-permute-start.4 = (bf16[4,32,1664]{2,1,0:T(8,128)(2,1)}, bf16[4,32,1664]{2,1,0:T(8,128)(2,1)}, u32[]{:S(2)}, u32[]{:S(2)}) collective-permute-start(bf16[4,32,1664]{2,1,0:T(8,128)(2,1)} %pad_maximum_fusion.2.refs_0_.refs_18_), channel_id=1, source_target_pairs={{0,32},{16,48},{32,64},{48,80},{64,96},{80,112},{96,128},{112,144}... | collective-permute-start | bytes 1277960 | tf_op jit(solution)/shard_map/ppermute | solution.py:200
  12.3 34.7 %collective-permute-start.7 = (bf16[4,32,1664]{2,1,0:T(8,128)(2,1)}, bf16[4,32,1664]{2,1,0:T(8,128)(2,1)}, u32[]{:S(2)}, u32[]{:S(2)}) collective-permute-start(bf16[4,32,1664]{2,1,0:T(8,128)(2,1)} %pad_maximum_fusion.2.refs_0_.refs_18_), channel_id=1, source_target_pairs={{0,224},{16,240},{32,0},{48,16},{64,32},{80,48},{96,64},{112,80},{... | collective-permute-start | bytes 1277960 | tf_op jit(solution)/shard_map/ppermute | solution.py:201
  45.8 17.2 %collective-permute-start.3 = (bf16[8,128,256]{1,2,0:T(8,128)(2,1)S(1)}, bf16[8,128,256]{1,2,0:T(8,128)(2,1)}, u32[]{:S(2)}, u32[]{:S(2)}) collective-permute-start(bf16[8,128,256]{1,2,0:T(8,128)(2,1)S(1)} %get-tuple-element.51), channel_id=1, source_target_pairs={{0,16},{16,0},{32,48},{48,32},{64,80},{80,64},{96,112},{112,96},{1... | collective-permute-start | bytes 1572872 | tf_op jit(solution)/shard_map/ppermute | solution.py:153
  47.0 12.5 %collective-permute-start.8 = (bf16[4,32,1664]{2,1,0:T(8,128)(2,1)}, bf16[4,32,1664]{2,1,0:T(8,128)(2,1)}, u32[]{:S(2)}, u32[]{:S(2)}) collective-permute-start(bf16[4,32,1664]{2,1,0:T(8,128)(2,1)} %collective-permute-done.7.refs_2_.refs_20_), channel_id=1, source_target_pairs={{0,224},{16,240},{32,0},{48,16},{64,32},{80,48},{96,64},{112,80},{... | collective-permute-start | bytes 1277960 | tf_op jit(solution)/shard_map/ppermute | solution.py:201
  64.1 13.5 %collective-permute-start.16 = (bf16[4,32,1664]{2,1,0:T(8,128)(2,1)}, bf16[4,32,1664]{2,1,0:T(8,128)(2,1)}, u32[]{:S(2)}, u32[]{:S(2)}) collective-permute-start(bf16[4,32,1664]{2,1,0:T(8,128)(2,1)} %collective-permute-done.7.refs_2_.refs_20_), channel_id=1, source_target_pairs={{0,16},{16,0},{32,48},{48,32},{64,80},{80,64},{96,112},{112,96},{1... | collective-permute-start | bytes 1277960 | tf_op jit(solution)/shard_map/ppermute | solution.py:213
  71.6 49.9 %collective-permute-start.10 = (bf16[256,2432]{1,0:T(8,128)(2,1)S(1)}, bf16[256,2432]{1,0:T(8,128)(2,1)}, u32[]{:S(2)}, u32[]{:S(2)}) collective-permute-start(bf16[256,2432]{1,0:T(8,128)(2,1)S(1)} %collective-permute-done.1.refs_1_), channel_id=1, source_target_pairs={{0,32},{16,48},{32,64},{48,80},{64,96},{80,112},{96,128},{112,144}... | collective-permute-start | bytes 3735560 | tf_op jit(solution)/shard_map/ppermute | solution.py:206
  72.5 49.1 %collective-permute-start.11 = (bf16[256,2432]{1,0:T(8,128)(2,1)S(1)}, bf16[256,2432]{1,0:T(8,128)(2,1)}, u32[]{:S(2)}, u32[]{:S(2)}) collective-permute-start(bf16[256,2432]{1,0:T(8,128)(2,1)S(1)} %collective-permute-done.2.refs_2_), channel_id=1, source_target_pairs={{0,224},{16,240},{32,0},{48,16},{64,32},{80,48},{96,64},{112,80},{... | collective-permute-start | bytes 3735560 | tf_op jit(solution)/shard_map/ppermute | solution.py:207
  77.6 27.8 %collective-permute-start.12 = (bf16[2,32,1664]{2,1,0:T(8,128)(2,1)S(1)}, bf16[2,32,1664]{2,1,0:T(8,128)(2,1)S(1)}, u32[]{:S(2)}, u32[]{:S(2)}) collective-permute-start(bf16[2,32,1664]{2,1,0:T(8,128)(2,1)S(1)} %slice.49), channel_id=1, source_target_pairs={{0,32},{16,48},{32,64},{48,80},{64,96},{80,112},{96,128},{112,144}... | collective-permute-start | bytes 638984 | tf_op jit(solution)/shard_map/ppermute | solution.py:210
  77.7 31.7 %collective-permute-start.19 = (bf16[4,32,1664]{2,1,0:T(8,128)(2,1)S(1)}, bf16[4,32,1664]{2,1,0:T(8,128)(2,1)S(1)}, u32[]{:S(2)}, u32[]{:S(2)}) collective-permute-start(bf16[4,32,1664]{2,1,0:T(8,128)(2,1)S(1)} %collective-permute-done.6.refs_5_.refs_23_), channel_id=1, source_target_pairs={{0,16},{16,0},{32,48},{48,32},{64,80},{80,64},{96,112},{112,96},{1... | collective-permute-start | bytes 1277960 | tf_op jit(solution)/shard_map/ppermute | solution.py:213
  79.8 29.5 %collective-permute-start.13 = (bf16[2,32,1664]{2,1,0:T(8,128)(2,1)S(1)}, bf16[2,32,1664]{2,1,0:T(8,128)(2,1)S(1)}, u32[]{:S(2)}, u32[]{:S(2)}) collective-permute-start(bf16[2,32,1664]{2,1,0:T(8,128)(2,1)S(1)} %slice.50), channel_id=1, source_target_pairs={{0,224},{16,240},{32,0},{48,16},{64,32},{80,48},{96,64},{112,80},{... | collective-permute-start | bytes 638984 | tf_op jit(solution)/shard_map/ppermute | solution.py:211
  121.6 30.3 %collective-permute-start.23 = (bf16[256,2432]{1,0:T(8,128)(2,1)}, bf16[256,2432]{1,0:T(8,128)(2,1)S(1)}, u32[]{:S(2)}, u32[]{:S(2)}) collective-permute-start(bf16[256,2432]{1,0:T(8,128)(2,1)} %collective-permute-done.10.refs_3_), channel_id=1, source_target_pairs={{0,32},{16,48},{32,64},{48,80},{64,96},{80,112},{96,128},{112,144}... | collective-permute-start | bytes 3735560 | tf_op jit(solution)/shard_map/ppermute | solution.py:252
  121.9 30.0 %collective-permute-start.24 = (bf16[256,2432]{1,0:T(8,128)(2,1)}, bf16[256,2432]{1,0:T(8,128)(2,1)}, u32[]{:S(2)}, u32[]{:S(2)}) collective-permute-start(bf16[256,2432]{1,0:T(8,128)(2,1)} %collective-permute-done.11.refs_4_), channel_id=1, source_target_pairs={{0,224},{16,240},{32,0},{48,16},{64,32},{80,48},{96,64},{112,80},{... | collective-permute-start | bytes 3735560 | tf_op jit(solution)/shard_map/ppermute | solution.py:253
  125.3 52.8 %all-to-all-start = ((f32[16,128,256]{2,1,0:T(8,128)}), f32[16,128,256]{2,1,0:T(8,128)S(1)}, u32[]{:S(2)}, u32[]{:S(2)}) async-start(f32[16,128,256]{2,1,0:T(8,128)} %bitcast.86), calls=%async_computation | async-start | bytes 4194304 | tf_op jit(solution)/shard_map/all_to_all | solution.py:257
  151.9 15.9 %collective-permute-start.25 = (bf16[128,2432]{1,0:T(8,128)(2,1)S(1)}, bf16[128,2432]{1,0:T(8,128)(2,1)S(1)}, u32[]{:S(2)}, u32[]{:S(2)}) collective-permute-start(bf16[128,2432]{1,0:T(8,128)(2,1)S(1)} %slice.53), channel_id=1, source_target_pairs={{0,32},{16,48},{32,64},{48,80},{64,96},{80,112},{96,128},{112,144}... | collective-permute-start | bytes 1867784 | tf_op jit(solution)/shard_map/ppermute | solution.py:264
  154.2 14.6 %collective-permute-start.26 = (bf16[128,2432]{1,0:T(8,128)(2,1)S(1)}, bf16[128,2432]{1,0:T(8,128)(2,1)S(1)}, u32[]{:S(2)}, u32[]{:S(2)}) collective-permute-start(bf16[128,2432]{1,0:T(8,128)(2,1)S(1)} %slice.55), channel_id=1, source_target_pairs={{0,224},{16,240},{32,0},{48,16},{64,32},{80,48},{96,64},{112,80},{... | collective-permute-start | bytes 1867784 | tf_op jit(solution)/shard_map/ppermute | solution.py:265
  204.7 21.3 %all-to-all-start.2 = ((bf16[16,256,128]{2,1,0:T(8,128)(2,1)}), bf16[16,256,128]{2,1,0:T(8,128)(2,1)S(1)}, u32[]{:S(2)}, u32[]{:S(2)}) async-start(bf16[16,256,128]{2,1,0:T(8,128)(2,1)} %copy-done.10), calls=%async_computation.2 | async-start | bytes 2097152 | tf_op jit(solution)/shard_map/all_to_all | solution.py:317
  209.3 19.2 %collective-permute-start.31 = (bf16[128,256]{1,0:T(8,128)(2,1)S(1)}, bf16[128,256]{1,0:T(8,128)(2,1)S(1)}, u32[]{:S(2)}, u32[]{:S(2)}) collective-permute-start(bf16[128,256]{1,0:T(8,128)(2,1)S(1)} %constant_dynamic-slice_fusion), channel_id=1, source_target_pairs={{0,0},{1,16},{2,32},{3,48},{4,64},{5,80},{6,96},{7,112},{8,128},{9... | collective-permute-start | bytes 196616 | tf_op jit(solution)/shard_map/ppermute | solution.py:155
  213.8 14.8 %collective-permute-start.28 = (f32[2,128]{1,0:T(2,128)S(1)}, f32[2,128]{1,0:T(2,128)S(1)}, u32[]{:S(2)}, u32[]{:S(2)}) collective-permute-start(f32[2,128]{1,0:T(2,128)S(1)} %pad_maximum_fusion.4), channel_id=1, source_target_pairs={{0,0},{1,16},{2,32},{3,48},{4,64},{5,80},{6,96},{7,112},{8,128},{9... | collective-permute-start | bytes 3080 | tf_op jit(solution)/shard_map/ppermute | solution.py:299
  229.7 65.8 %all-to-all-start.3 = ((bf16[16,128,256]{2,1,0:T(8,128)(2,1)}), bf16[16,128,256]{2,1,0:T(8,128)(2,1)S(1)}, u32[]{:S(2)}, u32[]{:S(2)}) async-start(bf16[16,128,256]{2,1,0:T(8,128)(2,1)} %broadcast_in_dim.141), calls=%async_computation.3 | async-start | bytes 2097152 | tf_op jit(solution)/shard_map/all_to_all | solution.py:330
  253.9 41.6 %collective-permute-start.33 = (f32[128,256]{1,0:T(8,128)S(1)}, f32[128,256]{1,0:T(8,128)}, u32[]{:S(2)}, u32[]{:S(2)}) collective-permute-start(f32[128,256]{1,0:T(8,128)S(1)} %get-tuple-element.43), channel_id=1, source_target_pairs={{0,0},{1,16},{2,32},{3,48},{4,64},{5,80},{6,96},{7,112},{8,128},{9... | collective-permute-start | bytes 393224 | tf_op jit(solution)/shard_map/ppermute | solution.py:328
  258.3 28.9 %collective-permute-start = (s32[128,16]{1,0:T(8,128)S(1)}, s32[128,16]{1,0:T(8,128)S(1)}, u32[]{:S(2)}, u32[]{:S(2)}) collective-permute-start(s32[128,16]{1,0:T(8,128)S(1)} %bitcast.97), channel_id=1, source_target_pairs={{0,0},{1,16},{2,32},{3,48},{4,64},{5,80},{6,96},{7,112},{8,128},{9... | collective-permute-start | bytes 24584 | tf_op jit(solution)/shard_map/ppermute | solution.py:175
  296.2 13.5 %all-to-all-start.4 = ((f32[16,16,128]{2,1,0:T(8,128)}), f32[16,16,128]{2,1,0:T(8,128)S(1)}, u32[]{:S(2)}, u32[]{:S(2)}) async-start(f32[16,16,128]{2,1,0:T(8,128)} %broadcast_in_dim.142), calls=%async_computation.4 | async-start | bytes 262144 | tf_op jit(solution)/shard_map/all_to_all | solution.py:364
  (54 other events, 534.2 us)

commit v5 on v1

v5 whole, which is shorter than its diff:
```python
import functools

import jax
import jax.numpy as jnp
from jax import lax
from jax.experimental import pallas as pl
from jax.experimental.pallas import tpu as pltpu
from jax.sharding import PartitionSpec as P

clip_low = 0.8
clip_high = 1.2
norm_eps = 1e-06
f32 = jnp.float32
bf16 = jnp.bfloat16
lanes = 128


def z_shift(step, nz):
    return [(2 * z + c, 2 * ((z + step) % nz) + c) for z in range(nz) for c in range(2)]


def core_swap(nz):
    return [(2 * z + c, 2 * z + 1 - c) for z in range(nz) for c in range(2)]


def home_turn(nz):
    return [
        ((2 * z + c) * 16 + 2 * b + low, (2 * z + low) * 16 + 2 * b + c)
        for z in range(nz) for c in range(2) for b in range(nz) for low in range(2)
    ]


def sum_turn(nz):
    return [
        ((2 * z + c) * 16 + 2 * b + low, (2 * b + c) * 16 + 2 * z + low)
        for z in range(nz) for c in range(2) for b in range(nz) for low in range(2)
    ]


def proj_kernel(acts_ref, down_ref, proj_ref):
    groups, _, slots, wide = acts_ref.shape
    acts = acts_ref[:, 0].reshape(groups * slots, wide)
    out = jnp.dot(acts, down_ref[0], preferred_element_type=f32)
    proj_ref[...] = out.astype(proj_ref.dtype).reshape(proj_ref.shape)


def slot_kernel(side_ref, rows_ref, proj_ref, weighted_ref, gate_ref):
    groups, per_expert, slots, _ = side_ref.shape
    tokens, width = rows_ref.shape[1:]
    count = per_expert * slots
    column = lax.broadcasted_iota(jnp.int32, (count, tokens), 1)
    gates = jnp.zeros((count, lanes), f32)
    for group in range(groups):
        side = side_ref[group].reshape(count, lanes).astype(f32)
        match = jnp.where(column.astype(f32) == side[:, 1:2], 1.0, 0.0).astype(bf16)
        rows = jnp.dot(match, rows_ref[group], preferred_element_type=f32)
        proj = proj_ref[group].reshape(count, width)
        gate = jnp.sum(rows * proj, axis=1, keepdims=True)
        gates = jnp.where(column == group, gate, gates)
        weighted = (side[:, 0:1] * rows).astype(bf16)
        weighted_ref[:, group] = weighted.reshape(per_expert, slots, width)
    gate_ref[...] = gates.T[:groups]


def hidden_kernel(nz, place_ref, grad_ref, *refs):
    pieces, out_ref = refs[: nz + 1], refs[nz + 1]
    z_index, core = place_ref[0], place_ref[1]
    tokens = grad_ref.shape[0] // 2
    half = pieces[0].shape[0] // 2
    grad = grad_ref[...]
    for number in range(nz + 1):
        step = (number + 1) // 2
        offset = step if number % 2 == 0 else nz - step
        first = 0
        if number >= nz - 1:
            offset, first = nz // 2, half * (number - nz + 1)
        part = lax.dot_general(
            pieces[number][...], grad, (((1,), (1,)), ((), ())), preferred_element_type=f32
        ).astype(out_ref.dtype)
        rows = slice(first, first + part.shape[0])
        block = lax.rem(z_index + offset, nz)
        out_ref[2 * block + core, rows] = part[:, :tokens]
        out_ref[2 * block + 1 - core, rows] = part[:, tokens:]


def down_kernel(acts_ref, weighted_ref, out_ref):
    groups, _, slots, wide = acts_ref.shape
    acts = acts_ref[:, 0].reshape(groups * slots, wide)
    weighted = weighted_ref[0].reshape(groups * slots, weighted_ref.shape[3])
    out_ref[0] = lax.dot_general(
        acts, weighted, (((0,), (0,)), ((), ())), preferred_element_type=f32
    ).astype(bf16)


def local(
    residual,
    norm_gain,
    head_weight,
    token_ids,
    old_logp,
    advantages,
    resp_mask,
    routes,
    combine_weights,
    expert_acts,
    down_weight,
):
    tokens, model_width = residual.shape
    block, vocab_dev = head_weight.shape
    per_expert, _, capacity, hidden_width = expert_acts.shape
    dp_count = lax.axis_size("dp")
    mp_count = lax.axis_size("mp")
    nz = dp_count // 2
    dp_index = lax.axis_index("dp")
    mp_index = lax.axis_index("mp")
    z_index, core = dp_index // 2, dp_index % 2
    both = ("dp", "mp")
    experts_all = per_expert * mp_count
    swap = functools.partial(lax.ppermute, axis_name="dp", perm=core_swap(nz))

    stream = residual.astype(f32)
    inv_rms = lax.rsqrt(jnp.mean(stream * stream, axis=1, keepdims=True) + norm_eps)
    normed = (stream * inv_rms * norm_gain[None, :]).astype(bf16)
    by_block = normed.reshape(tokens, nz, 2, block).transpose(2, 1, 0, 3)
    mine = lax.dynamic_index_in_dim(by_block, core, 0, keepdims=False)
    theirs = lax.dynamic_index_in_dim(by_block, 1 - core, 0, keepdims=False)
    chip_normed = jnp.concatenate([mine, swap(theirs)], axis=1)

    low = mp_index % 2
    landed_block = mp_index - low + core
    other_stream = swap(
        lax.dynamic_slice_in_dim(residual, (mp_index - low + 1 - core) * block, block, 1)
    )
    landed_stream = jnp.where(
        low == core, lax.dynamic_slice_in_dim(residual, landed_block * block, block, 1), other_stream
    )

    expert_ids = jnp.arange(experts_all, dtype=jnp.int32)
    hit_routes = routes[:, :, None] == expert_ids[None, None, :]
    hit_token = jnp.sum(hit_routes.astype(jnp.int32), axis=1)
    before = jnp.cumsum(hit_token, axis=0) - hit_token
    slot_ids = jnp.arange(capacity, dtype=jnp.int32)
    matches = (hit_token.T[:, None, :] == 1) & (before.T[:, None, :] == slot_ids[None, :, None])
    weight_token = jnp.sum(
        jnp.where(hit_routes, combine_weights[:, :, None].astype(f32), 0.0), axis=1
    )
    first_expert = mp_index * per_expert
    own_matches = lax.dynamic_slice_in_dim(matches, first_expert, per_expert, 0)
    own_weights = lax.dynamic_slice_in_dim(weight_token, first_expert, per_expert, 1)
    token_numbers = jnp.arange(tokens, dtype=jnp.int32)
    slot_token = jnp.sum(jnp.where(own_matches, token_numbers[None, None, :] + 1, 0), axis=2) - 1
    slot_weight = jnp.sum(jnp.where(own_matches, own_weights.T[:, None, :], 0.0), axis=2)
    lane = jnp.arange(lanes, dtype=jnp.int32)
    side = jnp.where(
        lane == 0,
        slot_weight[:, :, None],
        jnp.where(lane == 1, slot_token.astype(f32)[:, :, None], 0.0),
    ).astype(bf16)
    acts_block = jnp.concatenate([expert_acts[:, 0], side], axis=2)

    def logits_of(rows, offset, first, piece):
        features = lax.dynamic_index_in_dim(
            chip_normed, lax.rem(z_index + offset, nz), 0, keepdims=False
        )[rows, first : first + piece.shape[0]]
        return jnp.dot(features, piece, preferred_element_type=f32)

    everything = slice(0, 2 * tokens)
    ahead = lax.ppermute(head_weight, "dp", z_shift(1, nz))
    back = lax.ppermute(head_weight, "dp", z_shift(-1, nz))
    head_pieces = [(0, 0, head_weight), (nz - 1, 0, ahead), (1, 0, back)]
    back, chip_normed, landed_stream, acts_block = lax.optimization_barrier(
        (back, chip_normed, landed_stream, acts_block)
    )
    partial, used = None, 0
    for step in range(2, nz // 2):
        if step > 2:
            back, partial = lax.optimization_barrier((back, partial))
        for piece in head_pieces[used:]:
            added = logits_of(everything, *piece)
            partial = added if partial is None else partial + added
        used = len(head_pieces)
        ahead = lax.ppermute(ahead, "dp", z_shift(1, nz))
        back = lax.ppermute(back, "dp", z_shift(-1, nz))
        head_pieces += [(nz - step, 0, ahead), (step, 0, back)]
    back, partial = lax.optimization_barrier((back, partial))
    half = block // 2
    last_pieces = [
        (nz // 2, 0, lax.ppermute(ahead[:half], "dp", z_shift(1, nz))),
        (nz // 2, half, lax.ppermute(back[half:], "dp", z_shift(-1, nz))),
    ]
    for piece in head_pieces[used:]:
        partial = partial + logits_of(everything, *piece)
    own_part, other_part = partial[:tokens], partial[tokens:]
    for piece in last_pieces:
        other_part = other_part + logits_of(slice(tokens, None), *piece)
        own_part = own_part + logits_of(slice(0, tokens), *piece)
    head_pieces += last_pieces
    logits = own_part + swap(other_part)

    acts_block, _ = lax.optimization_barrier((acts_block, tuple(p for _, _, p in last_pieces)))
    acts_all = lax.all_gather(acts_block, "dp", axis=0, tiled=False)
    proj = pl.pallas_call(
        proj_kernel,
        grid=(per_expert,),
        in_specs=[
            pl.BlockSpec((dp_count, 1, capacity, hidden_width), lambda e: (0, e, 0, 0)),
            pl.BlockSpec((1, hidden_width, block), lambda e: (e, 0, 0)),
        ],
        out_specs=pl.BlockSpec((dp_count, 1, capacity, block), lambda e: (0, e, 0, 0)),
        out_shape=jax.ShapeDtypeStruct((dp_count, per_expert, capacity, block), f32),
        compiler_params=pltpu.CompilerParams(vmem_limit_bytes=58 * 1024 * 1024),
    )(acts_all, down_weight)

    local_ids = token_ids - mp_index * vocab_dev
    column = jnp.arange(vocab_dev, dtype=jnp.int32)
    onehot = column[None, :] == local_ids[:, None]
    local_top = jnp.max(logits, axis=1)
    local_exp = jnp.exp(logits - local_top[:, None])
    local_total = jnp.sum(local_exp, axis=1)
    local_mean = jnp.sum(local_exp * logits, axis=1)
    local_picked = jnp.sum(jnp.where(onehot, logits, 0.0), axis=1)
    stats = jnp.stack([local_top, local_total, local_mean, local_picked])
    stats = lax.all_to_all(
        jnp.broadcast_to(stats[None], (mp_count, 4, tokens)), "mp", 0, 0, tiled=True
    )
    row_top = jnp.max(stats[:, 0], axis=0)
    rescale = jnp.exp(stats[:, 0] - row_top[None])
    row_total = jnp.sum(stats[:, 1] * rescale, axis=0)
    mean_logit = jnp.sum(stats[:, 2] * rescale, axis=0) / row_total
    picked = jnp.sum(stats[:, 3], axis=0)

    logp = picked - row_top - jnp.log(row_total)
    prob_ratio = jnp.exp(logp - old_logp)
    weight_row = -jnp.clip(prob_ratio, clip_low, clip_high) * advantages * resp_mask.astype(f32)
    inner = weight_row * (picked - mean_logit) / model_width
    own_rows = jnp.stack([inv_rms[:, 0], inner])
    landed_rows = jnp.where(low == core, own_rows, swap(own_rows))
    logit_grad = (
        weight_row[:, None]
        * (onehot.astype(f32) - jnp.exp(logits - row_top[:, None]) / row_total[:, None])
    ).astype(bf16)
    chip_grad = jnp.concatenate([logit_grad, swap(logit_grad)], axis=0)

    place = jnp.stack([z_index, core]).astype(jnp.int32)
    hidden = pl.pallas_call(
        functools.partial(hidden_kernel, nz),
        in_specs=[pl.BlockSpec(memory_space=pltpu.SMEM)]
        + [pl.BlockSpec(memory_space=pltpu.VMEM)] * (nz + 2),
        out_specs=pl.BlockSpec(memory_space=pltpu.VMEM),
        out_shape=jax.ShapeDtypeStruct((mp_count, block, tokens), f32),
        compiler_params=pltpu.CompilerParams(vmem_limit_bytes=40 * 1024 * 1024),
    )(place, chip_grad, *[piece for _, _, piece in head_pieces])

    hidden = lax.all_to_all(hidden, "mp", 0, 0, tiled=True)
    hidden_grad = jnp.sum(hidden, axis=0).T

    landed_gain = lax.dynamic_slice_in_dim(norm_gain, landed_block * block, block, 0)
    landed_rms, landed_inner = landed_rows[0][:, None], landed_rows[1][:, None]
    scaled_grad = landed_gain[None, :] * hidden_grad
    landed_resid = landed_rms * (
        scaled_grad - landed_stream.astype(f32) * landed_rms * landed_inner
    )
    resid_grad = lax.ppermute(landed_resid, both, home_turn(nz))
    stream_grad = lax.ppermute(landed_resid.astype(bf16), both, sum_turn(nz))

    all_rows = lax.all_to_all(
        jnp.broadcast_to(stream_grad[None], (mp_count, tokens, block)), "mp", 0, 0, tiled=True
    )
    all_rows, resid_grad, proj = lax.optimization_barrier((all_rows, resid_grad, proj))
    weighted, gate = pl.pallas_call(
        slot_kernel,
        grid=(1,),
        in_specs=[
            pl.BlockSpec(
                (dp_count, per_expert, capacity, lanes), lambda n: (0, 0, 0, hidden_width // lanes)
            ),
            pl.BlockSpec((dp_count, tokens, block), lambda n: (0, 0, 0)),
            pl.BlockSpec((dp_count, per_expert, capacity, block), lambda n: (0, 0, 0, 0)),
        ],
        out_specs=[
            pl.BlockSpec((per_expert, dp_count, capacity, block), lambda n: (0, 0, 0, 0)),
            pl.BlockSpec((dp_count, per_expert * capacity), lambda n: (0, 0)),
        ],
        out_shape=[
            jax.ShapeDtypeStruct((per_expert, dp_count, capacity, block), bf16),
            jax.ShapeDtypeStruct((dp_count, per_expert * capacity), f32),
        ],
        compiler_params=pltpu.CompilerParams(vmem_limit_bytes=56 * 1024 * 1024),
    )(acts_all, all_rows, proj)
    down_grad = pl.pallas_call(
        down_kernel,
        grid=(per_expert,),
        in_specs=[
            pl.BlockSpec((dp_count, 1, capacity, hidden_width), lambda e: (0, e, 0, 0)),
            pl.BlockSpec((1, dp_count, capacity, block), lambda e: (e, 0, 0, 0)),
        ],
        out_specs=pl.BlockSpec((1, hidden_width, block), lambda e: (e, 0, 0)),
        out_shape=jax.ShapeDtypeStruct((per_expert, hidden_width, block), bf16),
        compiler_params=pltpu.CompilerParams(vmem_limit_bytes=56 * 1024 * 1024),
    )(acts_all, weighted)

    gate = lax.all_to_all(
        jnp.broadcast_to(gate[:, None, :], (dp_count, mp_count, per_expert * capacity)).reshape(
            dp_count * mp_count, 1, per_expert * capacity
        ),
        both, 0, 0, tiled=True,
    ).reshape(dp_count, mp_count, per_expert * capacity)
    slot_gate = jnp.sum(gate, axis=0).reshape(experts_all, capacity)
    per_token = jnp.sum(jnp.where(matches, slot_gate[:, :, None], 0.0), axis=1)
    gate_grad = jnp.sum(jnp.where(hit_routes, per_token.T[:, None, :], 0.0), axis=2)
    return (resid_grad, down_grad, gate_grad)


def solution(mesh):
    placed = (
        P("dp", None),
        P(),
        P("dp", "mp"),
        P("dp"),
        P("dp"),
        P("dp"),
        P("dp"),
        P("dp", None),
        P("dp", None),
        P("mp", "dp", None, None),
        P("mp", None, "dp"),
    )
    return jax.shard_map(
        local,
        mesh=mesh,
        in_specs=placed,
        out_specs=(P("dp", "mp"), P("mp", None, "dp"), P("dp", None)),
        check_vma=False,
    )
```

time: 301 us -> 267 us (0.89)
  waiting for transfers between devices: 132 us -> 98.6 us
  local copies, waits for them, and re-layouts: 29.6 us -> 15.9 us
  between operations: 1.4 us -> 14.5 us
  other arithmetic: 16.1 us -> 23 us
  starting transfers between devices: 62.2 us -> 58 us
    ppermute x20 -> x13, waiting for transfers between devices: 91.9 us -> 58.7 us  [the longest x2 42 us: local(): ahead = lax.ppermute(ahead, 'dp', z_shift(1, nz))]
    unnamed x68 -> x46, local copies, waits for them, and re-layouts: 17 us -> 4.8 us
    ppermute x20 -> x13, starting transfers between devices: 33.8 us -> 24.8 us  [the longest x2 5.35 us: local(): back = lax.ppermute(back, 'dp', z_shift(-1, nz))]
    all_to_all x4 -> x3, starting transfers between devices: 24.5 us -> 30.3 us  [the longest x1 17.5 us: local(): lax.all_to_all(jnp.broadcast_to(stream_grad[None], (mp_count, tokens, blo...]
    concatenate x2 -> x0, local copies, waits for them, and re-layouts: 4.19 us -> none  [the longest x1 4.17 us: local(): acts_all = jnp.concatenate([acts_own, swap(acts_own)], axis=0)]
    convert_element_type x2 -> x1, other arithmetic: 3.2 us -> 0.11 us  [local(): stream_grad = lax.ppermute(landed_resid.astype(bf16), both, sum_turn(nz))]
    dot_general x18 -> x11, matrix products: 20.2 us -> 17.9 us  [logits_of(): return jnp.dot(features, piece, preferred_element_type=f32)]
    all_to_all x4 -> x3, waiting for transfers between devices: 40.2 us -> 38.2 us  [the longest x1 31.6 us: local(): hidden = lax.all_to_all(hidden, 'mp', 0, 0, tiled=True)]
  transfers between devices with their start and end apart: 26 -> 19, of which waited for: 10 -> 11; matrix products, arithmetic and copies ran while one was open for 18% -> 20% of each run, Pallas kernels for 4% -> 7%
where the time goes in v5:
time: 267 us; the launch traced here: 265 us
  waiting for transfers between devices  98.6 us (37%)
  starting transfers between devices  58 us (22%)
  Pallas kernels  24.7 us (9%)
  other arithmetic  23 us (9%)
  matrix products  17.9 us (7%)
  local copies, waits for them, and re-layouts  15.9 us (6%)
  between operations  14.5 us (5%)
  blocking collectives  13 us (5%)
    ppermute x2, waiting for transfers between devices, local(): ahead = lax.ppermute(ahead, 'dp', z_shift(1, nz))  42 us
    all_to_all x1, waiting for transfers between devices, local(): hidden = lax.all_to_all(hidden, 'mp', 0, 0, tiled=True)  31.6 us
    dot_general x11, matrix products, logits_of(): return jnp.dot(features, piece, preferred_element_type=f32)  17.9 us
    all_to_all x1, starting transfers between devices, local(): lax.all_to_all(jnp.broadcast_to(stream_grad[None], (mp_count, tokens, blo...  17.5 us
    all_to_all x1, blocking collectives, local(): lax.all_to_all(jnp.broadcast_to(stats[None], (mp_count, 4, tokens)), 'mp'...  13 us
    ppermute x1, waiting for transfers between devices, local(): lax.ppermute(ahead[:half], 'dp', z_shift(1, nz))  10.7 us
    all_to_all x1, starting transfers between devices, local(): lax.all_to_all(jnp.broadcast_to(gate[:, None, :], (dp_count, mp_count, pe...  8.92 us
    pallas_call x1, Pallas kernels, local(): pl.pallas_call(functools.partial(hidden_kernel, nz), in_specs=[pl.BlockSp...  6.51 us
  transfers between devices with their start and end apart: 19, of which 11 were waited for; matrix products, arithmetic and copies ran while one was open for 20% of the time, Pallas kernels for 7%

profile of v5, /device:TPU:1, one launch (start us, length us, event | category | flops | bytes accessed | tf_op | source)
XLA Modules:
  0.0 265.4 jit_solution(11576249289639105172)
XLA Ops:
  7.2 2.5 collective-permute-start.4
  9.8 4.0 %collective-permute-start = (bf16[256,2432]{1,0:T(8,128)(2,1)}, bf16[256,2432]{1,0:T(8,128)(2,1)S(1)}, u32[]{:S(2)}, u32[]{:S(2)}) collective-permute-start(bf16[256,2432]{1,0:T(8,128)(2,1)} %refs_0_.1), channel_id=1, source_target_pairs={{0,224},{16,240},{32,0},{48,16},{64,32},{80,48},{96,64},{112,80},{... | collective-permute-start | bytes 3735560 | tf_op jit(solution)/shard_map/ppermute | solution.py:169
  18.6 2.3 dynamic-slice_bitcast_fusion.1
  41.0 2.7 %collective-permute-start.3 = (bf16[256,2432]{1,0:T(8,128)(2,1)S(1)}, bf16[256,2432]{1,0:T(8,128)(2,1)}, u32[]{:S(2)}, u32[]{:S(2)}) collective-permute-start(bf16[256,2432]{1,0:T(8,128)(2,1)S(1)} %collective-permute-done.refs_2_), channel_id=1, source_target_pairs={{0,224},{16,240},{32,0},{48,16},{64,32},{80,48},{96,64},{112,80},{... | collective-permute-start | bytes 3735560 | tf_op jit(solution)/shard_map/ppermute | solution.py:183
  48.1 21.9 %collective-permute-done.6.refs_3_ = bf16[256,2432]{1,0:T(8,128)(2,1)} collective-permute-done((bf16[256,2432]{1,0:T(8,128)(2,1)S(1)}, bf16[256,2432]{1,0:T(8,128)(2,1)}, u32[]{:S(2)}, u32[]{:S(2)}) %collective-permute-start.6) | collective-permute-done | bytes 1245216 | tf_op jit(solution)/shard_map/ppermute | solution.py:182
  70.0 2.7 %collective-permute-start.5 = (bf16[256,2432]{1,0:T(8,128)(2,1)}, bf16[256,2432]{1,0:T(8,128)(2,1)S(1)}, u32[]{:S(2)}, u32[]{:S(2)}) collective-permute-start(bf16[256,2432]{1,0:T(8,128)(2,1)} %collective-permute-done.3.refs_4_), channel_id=1, source_target_pairs={{0,224},{16,240},{32,0},{48,16},{64,32},{80,48},{96,64},{112,80},{... | collective-permute-start | bytes 3735560 | tf_op jit(solution)/shard_map/ppermute | solution.py:183
  74.7 3.3 %fusion = f32[256,2432]{1,0:T(8,128)} fusion(f32[256,2432]{1,0:T(8,128)S(1)} %fusion.13, f32[256,2432]{1,0:T(8,128)S(1)} %copy-done.7, bf16[256,2432]{1,0:T(8,128)(2,1)} %collective-permute-done.6.refs_3_, bf16[8,256,256]{1,2,0:T(8,128)(2,1)S(1)} %pad_maximum_fusion.1, s32[]{:T(128)S(6)} %select_n.128), kind=kOutput, calls=%fused_computation.4 | convolution fusion | flops 320012288 | bytes 8847364 | tf_op jit(solution)/shard_map/dot_general | solution.py:165
  78.0 20.1 %collective-permute-done.7.refs_5_ = bf16[256,2432]{1,0:T(8,128)(2,1)S(1)} collective-permute-done((bf16[256,2432]{1,0:T(8,128)(2,1)}, bf16[256,2432]{1,0:T(8,128)(2,1)S(1)}, u32[]{:S(2)}, u32[]{:S(2)}) %collective-permute-start.7) | collective-permute-done | bytes 1245216 | tf_op jit(solution)/shard_map/ppermute | solution.py:182
  98.3 2.9 %collective-permute-start.9 = (bf16[128,2432]{1,0:T(8,128)(2,1)S(1)}, bf16[128,2432]{1,0:T(8,128)(2,1)}, u32[]{:S(2)}, u32[]{:S(2)}) collective-permute-start(bf16[128,2432]{1,0:T(8,128)(2,1)S(1)} %slice.47), channel_id=1, source_target_pairs={{0,224},{16,240},{32,0},{48,16},{64,32},{80,48},{96,64},{112,80},{... | collective-permute-start | bytes 1867784 | tf_op jit(solution)/shard_map/ppermute | solution.py:189
  101.2 10.7 %collective-permute-done.8.refs_7_ = bf16[128,2432]{1,0:T(8,128)(2,1)S(1)} collective-permute-done((bf16[128,2432]{1,0:T(8,128)(2,1)S(1)}, bf16[128,2432]{1,0:T(8,128)(2,1)S(1)}, u32[]{:S(2)}, u32[]{:S(2)}) %collective-permute-start.8) | collective-permute-done | bytes 622624 | tf_op jit(solution)/shard_map/ppermute | solution.py:188
  116.6 3.0 %fusion.5 = f32[128,2432]{1,0:T(8,128)} fusion(f32[128,2432]{1,0:T(8,128)S(1)} %fusion.35, f32[256,2432]{1,0:T(8,128)S(1)} %fusion.1, bf16[128,2432]{1,0:T(8,128)(2,1)} %collective-permute-done.9.refs_8_, bf16[256,256]{1,0:T(8,128)(2,1)S(1)} %bitcast.95), kind=kOutput, calls=%fused_computation.12 | convolution fusion | flops 80314368 | bytes 4390912 | tf_op jit(solution)/shard_map/dot_general | solution.py:165
  119.6 4.0 %collective-permute-start.10 = (f32[128,2432]{1,0:T(8,128)}, f32[128,2432]{1,0:T(8,128)}, u32[]{:S(2)}, u32[]{:S(2)}) collective-permute-start(f32[128,2432]{1,0:T(8,128)} %fusion.5), channel_id=1, source_target_pairs={{0,16},{16,0},{32,48},{48,32},{64,80},{80,64},{96,112},{112,96},{1... | collective-permute-start | bytes 3735560 | tf_op jit(solution)/shard_map/ppermute | solution.py:198
  129.8 13.0 %all_to_all.20 = f32[16,4,128]{2,1,0:T(4,128)S(1)} all-to-all(f32[16,4,128]{2,1,0:T(4,128)S(1)} %broadcast_in_dim.140), channel_id=1, replica_groups=mesh['dp'=16,'mp'=16] {'mp'}, dimensions={0} | all-to-all | bytes 65536 | tf_op jit(solution)/shard_map/all_to_all | solution.py:223
  148.7 6.5 %shard_map.130 = f32[16,256,128]{2,1,0:T(8,128)} custom-call(s32[2]{0:T(128)S(1)} %pad_add_fusion.place_ref, bf16[256,2432]{1,0:T(8,128)(2,1)S(1)} %pad_maximum_fusion.grad_ref, bf16[256,2432]{1,0:T(8,128)(2,1)S(1)} %copy-done.4, bf16[256,2432]{1,0:T(8,128)(2,1)S(1)} %copy-done.1, bf16[256,2432]{1,0:T(8,128)(2,1)S(1)} %copy-done.3, ...), custom_call_target="tpu_custom_call" | custom-call | tf_op jit(solution)/shard_map/pallas_call | solution.py:245
  155.2 3.9 %all-to-all-start.1 = ((f32[16,256,128]{2,1,0:T(8,128)}), f32[16,256,128]{2,1,0:T(8,128)S(1)}, u32[]{:S(2)}, u32[]{:S(2)}) async-start(f32[16,256,128]{2,1,0:T(8,128)} %shard_map.130), calls=%async_computation.1 | async-start | bytes 4194304 | tf_op jit(solution)/shard_map/all_to_all | solution.py:254
  160.5 31.6 %all-to-all-done.1 = f32[16,256,128]{2,1,0:T(8,128)S(1)} async-done(((f32[16,256,128]{2,1,0:T(8,128)}), f32[16,256,128]{2,1,0:T(8,128)S(1)}, u32[]{:S(2)}, u32[]{:S(2)}) %all-to-all-start.1) | async-done | bytes 2097184 | tf_op jit(solution)/shard_map/all_to_all | solution.py:254
  194.2 17.5 %all-to-all-start.2 = ((bf16[16,128,256]{2,1,0:T(8,128)(2,1)}), bf16[16,128,256]{2,1,0:T(8,128)(2,1)S(1)}, u32[]{:S(2)}, u32[]{:S(2)}) async-start(bf16[16,128,256]{2,1,0:T(8,128)(2,1)} %broadcast_in_dim.141), calls=%async_computation.2 | async-start | bytes 2097152 | tf_op jit(solution)/shard_map/all_to_all | solution.py:266
  211.7 4.8 %collective-permute-start.14 = (f32[128,256]{0,1:T(8,128)S(1)}, f32[128,256]{0,1:T(8,128)S(1)}, u32[]{:S(2)}, u32[]{:S(2)}) collective-permute-start(f32[128,256]{0,1:T(8,128)S(1)} %get-tuple-element.46), channel_id=1, source_target_pairs={{0,0},{1,16},{2,2},{3,18},{4,4},{5,20},{6,6},{7,22},{8,8},{9,24},{... | collective-permute-start | bytes 393224 | tf_op jit(solution)/shard_map/ppermute | solution.py:263
  216.5 6.4 %shard_map.131.proj_ref = f32[16,4,32,256]{3,2,1,0:T(8,128)} custom-call(bf16[16,4,32,1664]{3,2,1,0:T(8,128)(2,1)} %bitcast.89, bf16[4,1536,256]{2,1,0:T(8,128)(2,1)} %down_ref.1), custom_call_target="tpu_custom_call" | custom-call | tf_op jit(solution)/shard_map/pallas_call | solution.py:202
  222.9 4.0 %collective-permute-done.14 = f32[128,256]{0,1:T(8,128)S(1)} collective-permute-done((f32[128,256]{0,1:T(8,128)S(1)}, f32[128,256]{0,1:T(8,128)S(1)}, u32[]{:S(2)}, u32[]{:S(2)}) %collective-permute-start.14) | collective-permute-done | bytes 131104 | tf_op jit(solution)/shard_map/ppermute | solution.py:263
  228.4 5.5 %shard_map.132 = (bf16[4,16,32,256]{3,2,1,0:T(8,128)(2,1)}, f32[16,128]{1,0:T(8,128)}) custom-call(bf16[16,4,32,1664]{3,2,1,0:T(8,128)(2,1)} %bitcast.90, bf16[16,128,256]{2,1,0:T(8,128)(2,1)} %copy-done.11, f32[16,4,32,256]{3,2,1,0:T(8,128)} %shard_map.131.proj_ref), custom_call_target="tpu_custom_call" | custom-call | tf_op jit(solution)/shard_map/pallas_call | solution.py:270
  235.3 8.9 %all-to-all-start.3 = ((f32[256,1,128]{2,1,0:T(1,128)}), f32[256,1,128]{2,1,0:T(1,128)S(1)}, u32[]{:S(2)}, u32[]{:S(2)}) async-start(f32[256,1,128]{2,1,0:T(1,128)} %bitcast.33), calls=%async_computation.3 | async-start | bytes 262144 | tf_op jit(solution)/shard_map/all_to_all | solution.py:302
  244.9 6.2 %shard_map.133 = bf16[4,1536,256]{2,1,0:T(8,128)(2,1)} custom-call(bf16[16,4,32,1664]{3,2,1,0:T(8,128)(2,1)} %bitcast.91, bf16[4,16,32,256]{3,2,1,0:T(8,128)(2,1)} %get-tuple-element.29.weighted_ref), custom_call_target="tpu_custom_call" | custom-call | tf_op jit(solution)/shard_map/pallas_call | solution.py:290
  251.2 6.2 %all-to-all-done.3 = f32[256,1,128]{2,1,0:T(1,128)S(1)} async-done(((f32[256,1,128]{2,1,0:T(1,128)}), f32[256,1,128]{2,1,0:T(1,128)S(1)}, u32[]{:S(2)}, u32[]{:S(2)}) %all-to-all-start.3) | async-done | bytes 131104 | tf_op jit(solution)/shard_map/all_to_all | solution.py:302
  (130 shorter events, 56.3 us)
Async XLA Ops:
  7.2 209.3 %all-gather.3.cloned.1.call-start = ((), (), s32[]{:S(2)}) async-start(), calls=%async_computation.4 | async-start | bytes 7241728 | tf_op jit(solution)/shard_map/all_gather | solution.py:201
  7.2 33.8 %collective-permute-start.4 = (bf16[256,2432]{1,0:T(8,128)(2,1)}, bf16[256,2432]{1,0:T(8,128)(2,1)S(1)}, u32[]{:S(2)}, u32[]{:S(2)}) collective-permute-start(bf16[256,2432]{1,0:T(8,128)(2,1)} %refs_0_.1), channel_id=1, source_target_pairs={{0,32},{16,48},{32,64},{48,80},{64,96},{80,112},{96,128},{112,144}... | collective-permute-start | bytes 3735560 | tf_op jit(solution)/shard_map/ppermute | solution.py:168
  9.8 30.4 %collective-permute-start = (bf16[256,2432]{1,0:T(8,128)(2,1)}, bf16[256,2432]{1,0:T(8,128)(2,1)S(1)}, u32[]{:S(2)}, u32[]{:S(2)}) collective-permute-start(bf16[256,2432]{1,0:T(8,128)(2,1)} %refs_0_.1), channel_id=1, source_target_pairs={{0,224},{16,240},{32,0},{48,16},{64,32},{80,48},{96,64},{112,80},{... | collective-permute-start | bytes 3735560 | tf_op jit(solution)/shard_map/ppermute | solution.py:169
  20.9 17.8 %collective-permute-start.1 = (bf16[8,128,256]{1,2,0:T(8,128)(2,1)}, bf16[8,128,256]{1,2,0:T(8,128)(2,1)}, u32[]{:S(2)}, u32[]{:S(2)}) collective-permute-start(bf16[8,128,256]{1,2,0:T(8,128)(2,1)} %get-tuple-element.52), channel_id=1, source_target_pairs={{0,16},{16,0},{32,48},{48,32},{64,80},{80,64},{96,112},{112,96},{1... | collective-permute-start | bytes 1572872 | tf_op jit(solution)/shard_map/ppermute | solution.py:127
  22.5 14.7 %collective-permute-start.2 = (bf16[128,256]{0,1:T(8,128)(2,1)}, bf16[128,256]{0,1:T(8,128)(2,1)}, u32[]{:S(2)}, u32[]{:S(2)}) collective-permute-start(bf16[128,256]{0,1:T(8,128)(2,1)} %constant_dynamic-slice_fusion.3), channel_id=1, source_target_pairs={{0,16},{16,0},{32,48},{48,32},{64,80},{80,64},{96,112},{112,96},{1... | collective-permute-start | bytes 196616 | tf_op jit(solution)/shard_map/ppermute | solution.py:131
  40.1 34.5 %copy-start.10 = (bf16[8,256,256]{1,2,0:T(8,128)(2,1)}, bf16[8,256,256]{1,2,0:T(8,128)(2,1)S(1)}, u32[]{:S(2)}) copy-start(bf16[8,256,256]{1,2,0:T(8,128)(2,1)S(1)} %pad_maximum_fusion.1) | copy-start | bytes 3145732
  41.0 29.0 %collective-permute-start.6 = (bf16[256,2432]{1,0:T(8,128)(2,1)S(1)}, bf16[256,2432]{1,0:T(8,128)(2,1)}, u32[]{:S(2)}, u32[]{:S(2)}) collective-permute-start(bf16[256,2432]{1,0:T(8,128)(2,1)S(1)} %collective-permute-done.4.refs_1_), channel_id=1, source_target_pairs={{0,32},{16,48},{32,64},{48,80},{64,96},{80,112},{96,128},{112,144}... | collective-permute-start | bytes 3735560 | tf_op jit(solution)/shard_map/ppermute | solution.py:182
  41.0 29.0 %collective-permute-start.3 = (bf16[256,2432]{1,0:T(8,128)(2,1)S(1)}, bf16[256,2432]{1,0:T(8,128)(2,1)}, u32[]{:S(2)}, u32[]{:S(2)}) collective-permute-start(bf16[256,2432]{1,0:T(8,128)(2,1)S(1)} %collective-permute-done.refs_2_), channel_id=1, source_target_pairs={{0,224},{16,240},{32,0},{48,16},{64,32},{80,48},{96,64},{112,80},{... | collective-permute-start | bytes 3735560 | tf_op jit(solution)/shard_map/ppermute | solution.py:183
  70.0 28.1 %collective-permute-start.7 = (bf16[256,2432]{1,0:T(8,128)(2,1)}, bf16[256,2432]{1,0:T(8,128)(2,1)S(1)}, u32[]{:S(2)}, u32[]{:S(2)}) collective-permute-start(bf16[256,2432]{1,0:T(8,128)(2,1)} %collective-permute-done.6.refs_3_), channel_id=1, source_target_pairs={{0,32},{16,48},{32,64},{48,80},{64,96},{80,112},{96,128},{112,144}... | collective-permute-start | bytes 3735560 | tf_op jit(solution)/shard_map/ppermute | solution.py:182
  70.0 28.3 %collective-permute-start.5 = (bf16[256,2432]{1,0:T(8,128)(2,1)}, bf16[256,2432]{1,0:T(8,128)(2,1)S(1)}, u32[]{:S(2)}, u32[]{:S(2)}) collective-permute-start(bf16[256,2432]{1,0:T(8,128)(2,1)} %collective-permute-done.3.refs_4_), channel_id=1, source_target_pairs={{0,224},{16,240},{32,0},{48,16},{64,32},{80,48},{96,64},{112,80},{... | collective-permute-start | bytes 3735560 | tf_op jit(solution)/shard_map/ppermute | solution.py:183
  98.1 13.7 %collective-permute-start.8 = (bf16[128,2432]{1,0:T(8,128)(2,1)S(1)}, bf16[128,2432]{1,0:T(8,128)(2,1)S(1)}, u32[]{:S(2)}, u32[]{:S(2)}) collective-permute-start(bf16[128,2432]{1,0:T(8,128)(2,1)S(1)} %slice.59), channel_id=1, source_target_pairs={{0,32},{16,48},{32,64},{48,80},{64,96},{80,112},{96,128},{112,144}... | collective-permute-start | bytes 1867784 | tf_op jit(solution)/shard_map/ppermute | solution.py:188
  98.3 13.6 %collective-permute-start.9 = (bf16[128,2432]{1,0:T(8,128)(2,1)S(1)}, bf16[128,2432]{1,0:T(8,128)(2,1)}, u32[]{:S(2)}, u32[]{:S(2)}) collective-permute-start(bf16[128,2432]{1,0:T(8,128)(2,1)S(1)} %slice.47), channel_id=1, source_target_pairs={{0,224},{16,240},{32,0},{48,16},{64,32},{80,48},{96,64},{112,80},{... | collective-permute-start | bytes 1867784 | tf_op jit(solution)/shard_map/ppermute | solution.py:189
  119.6 6.9 %collective-permute-start.10 = (f32[128,2432]{1,0:T(8,128)}, f32[128,2432]{1,0:T(8,128)}, u32[]{:S(2)}, u32[]{:S(2)}) collective-permute-start(f32[128,2432]{1,0:T(8,128)} %fusion.5), channel_id=1, source_target_pairs={{0,16},{16,0},{32,48},{48,32},{64,80},{80,64},{96,112},{112,96},{1... | collective-permute-start | bytes 3735560 | tf_op jit(solution)/shard_map/ppermute | solution.py:198
  128.3 14.7 %copy-start.18 = (s32[128]{0:T(128)S(1)}, s32[128]{0:T(128)}, u32[]{:S(2)}) copy-start(s32[128]{0:T(128)} %param.17) | copy-start | bytes 1540
  128.3 14.7 %copy-start.19 = (f32[128]{0:T(128)S(1)}, f32[128]{0:T(128)}, u32[]{:S(2)}) copy-start(f32[128]{0:T(128)} %param.16) | copy-start | bytes 1540
  128.3 14.7 %copy-start.20 = (f32[128]{0:T(128)S(1)}, f32[128]{0:T(128)}, u32[]{:S(2)}) copy-start(f32[128]{0:T(128)} %param.15) | copy-start | bytes 1540
  145.0 3.6 %collective-permute-start.12 = (bf16[128,2432]{1,0:T(8,128)(2,1)S(1)}, bf16[128,2432]{1,0:T(8,128)(2,1)S(1)}, u32[]{:S(2)}, u32[]{:S(2)}) collective-permute-start(bf16[128,2432]{1,0:T(8,128)(2,1)S(1)} %multiply_convert_fusion), channel_id=1, source_target_pairs={{0,16},{16,0},{32,48},{48,32},{64,80},{80,64},{96,112},{112,96},{1... | collective-permute-start | bytes 1867784 | tf_op jit(solution)/shard_map/ppermute | solution.py:242
  155.2 36.8 %all-to-all-start.1 = ((f32[16,256,128]{2,1,0:T(8,128)}), f32[16,256,128]{2,1,0:T(8,128)S(1)}, u32[]{:S(2)}, u32[]{:S(2)}) async-start(f32[16,256,128]{2,1,0:T(8,128)} %shard_map.130), calls=%async_computation.1 | async-start | bytes 4194304 | tf_op jit(solution)/shard_map/all_to_all | solution.py:254
  159.1 33.1 %copy-start.13 = (bf16[128,256]{0,1:T(8,128)(2,1)S(1)}, bf16[128,256]{0,1:T(8,128)(2,1)}, u32[]{:S(2)}) copy-start(bf16[128,256]{0,1:T(8,128)(2,1)} %dynamic-slice_select_fusion) | copy-start | bytes 196612
  159.1 1.3 collective-permute-start.11
  192.3 0.7 collective-permute-start.13
  194.2 33.1 %all-to-all-start.2 = ((bf16[16,128,256]{2,1,0:T(8,128)(2,1)}), bf16[16,128,256]{2,1,0:T(8,128)(2,1)S(1)}, u32[]{:S(2)}, u32[]{:S(2)}) async-start(bf16[16,128,256]{2,1,0:T(8,128)(2,1)} %broadcast_in_dim.141), calls=%async_computation.2 | async-start | bytes 2097152 | tf_op jit(solution)/shard_map/all_to_all | solution.py:266
  211.7 15.2 %collective-permute-start.14 = (f32[128,256]{0,1:T(8,128)S(1)}, f32[128,256]{0,1:T(8,128)S(1)}, u32[]{:S(2)}, u32[]{:S(2)}) collective-permute-start(f32[128,256]{0,1:T(8,128)S(1)} %get-tuple-element.46), channel_id=1, source_target_pairs={{0,0},{1,16},{2,2},{3,18},{4,4},{5,20},{6,6},{7,22},{8,8},{9,24},{... | collective-permute-start | bytes 393224 | tf_op jit(solution)/shard_map/ppermute | solution.py:263
  235.3 22.1 %all-to-all-start.3 = ((f32[256,1,128]{2,1,0:T(1,128)}), f32[256,1,128]{2,1,0:T(1,128)S(1)}, u32[]{:S(2)}, u32[]{:S(2)}) async-start(f32[256,1,128]{2,1,0:T(1,128)} %bitcast.33), calls=%async_computation.3 | async-start | bytes 262144 | tf_op jit(solution)/shard_map/all_to_all | solution.py:302
  (17 other events, 73.8 us)
Sparse Core Ops, SparseCore 0:
  112.0 52.0 all-gather.2

commit v6 on v5

--- a/solution.py
+++ b/solution.py
@@ -252,6 +252,10 @@
     )(place, chip_grad, *[piece for _, _, piece in head_pieces])
 
     hidden = lax.all_to_all(hidden, "mp", 0, 0, tiled=True)
+    side_all = acts_all[..., hidden_width:]
+    hidden, proj, side_all, landed_rows = lax.optimization_barrier(
+        (hidden, proj, side_all, landed_rows)
+    )
     hidden_grad = jnp.sum(hidden, axis=0).T
 
     landed_gain = lax.dynamic_slice_in_dim(norm_gain, landed_block * block, block, 0)
@@ -260,33 +264,23 @@
     landed_resid = landed_rms * (
         scaled_grad - landed_stream.astype(f32) * landed_rms * landed_inner
     )
+    stream_grad = lax.ppermute(landed_resid.astype(bf16), both, sum_turn(nz))
     resid_grad = lax.ppermute(landed_resid, both, home_turn(nz))
-    stream_grad = lax.ppermute(landed_resid.astype(bf16), both, sum_turn(nz))
+    stream_grad, resid_grad = lax.optimization_barrier((stream_grad, resid_grad))
 
     all_rows = lax.all_to_all(
         jnp.broadcast_to(stream_grad[None], (mp_count, tokens, block)), "mp", 0, 0, tiled=True
     )
-    all_rows, resid_grad, proj = lax.optimization_barrier((all_rows, resid_grad, proj))
     weighted, gate = pl.pallas_call(
         slot_kernel,
-        grid=(1,),
-        in_specs=[
-            pl.BlockSpec(
-                (dp_count, per_expert, capacity, lanes), lambda n: (0, 0, 0, hidden_width // lanes)
-            ),
-            pl.BlockSpec((dp_count, tokens, block), lambda n: (0, 0, 0)),
-            pl.BlockSpec((dp_count, per_expert, capacity, block), lambda n: (0, 0, 0, 0)),
-        ],
-        out_specs=[
-            pl.BlockSpec((per_expert, dp_count, capacity, block), lambda n: (0, 0, 0, 0)),
-            pl.BlockSpec((dp_count, per_expert * capacity), lambda n: (0, 0)),
-        ],
+        in_specs=[pl.BlockSpec(memory_space=pltpu.VMEM)] * 3,
+        out_specs=[pl.BlockSpec(memory_space=pltpu.VMEM)] * 2,
         out_shape=[
             jax.ShapeDtypeStruct((per_expert, dp_count, capacity, block), bf16),
             jax.ShapeDtypeStruct((dp_count, per_expert * capacity), f32),
         ],
-        compiler_params=pltpu.CompilerParams(vmem_limit_bytes=56 * 1024 * 1024),
-    )(acts_all, all_rows, proj)
+        compiler_params=pltpu.CompilerParams(vmem_limit_bytes=32 * 1024 * 1024),
+    )(side_all, all_rows, proj)
     down_grad = pl.pallas_call(
         down_kernel,
         grid=(per_expert,),

time: 267 us -> 263 us (0.985)
  blocking collectives: 13 us -> 40.9 us
  starting transfers between devices: 58 us -> 36 us
  waiting for transfers between devices: 98.6 us -> 92.8 us
  Pallas kernels: 24.7 us -> 21.7 us
    all_to_all x0 -> x1, blocking collectives: none -> 27.9 us  [local(): lax.all_to_all(jnp.broadcast_to(stream_grad[None], (mp_count, tokens, blo...]
    all_to_all x1 -> x0, starting transfers between devices: 17.5 us -> none  [local(): lax.all_to_all(jnp.broadcast_to(stream_grad[None], (mp_count, tokens, blo...]
    all_to_all x1, waiting for transfers between devices: 31.6 us -> 20.4 us  [local(): hidden = lax.all_to_all(hidden, 'mp', 0, 0, tiled=True)]
    all_gather x1, waiting for transfers between devices: 0.02 us -> 3.66 us  [local(): acts_all = lax.all_gather(acts_block, 'dp', axis=0, tiled=False)]
    pallas_call x1, Pallas kernels: 5.52 us -> 2.48 us  [local(): pl.pallas_call(slot_kernel, in_specs=[pl.BlockSpec(memory_space=pltpu.VME...]
    ppermute x1, starting transfers between devices: 4.76 us -> 1.92 us  [local(): resid_grad = lax.ppermute(landed_resid, both, home_turn(nz))]
  transfers between devices with their start and end apart: 19 -> 18, of which waited for: 11 -> 11; matrix products, arithmetic and copies ran while one was open for 20% -> 20% of each run, Pallas kernels for 7% -> 7%
where the time goes in v6:
time: 263 us; the launch traced here: 262 us
  waiting for transfers between devices  92.8 us (35%)
  blocking collectives  40.9 us (16%)
  starting transfers between devices  36 us (14%)
  other arithmetic  23 us (9%)
  Pallas kernels  21.7 us (8%)
  matrix products  17.9 us (7%)
  local copies, waits for them, and re-layouts  15.2 us (6%)
  between operations  14.5 us (6%)
    ppermute x2, waiting for transfers between devices, local(): ahead = lax.ppermute(ahead, 'dp', z_shift(1, nz))  42 us
    all_to_all x1, blocking collectives, local(): lax.all_to_all(jnp.broadcast_to(stream_grad[None], (mp_count, tokens, blo...  27.9 us
    all_to_all x1, waiting for transfers between devices, local(): hidden = lax.all_to_all(hidden, 'mp', 0, 0, tiled=True)  20.4 us
    dot_general x11, matrix products, logits_of(): return jnp.dot(features, piece, preferred_element_type=f32)  17.9 us
    all_to_all x1, blocking collectives, local(): lax.all_to_all(jnp.broadcast_to(stats[None], (mp_count, 4, tokens)), 'mp'...  13 us
    ppermute x1, waiting for transfers between devices, local(): lax.ppermute(ahead[:half], 'dp', z_shift(1, nz))  10.7 us
    all_to_all x1, starting transfers between devices, local(): lax.all_to_all(jnp.broadcast_to(gate[:, None, :], (dp_count, mp_count, pe...  7.3 us
    pallas_call x1, Pallas kernels, local(): pl.pallas_call(functools.partial(hidden_kernel, nz), in_specs=[pl.BlockSp...  6.51 us
  transfers between devices with their start and end apart: 18, of which 11 were waited for; matrix products, arithmetic and copies ran while one was open for 20% of the time, Pallas kernels for 7%

profile of v6, /device:TPU:1, one launch (start us, length us, event | category | flops | bytes accessed | tf_op | source)
XLA Modules:
  0.0 262.0 jit_solution(9722343239943703588)
XLA Ops:
  7.2 2.5 collective-permute-start.4
  9.8 4.0 %collective-permute-start = (bf16[256,2432]{1,0:T(8,128)(2,1)}, bf16[256,2432]{1,0:T(8,128)(2,1)S(1)}, u32[]{:S(2)}, u32[]{:S(2)}) collective-permute-start(bf16[256,2432]{1,0:T(8,128)(2,1)} %refs_0_.1), channel_id=1, source_target_pairs={{0,224},{16,240},{32,0},{48,16},{64,32},{80,48},{96,64},{112,80},{... | collective-permute-start | bytes 3735560 | tf_op jit(solution)/shard_map/ppermute | solution.py:169
  18.6 2.3 dynamic-slice_bitcast_fusion.1
  41.0 2.7 %collective-permute-start.3 = (bf16[256,2432]{1,0:T(8,128)(2,1)S(1)}, bf16[256,2432]{1,0:T(8,128)(2,1)}, u32[]{:S(2)}, u32[]{:S(2)}) collective-permute-start(bf16[256,2432]{1,0:T(8,128)(2,1)S(1)} %collective-permute-done.refs_2_), channel_id=1, source_target_pairs={{0,224},{16,240},{32,0},{48,16},{64,32},{80,48},{96,64},{112,80},{... | collective-permute-start | bytes 3735560 | tf_op jit(solution)/shard_map/ppermute | solution.py:183
  48.1 21.9 %collective-permute-done.6.refs_3_ = bf16[256,2432]{1,0:T(8,128)(2,1)} collective-permute-done((bf16[256,2432]{1,0:T(8,128)(2,1)S(1)}, bf16[256,2432]{1,0:T(8,128)(2,1)}, u32[]{:S(2)}, u32[]{:S(2)}) %collective-permute-start.6) | collective-permute-done | bytes 1245216 | tf_op jit(solution)/shard_map/ppermute | solution.py:182
  70.0 2.7 %collective-permute-start.5 = (bf16[256,2432]{1,0:T(8,128)(2,1)}, bf16[256,2432]{1,0:T(8,128)(2,1)S(1)}, u32[]{:S(2)}, u32[]{:S(2)}) collective-permute-start(bf16[256,2432]{1,0:T(8,128)(2,1)} %collective-permute-done.3.refs_4_), channel_id=1, source_target_pairs={{0,224},{16,240},{32,0},{48,16},{64,32},{80,48},{96,64},{112,80},{... | collective-permute-start | bytes 3735560 | tf_op jit(solution)/shard_map/ppermute | solution.py:183
  74.7 3.3 %fusion = f32[256,2432]{1,0:T(8,128)} fusion(f32[256,2432]{1,0:T(8,128)S(1)} %fusion.13, f32[256,2432]{1,0:T(8,128)S(1)} %copy-done.9, bf16[256,2432]{1,0:T(8,128)(2,1)} %collective-permute-done.6.refs_3_, bf16[8,256,256]{1,2,0:T(8,128)(2,1)S(1)} %pad_maximum_fusion.1, s32[]{:T(128)S(6)} %select_n.127), kind=kOutput, calls=%fused_computation.4 | convolution fusion | flops 320012288 | bytes 8847364 | tf_op jit(solution)/shard_map/dot_general | solution.py:165
  78.0 20.1 %collective-permute-done.7.refs_5_ = bf16[256,2432]{1,0:T(8,128)(2,1)S(1)} collective-permute-done((bf16[256,2432]{1,0:T(8,128)(2,1)}, bf16[256,2432]{1,0:T(8,128)(2,1)S(1)}, u32[]{:S(2)}, u32[]{:S(2)}) %collective-permute-start.7) | collective-permute-done | bytes 1245216 | tf_op jit(solution)/shard_map/ppermute | solution.py:182
  98.3 2.9 %collective-permute-start.9 = (bf16[128,2432]{1,0:T(8,128)(2,1)S(1)}, bf16[128,2432]{1,0:T(8,128)(2,1)}, u32[]{:S(2)}, u32[]{:S(2)}) collective-permute-start(bf16[128,2432]{1,0:T(8,128)(2,1)S(1)} %slice.50), channel_id=1, source_target_pairs={{0,224},{16,240},{32,0},{48,16},{64,32},{80,48},{96,64},{112,80},{... | collective-permute-start | bytes 1867784 | tf_op jit(solution)/shard_map/ppermute | solution.py:189
  101.2 10.7 %collective-permute-done.8.refs_7_ = bf16[128,2432]{1,0:T(8,128)(2,1)S(1)} collective-permute-done((bf16[128,2432]{1,0:T(8,128)(2,1)S(1)}, bf16[128,2432]{1,0:T(8,128)(2,1)S(1)}, u32[]{:S(2)}, u32[]{:S(2)}) %collective-permute-start.8) | collective-permute-done | bytes 622624 | tf_op jit(solution)/shard_map/ppermute | solution.py:188
  116.6 3.0 %fusion.5 = f32[128,2432]{1,0:T(8,128)} fusion(f32[128,2432]{1,0:T(8,128)S(1)} %fusion.35, f32[256,2432]{1,0:T(8,128)S(1)} %fusion.1, bf16[128,2432]{1,0:T(8,128)(2,1)} %collective-permute-done.9.refs_8_, bf16[256,256]{1,0:T(8,128)(2,1)S(1)} %bitcast.95), kind=kOutput, calls=%fused_computation.12 | convolution fusion | flops 80314368 | bytes 4390912 | tf_op jit(solution)/shard_map/dot_general | solution.py:165
  119.6 4.0 %collective-permute-start.10 = (f32[128,2432]{1,0:T(8,128)}, f32[128,2432]{1,0:T(8,128)}, u32[]{:S(2)}, u32[]{:S(2)}) collective-permute-start(f32[128,2432]{1,0:T(8,128)} %fusion.5), channel_id=1, source_target_pairs={{0,16},{16,0},{32,48},{48,32},{64,80},{80,64},{96,112},{112,96},{1... | collective-permute-start | bytes 3735560 | tf_op jit(solution)/shard_map/ppermute | solution.py:198
  129.8 13.0 %all_to_all.20 = f32[16,4,128]{2,1,0:T(4,128)S(1)} all-to-all(f32[16,4,128]{2,1,0:T(4,128)S(1)} %broadcast_in_dim.140), channel_id=1, replica_groups=mesh['dp'=16,'mp'=16] {'mp'}, dimensions={0} | all-to-all | bytes 65536 | tf_op jit(solution)/shard_map/all_to_all | solution.py:223
  148.7 6.5 %shard_map.130 = f32[16,256,128]{2,1,0:T(8,128)} custom-call(s32[2]{0:T(128)S(1)} %pad_add_fusion.place_ref, bf16[256,2432]{1,0:T(8,128)(2,1)S(1)} %pad_maximum_fusion.grad_ref, bf16[256,2432]{1,0:T(8,128)(2,1)S(1)} %copy-done.5, bf16[256,2432]{1,0:T(8,128)(2,1)S(1)} %copy-done.2, bf16[256,2432]{1,0:T(8,128)(2,1)S(1)} %copy-done.4, ...), custom_call_target="tpu_custom_call" | custom-call | tf_op jit(solution)/shard_map/pallas_call | solution.py:245
  155.2 3.9 %all-to-all-start.1 = ((f32[16,256,128]{2,1,0:T(8,128)}), f32[16,256,128]{2,1,0:T(8,128)S(1)}, u32[]{:S(2)}, u32[]{:S(2)}) async-start(f32[16,256,128]{2,1,0:T(8,128)} %shard_map.130), calls=%async_computation.1 | async-start | bytes 4194304 | tf_op jit(solution)/shard_map/all_to_all | solution.py:254
  160.5 3.7 %all-gather.3.cloned.1.call-done = bf16[64,32,1664]{2,1,0:T(8,128)(2,1)} async-done(((bf16[4,32,1664]{2,1,0:T(8,128)(2,1)}), bf16[64,32,1664]{2,1,0:T(8,128)(2,1)}) %all-gather.3.cloned.1.call-update) | async-done | bytes 6815760 | tf_op jit(solution)/shard_map/all_gather | solution.py:201
  165.2 6.5 %shard_map.131.proj_ref = f32[16,4,32,256]{3,2,1,0:T(8,128)} custom-call(bf16[16,4,32,1664]{3,2,1,0:T(8,128)(2,1)} %bitcast.90, bf16[4,1536,256]{2,1,0:T(8,128)(2,1)} %down_ref.1), custom_call_target="tpu_custom_call" | custom-call | tf_op jit(solution)/shard_map/pallas_call | solution.py:202
  171.7 20.4 %all-to-all-done.1 = f32[16,256,128]{2,1,0:T(8,128)S(1)} async-done(((f32[16,256,128]{2,1,0:T(8,128)}), f32[16,256,128]{2,1,0:T(8,128)S(1)}, u32[]{:S(2)}, u32[]{:S(2)}) %all-to-all-start.1) | async-done | bytes 2097184 | tf_op jit(solution)/shard_map/all_to_all | solution.py:254
  194.9 6.4 %collective-permute-done.14 = f32[128,256]{0,1:T(8,128)S(1)} collective-permute-done((f32[128,256]{0,1:T(8,128)S(1)}, f32[128,256]{0,1:T(8,128)S(1)}, u32[]{:S(2)}, u32[]{:S(2)}) %collective-permute-start.14) | collective-permute-done | bytes 131104 | tf_op jit(solution)/shard_map/ppermute | solution.py:268
  201.5 27.9 %all_to_all.21.rows_ref = bf16[16,128,256]{2,1,0:T(8,128)(2,1)S(1)} all-to-all(bf16[16,128,256]{2,1,0:T(8,128)(2,1)S(1)} %broadcast_in_dim.141), channel_id=1, replica_groups=mesh['dp'=16,'mp'=16] {'mp'}, dimensions={0} | all-to-all | bytes 2097152 | tf_op jit(solution)/shard_map/all_to_all | solution.py:271
  229.5 2.5 shard_map.132
  233.6 7.3 %all-to-all-start.3 = ((f32[256,1,128]{2,1,0:T(1,128)}), f32[256,1,128]{2,1,0:T(1,128)S(1)}, u32[]{:S(2)}, u32[]{:S(2)}) async-start(f32[256,1,128]{2,1,0:T(1,128)} %bitcast.33), calls=%async_computation.3 | async-start | bytes 262144 | tf_op jit(solution)/shard_map/all_to_all | solution.py:296
  241.7 6.2 %shard_map.133 = bf16[4,1536,256]{2,1,0:T(8,128)(2,1)} custom-call(bf16[16,4,32,1664]{3,2,1,0:T(8,128)(2,1)} %bitcast.91, bf16[4,16,32,256]{3,2,1,0:T(8,128)(2,1)} %copy-done.6), custom_call_target="tpu_custom_call" | custom-call | tf_op jit(solution)/shard_map/pallas_call | solution.py:284
  247.9 6.1 %all-to-all-done.3 = f32[256,1,128]{2,1,0:T(1,128)S(1)} async-done(((f32[256,1,128]{2,1,0:T(1,128)}), f32[256,1,128]{2,1,0:T(1,128)S(1)}, u32[]{:S(2)}, u32[]{:S(2)}) %all-to-all-start.3) | async-done | bytes 131104 | tf_op jit(solution)/shard_map/all_to_all | solution.py:296
  (132 shorter events, 57.1 us)
Async XLA Ops:
  7.2 156.9 %all-gather.3.cloned.1.call-start = ((), (), s32[]{:S(2)}) async-start(), calls=%async_computation.4 | async-start | bytes 7241728 | tf_op jit(solution)/shard_map/all_gather | solution.py:201
  7.2 33.8 %collective-permute-start.4 = (bf16[256,2432]{1,0:T(8,128)(2,1)}, bf16[256,2432]{1,0:T(8,128)(2,1)S(1)}, u32[]{:S(2)}, u32[]{:S(2)}) collective-permute-start(bf16[256,2432]{1,0:T(8,128)(2,1)} %refs_0_.1), channel_id=1, source_target_pairs={{0,32},{16,48},{32,64},{48,80},{64,96},{80,112},{96,128},{112,144}... | collective-permute-start | bytes 3735560 | tf_op jit(solution)/shard_map/ppermute | solution.py:168
  9.8 30.4 %collective-permute-start = (bf16[256,2432]{1,0:T(8,128)(2,1)}, bf16[256,2432]{1,0:T(8,128)(2,1)S(1)}, u32[]{:S(2)}, u32[]{:S(2)}) collective-permute-start(bf16[256,2432]{1,0:T(8,128)(2,1)} %refs_0_.1), channel_id=1, source_target_pairs={{0,224},{16,240},{32,0},{48,16},{64,32},{80,48},{96,64},{112,80},{... | collective-permute-start | bytes 3735560 | tf_op jit(solution)/shard_map/ppermute | solution.py:169
  20.9 17.8 %collective-permute-start.1 = (bf16[8,128,256]{1,2,0:T(8,128)(2,1)}, bf16[8,128,256]{1,2,0:T(8,128)(2,1)}, u32[]{:S(2)}, u32[]{:S(2)}) collective-permute-start(bf16[8,128,256]{1,2,0:T(8,128)(2,1)} %get-tuple-element.58), channel_id=1, source_target_pairs={{0,16},{16,0},{32,48},{48,32},{64,80},{80,64},{96,112},{112,96},{1... | collective-permute-start | bytes 1572872 | tf_op jit(solution)/shard_map/ppermute | solution.py:127
  22.5 14.8 %collective-permute-start.2 = (bf16[128,256]{0,1:T(8,128)(2,1)}, bf16[128,256]{0,1:T(8,128)(2,1)}, u32[]{:S(2)}, u32[]{:S(2)}) collective-permute-start(bf16[128,256]{0,1:T(8,128)(2,1)} %constant_dynamic-slice_fusion.3), channel_id=1, source_target_pairs={{0,16},{16,0},{32,48},{48,32},{64,80},{80,64},{96,112},{112,96},{1... | collective-permute-start | bytes 196616 | tf_op jit(solution)/shard_map/ppermute | solution.py:131
  40.1 34.5 %copy-start.12 = (bf16[8,256,256]{1,2,0:T(8,128)(2,1)}, bf16[8,256,256]{1,2,0:T(8,128)(2,1)S(1)}, u32[]{:S(2)}) copy-start(bf16[8,256,256]{1,2,0:T(8,128)(2,1)S(1)} %pad_maximum_fusion.1) | copy-start | bytes 3145732
  41.0 29.0 %collective-permute-start.6 = (bf16[256,2432]{1,0:T(8,128)(2,1)S(1)}, bf16[256,2432]{1,0:T(8,128)(2,1)}, u32[]{:S(2)}, u32[]{:S(2)}) collective-permute-start(bf16[256,2432]{1,0:T(8,128)(2,1)S(1)} %collective-permute-done.4.refs_1_), channel_id=1, source_target_pairs={{0,32},{16,48},{32,64},{48,80},{64,96},{80,112},{96,128},{112,144}... | collective-permute-start | bytes 3735560 | tf_op jit(solution)/shard_map/ppermute | solution.py:182
  41.0 29.0 %collective-permute-start.3 = (bf16[256,2432]{1,0:T(8,128)(2,1)S(1)}, bf16[256,2432]{1,0:T(8,128)(2,1)}, u32[]{:S(2)}, u32[]{:S(2)}) collective-permute-start(bf16[256,2432]{1,0:T(8,128)(2,1)S(1)} %collective-permute-done.refs_2_), channel_id=1, source_target_pairs={{0,224},{16,240},{32,0},{48,16},{64,32},{80,48},{96,64},{112,80},{... | collective-permute-start | bytes 3735560 | tf_op jit(solution)/shard_map/ppermute | solution.py:183
  70.0 28.1 %collective-permute-start.7 = (bf16[256,2432]{1,0:T(8,128)(2,1)}, bf16[256,2432]{1,0:T(8,128)(2,1)S(1)}, u32[]{:S(2)}, u32[]{:S(2)}) collective-permute-start(bf16[256,2432]{1,0:T(8,128)(2,1)} %collective-permute-done.6.refs_3_), channel_id=1, source_target_pairs={{0,32},{16,48},{32,64},{48,80},{64,96},{80,112},{96,128},{112,144}... | collective-permute-start | bytes 3735560 | tf_op jit(solution)/shard_map/ppermute | solution.py:182
  70.0 28.3 %collective-permute-start.5 = (bf16[256,2432]{1,0:T(8,128)(2,1)}, bf16[256,2432]{1,0:T(8,128)(2,1)S(1)}, u32[]{:S(2)}, u32[]{:S(2)}) collective-permute-start(bf16[256,2432]{1,0:T(8,128)(2,1)} %collective-permute-done.3.refs_4_), channel_id=1, source_target_pairs={{0,224},{16,240},{32,0},{48,16},{64,32},{80,48},{96,64},{112,80},{... | collective-permute-start | bytes 3735560 | tf_op jit(solution)/shard_map/ppermute | solution.py:183
  98.1 13.7 %collective-permute-start.8 = (bf16[128,2432]{1,0:T(8,128)(2,1)S(1)}, bf16[128,2432]{1,0:T(8,128)(2,1)S(1)}, u32[]{:S(2)}, u32[]{:S(2)}) collective-permute-start(bf16[128,2432]{1,0:T(8,128)(2,1)S(1)} %slice.63), channel_id=1, source_target_pairs={{0,32},{16,48},{32,64},{48,80},{64,96},{80,112},{96,128},{112,144}... | collective-permute-start | bytes 1867784 | tf_op jit(solution)/shard_map/ppermute | solution.py:188
  98.3 13.6 %collective-permute-start.9 = (bf16[128,2432]{1,0:T(8,128)(2,1)S(1)}, bf16[128,2432]{1,0:T(8,128)(2,1)}, u32[]{:S(2)}, u32[]{:S(2)}) collective-permute-start(bf16[128,2432]{1,0:T(8,128)(2,1)S(1)} %slice.50), channel_id=1, source_target_pairs={{0,224},{16,240},{32,0},{48,16},{64,32},{80,48},{96,64},{112,80},{... | collective-permute-start | bytes 1867784 | tf_op jit(solution)/shard_map/ppermute | solution.py:189
  119.6 6.9 %collective-permute-start.10 = (f32[128,2432]{1,0:T(8,128)}, f32[128,2432]{1,0:T(8,128)}, u32[]{:S(2)}, u32[]{:S(2)}) collective-permute-start(f32[128,2432]{1,0:T(8,128)} %fusion.5), channel_id=1, source_target_pairs={{0,16},{16,0},{32,48},{48,32},{64,80},{80,64},{96,112},{112,96},{1... | collective-permute-start | bytes 3735560 | tf_op jit(solution)/shard_map/ppermute | solution.py:198
  128.3 14.7 %copy-start.19 = (s32[128]{0:T(128)S(1)}, s32[128]{0:T(128)}, u32[]{:S(2)}) copy-start(s32[128]{0:T(128)} %param.17) | copy-start | bytes 1540
  128.3 14.7 %copy-start.20 = (f32[128]{0:T(128)S(1)}, f32[128]{0:T(128)}, u32[]{:S(2)}) copy-start(f32[128]{0:T(128)} %param.16) | copy-start | bytes 1540
  128.3 14.7 %copy-start.21 = (f32[128]{0:T(128)S(1)}, f32[128]{0:T(128)}, u32[]{:S(2)}) copy-start(f32[128]{0:T(128)} %param.15) | copy-start | bytes 1540
  145.0 3.6 %collective-permute-start.11 = (bf16[128,2432]{1,0:T(8,128)(2,1)S(1)}, bf16[128,2432]{1,0:T(8,128)(2,1)S(1)}, u32[]{:S(2)}, u32[]{:S(2)}) collective-permute-start(bf16[128,2432]{1,0:T(8,128)(2,1)S(1)} %multiply_convert_fusion), channel_id=1, source_target_pairs={{0,16},{16,0},{32,48},{48,32},{64,80},{80,64},{96,112},{112,96},{1... | collective-permute-start | bytes 1867784 | tf_op jit(solution)/shard_map/ppermute | solution.py:242
  155.2 36.8 %all-to-all-start.1 = ((f32[16,256,128]{2,1,0:T(8,128)}), f32[16,256,128]{2,1,0:T(8,128)S(1)}, u32[]{:S(2)}, u32[]{:S(2)}) async-start(f32[16,256,128]{2,1,0:T(8,128)} %shard_map.130), calls=%async_computation.1 | async-start | bytes 4194304 | tf_op jit(solution)/shard_map/all_to_all | solution.py:254
  159.1 1.3 collective-permute-start.12
  171.7 20.5 %copy-start.14 = (bf16[128,256]{0,1:T(8,128)(2,1)S(1)}, bf16[128,256]{0,1:T(8,128)(2,1)}, u32[]{:S(2)}) copy-start(bf16[128,256]{0,1:T(8,128)(2,1)} %dynamic-slice_select_fusion) | copy-start | bytes 196612
  192.3 9.0 %collective-permute-start.14 = (f32[128,256]{0,1:T(8,128)S(1)}, f32[128,256]{0,1:T(8,128)S(1)}, u32[]{:S(2)}, u32[]{:S(2)}) collective-permute-start(f32[128,256]{0,1:T(8,128)S(1)} %get-tuple-element.52), channel_id=1, source_target_pairs={{0,0},{1,16},{2,2},{3,18},{4,4},{5,20},{6,6},{7,22},{8,8},{9,24},{... | collective-permute-start | bytes 393224 | tf_op jit(solution)/shard_map/ppermute | solution.py:268
  194.2 0.7 collective-permute-start.13
  201.5 27.9 %copy-start = (f32[16,4,32,256]{3,2,1,0:T(8,128)S(1)}, f32[16,4,32,256]{3,2,1,0:T(8,128)}, u32[]{:S(2)}) copy-start(f32[16,4,32,256]{3,2,1,0:T(8,128)} %shard_map.131.proj_ref) | copy-start | bytes 6291460
  233.6 20.4 %all-to-all-start.3 = ((f32[256,1,128]{2,1,0:T(1,128)}), f32[256,1,128]{2,1,0:T(1,128)S(1)}, u32[]{:S(2)}, u32[]{:S(2)}) async-start(f32[256,1,128]{2,1,0:T(1,128)} %bitcast.33), calls=%async_computation.3 | async-start | bytes 262144 | tf_op jit(solution)/shard_map/all_to_all | solution.py:296
  (17 other events, 73.6 us)
Sparse Core Ops, SparseCore 0:
  112.0 52.0 all-gather.2

commit v7 on v6

--- a/solution.py
+++ b/solution.py
@@ -44,22 +44,21 @@
     proj_ref[...] = out.astype(proj_ref.dtype).reshape(proj_ref.shape)
 
 
-def slot_kernel(side_ref, rows_ref, proj_ref, weighted_ref, gate_ref):
+def gate_kernel(side_ref, rows_ref, proj_ref, gate_ref):
     groups, per_expert, slots, _ = side_ref.shape
     tokens, width = rows_ref.shape[1:]
     count = per_expert * slots
     column = lax.broadcasted_iota(jnp.int32, (count, tokens), 1)
     gates = jnp.zeros((count, lanes), f32)
     for group in range(groups):
-        side = side_ref[group].reshape(count, lanes).astype(f32)
-        match = jnp.where(column.astype(f32) == side[:, 1:2], 1.0, 0.0).astype(bf16)
+        token = side_ref[group].reshape(count, lanes)[:, 1:2].astype(f32)
+        match = jnp.where(column.astype(f32) == token, 1.0, 0.0).astype(bf16)
         rows = jnp.dot(match, rows_ref[group], preferred_element_type=f32)
-        proj = proj_ref[group].reshape(count, width)
-        gate = jnp.sum(rows * proj, axis=1, keepdims=True)
+        gate = jnp.sum(rows * proj_ref[group].reshape(count, width), axis=1, keepdims=True)
         gates = jnp.where(column == group, gate, gates)
-        weighted = (side[:, 0:1] * rows).astype(bf16)
-        weighted_ref[:, group] = weighted.reshape(per_expert, slots, width)
-    gate_ref[...] = gates.T[:groups]
+    gates = gates.T
+    for group in range(groups):
+        gate_ref[group] = jnp.broadcast_to(gates[group : group + 1], gate_ref.shape[1:])
 
 
 def hidden_kernel(nz, place_ref, grad_ref, *refs):
@@ -83,12 +82,28 @@
         out_ref[2 * block + 1 - core, rows] = part[:, tokens:]
 
 
-def down_kernel(acts_ref, weighted_ref, out_ref):
-    groups, _, slots, wide = acts_ref.shape
-    acts = acts_ref[:, 0].reshape(groups * slots, wide)
-    weighted = weighted_ref[0].reshape(groups * slots, weighted_ref.shape[3])
+def down_kernel(side_ref, rows_ref, acts_ref, out_ref, weighted):
+    groups, per_expert, slots, _ = side_ref.shape
+    tokens, width = rows_ref.shape[1:]
+    count = per_expert * slots
+    expert = pl.program_id(0)
+
+    @pl.when(expert == 0)
+    def _():
+        column = lax.broadcasted_iota(jnp.int32, (count, tokens), 1).astype(f32)
+        for group in range(groups):
+            side = side_ref[group].reshape(count, lanes).astype(f32)
+            match = jnp.where(column == side[:, 1:2], 1.0, 0.0).astype(bf16)
+            rows = jnp.dot(match, rows_ref[group], preferred_element_type=f32)
+            made = (side[:, 0:1] * rows).astype(bf16)
+            weighted[:, group] = made.reshape(per_expert, slots, width)
+
+    acts = acts_ref[:, 0].reshape(groups * slots, acts_ref.shape[3])
     out_ref[0] = lax.dot_general(
-        acts, weighted, (((0,), (0,)), ((), ())), preferred_element_type=f32
+        acts,
+        weighted[expert].reshape(groups * slots, width),
+        (((0,), (0,)), ((), ())),
+        preferred_element_type=f32,
     ).astype(bf16)
 
 
@@ -271,33 +286,29 @@
     all_rows = lax.all_to_all(
         jnp.broadcast_to(stream_grad[None], (mp_count, tokens, block)), "mp", 0, 0, tiled=True
     )
-    weighted, gate = pl.pallas_call(
-        slot_kernel,
+    gate = pl.pallas_call(
+        gate_kernel,
         in_specs=[pl.BlockSpec(memory_space=pltpu.VMEM)] * 3,
-        out_specs=[pl.BlockSpec(memory_space=pltpu.VMEM)] * 2,
-        out_shape=[
-            jax.ShapeDtypeStruct((per_expert, dp_count, capacity, block), bf16),
-            jax.ShapeDtypeStruct((dp_count, per_expert * capacity), f32),
-        ],
+        out_specs=pl.BlockSpec(memory_space=pltpu.VMEM),
+        out_shape=jax.ShapeDtypeStruct((dp_count, mp_count, per_expert * capacity), f32),
         compiler_params=pltpu.CompilerParams(vmem_limit_bytes=32 * 1024 * 1024),
     )(side_all, all_rows, proj)
     down_grad = pl.pallas_call(
         down_kernel,
         grid=(per_expert,),
         in_specs=[
+            pl.BlockSpec((dp_count, per_expert, capacity, lanes), lambda e: (0, 0, 0, 0)),
+            pl.BlockSpec((dp_count, tokens, block), lambda e: (0, 0, 0)),
             pl.BlockSpec((dp_count, 1, capacity, hidden_width), lambda e: (0, e, 0, 0)),
-            pl.BlockSpec((1, dp_count, capacity, block), lambda e: (e, 0, 0, 0)),
         ],
         out_specs=pl.BlockSpec((1, hidden_width, block), lambda e: (e, 0, 0)),
         out_shape=jax.ShapeDtypeStruct((per_expert, hidden_width, block), bf16),
+        scratch_shapes=[pltpu.VMEM((per_expert, dp_count, capacity, block), bf16)],
         compiler_params=pltpu.CompilerParams(vmem_limit_bytes=56 * 1024 * 1024),
-    )(acts_all, weighted)
+    )(side_all, all_rows, acts_all)
 
     gate = lax.all_to_all(
-        jnp.broadcast_to(gate[:, None, :], (dp_count, mp_count, per_expert * capacity)).reshape(
-            dp_count * mp_count, 1, per_expert * capacity
-        ),
-        both, 0, 0, tiled=True,
+        gate.reshape(dp_count * mp_count, 1, per_expert * capacity), both, 0, 0, tiled=True
     ).reshape(dp_count, mp_count, per_expert * capacity)
     slot_gate = jnp.sum(gate, axis=0).reshape(experts_all, capacity)
     per_token = jnp.sum(jnp.where(matches, slot_gate[:, :, None], 0.0), axis=1)

time: 263 us -> 262 us (level)
  transfers between devices with their start and end apart: 18 -> 18, of which waited for: 11 -> 11; matrix products, arithmetic and copies ran while one was open for 20% -> 20% of each run, Pallas kernels for 7% -> 8%
where the time goes in v7:
time: 262 us; the launch traced here: 261 us
  waiting for transfers between devices  91.7 us (35%)
  blocking collectives  40.9 us (16%)
  starting transfers between devices  36 us (14%)
  Pallas kernels  23.1 us (9%)
  other arithmetic  23 us (9%)
  matrix products  17.9 us (7%)
  between operations  14.5 us (6%)
  local copies, waits for them, and re-layouts  13.6 us (5%)
    ppermute x2, waiting for transfers between devices, local(): ahead = lax.ppermute(ahead, 'dp', z_shift(1, nz))  42 us
    all_to_all x1, blocking collectives, local(): lax.all_to_all(jnp.broadcast_to(stream_grad[None], (mp_count, tokens, blo...  27.9 us
    all_to_all x1, waiting for transfers between devices, local(): hidden = lax.all_to_all(hidden, 'mp', 0, 0, tiled=True)  20.2 us
    dot_general x11, matrix products, logits_of(): return jnp.dot(features, piece, preferred_element_type=f32)  17.9 us
    all_to_all x1, blocking collectives, local(): lax.all_to_all(jnp.broadcast_to(stats[None], (mp_count, 4, tokens)), 'mp'...  13 us
    ppermute x1, waiting for transfers between devices, local(): lax.ppermute(ahead[:half], 'dp', z_shift(1, nz))  10.7 us
    all_to_all x1, starting transfers between devices, local(): lax.all_to_all(gate.reshape(dp_count * mp_count, 1, per_expert * capacity...  7.3 us
    pallas_call x1, Pallas kernels, local(): pl.pallas_call(down_kernel, grid=(per_expert,), in_specs=[pl.BlockSpec((d...  7.17 us
  transfers between devices with their start and end apart: 18, of which 11 were waited for; matrix products, arithmetic and copies ran while one was open for 20% of the time, Pallas kernels for 8%

profile of v7, /device:TPU:1, one launch (start us, length us, event | category | flops | bytes accessed | tf_op | source)
XLA Modules:
  0.0 260.7 jit_solution(5628013588073070731)
XLA Ops:
  7.2 2.5 collective-permute-start.4
  9.8 4.0 %collective-permute-start = (bf16[256,2432]{1,0:T(8,128)(2,1)}, bf16[256,2432]{1,0:T(8,128)(2,1)S(1)}, u32[]{:S(2)}, u32[]{:S(2)}) collective-permute-start(bf16[256,2432]{1,0:T(8,128)(2,1)} %refs_0_.1), channel_id=1, source_target_pairs={{0,224},{16,240},{32,0},{48,16},{64,32},{80,48},{96,64},{112,80},{... | collective-permute-start | bytes 3735560 | tf_op jit(solution)/shard_map/ppermute | solution.py:184
  18.6 2.3 dynamic-slice_bitcast_fusion.1
  41.0 2.7 %collective-permute-start.3 = (bf16[256,2432]{1,0:T(8,128)(2,1)S(1)}, bf16[256,2432]{1,0:T(8,128)(2,1)}, u32[]{:S(2)}, u32[]{:S(2)}) collective-permute-start(bf16[256,2432]{1,0:T(8,128)(2,1)S(1)} %collective-permute-done.refs_2_), channel_id=1, source_target_pairs={{0,224},{16,240},{32,0},{48,16},{64,32},{80,48},{96,64},{112,80},{... | collective-permute-start | bytes 3735560 | tf_op jit(solution)/shard_map/ppermute | solution.py:198
  48.1 21.9 %collective-permute-done.6.refs_3_ = bf16[256,2432]{1,0:T(8,128)(2,1)} collective-permute-done((bf16[256,2432]{1,0:T(8,128)(2,1)S(1)}, bf16[256,2432]{1,0:T(8,128)(2,1)}, u32[]{:S(2)}, u32[]{:S(2)}) %collective-permute-start.6) | collective-permute-done | bytes 1245216 | tf_op jit(solution)/shard_map/ppermute | solution.py:197
  70.0 2.7 %collective-permute-start.5 = (bf16[256,2432]{1,0:T(8,128)(2,1)}, bf16[256,2432]{1,0:T(8,128)(2,1)S(1)}, u32[]{:S(2)}, u32[]{:S(2)}) collective-permute-start(bf16[256,2432]{1,0:T(8,128)(2,1)} %collective-permute-done.3.refs_4_), channel_id=1, source_target_pairs={{0,224},{16,240},{32,0},{48,16},{64,32},{80,48},{96,64},{112,80},{... | collective-permute-start | bytes 3735560 | tf_op jit(solution)/shard_map/ppermute | solution.py:198
  74.7 3.3 %fusion = f32[256,2432]{1,0:T(8,128)} fusion(f32[256,2432]{1,0:T(8,128)S(1)} %fusion.13, f32[256,2432]{1,0:T(8,128)S(1)} %copy-done.10, bf16[256,2432]{1,0:T(8,128)(2,1)} %collective-permute-done.6.refs_3_, bf16[8,256,256]{1,2,0:T(8,128)(2,1)S(1)} %pad_maximum_fusion.1, s32[]{:T(128)S(6)} %select_n.127), kind=kOutput, calls=%fused_computation.4 | convolution fusion | flops 320012288 | bytes 8847364 | tf_op jit(solution)/shard_map/dot_general | solution.py:180
  78.0 20.1 %collective-permute-done.7.refs_5_ = bf16[256,2432]{1,0:T(8,128)(2,1)S(1)} collective-permute-done((bf16[256,2432]{1,0:T(8,128)(2,1)}, bf16[256,2432]{1,0:T(8,128)(2,1)S(1)}, u32[]{:S(2)}, u32[]{:S(2)}) %collective-permute-start.7) | collective-permute-done | bytes 1245216 | tf_op jit(solution)/shard_map/ppermute | solution.py:197
  98.3 2.9 %collective-permute-start.9 = (bf16[128,2432]{1,0:T(8,128)(2,1)S(1)}, bf16[128,2432]{1,0:T(8,128)(2,1)}, u32[]{:S(2)}, u32[]{:S(2)}) collective-permute-start(bf16[128,2432]{1,0:T(8,128)(2,1)S(1)} %slice.50), channel_id=1, source_target_pairs={{0,224},{16,240},{32,0},{48,16},{64,32},{80,48},{96,64},{112,80},{... | collective-permute-start | bytes 1867784 | tf_op jit(solution)/shard_map/ppermute | solution.py:204
  101.2 10.7 %collective-permute-done.8.refs_7_ = bf16[128,2432]{1,0:T(8,128)(2,1)S(1)} collective-permute-done((bf16[128,2432]{1,0:T(8,128)(2,1)S(1)}, bf16[128,2432]{1,0:T(8,128)(2,1)S(1)}, u32[]{:S(2)}, u32[]{:S(2)}) %collective-permute-start.8) | collective-permute-done | bytes 622624 | tf_op jit(solution)/shard_map/ppermute | solution.py:203
  116.6 3.0 %fusion.5 = f32[128,2432]{1,0:T(8,128)} fusion(f32[128,2432]{1,0:T(8,128)S(1)} %fusion.35, f32[256,2432]{1,0:T(8,128)S(1)} %fusion.1, bf16[128,2432]{1,0:T(8,128)(2,1)} %collective-permute-done.9.refs_8_, bf16[256,256]{1,0:T(8,128)(2,1)S(1)} %bitcast.97), kind=kOutput, calls=%fused_computation.12 | convolution fusion | flops 80314368 | bytes 4390912 | tf_op jit(solution)/shard_map/dot_general | solution.py:180
  119.6 4.0 %collective-permute-start.10 = (f32[128,2432]{1,0:T(8,128)}, f32[128,2432]{1,0:T(8,128)}, u32[]{:S(2)}, u32[]{:S(2)}) collective-permute-start(f32[128,2432]{1,0:T(8,128)} %fusion.5), channel_id=1, source_target_pairs={{0,16},{16,0},{32,48},{48,32},{64,80},{80,64},{96,112},{112,96},{1... | collective-permute-start | bytes 3735560 | tf_op jit(solution)/shard_map/ppermute | solution.py:213
  129.8 13.0 %all_to_all.20 = f32[16,4,128]{2,1,0:T(4,128)S(1)} all-to-all(f32[16,4,128]{2,1,0:T(4,128)S(1)} %broadcast_in_dim.134), channel_id=1, replica_groups=mesh['dp'=16,'mp'=16] {'mp'}, dimensions={0} | all-to-all | bytes 65536 | tf_op jit(solution)/shard_map/all_to_all | solution.py:238
  148.7 6.5 %shard_map.130 = f32[16,256,128]{2,1,0:T(8,128)} custom-call(s32[2]{0:T(128)S(1)} %pad_add_fusion.place_ref, bf16[256,2432]{1,0:T(8,128)(2,1)S(1)} %pad_maximum_fusion.grad_ref, bf16[256,2432]{1,0:T(8,128)(2,1)S(1)} %copy-done.6, bf16[256,2432]{1,0:T(8,128)(2,1)S(1)} %copy-done.3, bf16[256,2432]{1,0:T(8,128)(2,1)S(1)} %copy-done.5, ...), custom_call_target="tpu_custom_call" | custom-call | tf_op jit(solution)/shard_map/pallas_call | solution.py:260
  155.2 3.9 %all-to-all-start.1 = ((f32[16,256,128]{2,1,0:T(8,128)}), f32[16,256,128]{2,1,0:T(8,128)S(1)}, u32[]{:S(2)}, u32[]{:S(2)}) async-start(f32[16,256,128]{2,1,0:T(8,128)} %shard_map.130), calls=%async_computation.1 | async-start | bytes 4194304 | tf_op jit(solution)/shard_map/all_to_all | solution.py:269
  160.5 3.7 %all-gather.3.cloned.1.call-done = bf16[64,32,1664]{2,1,0:T(8,128)(2,1)} async-done(((bf16[4,32,1664]{2,1,0:T(8,128)(2,1)}), bf16[64,32,1664]{2,1,0:T(8,128)(2,1)}) %all-gather.3.cloned.1.call-update) | async-done | bytes 6815760 | tf_op jit(solution)/shard_map/all_gather | solution.py:216
  165.2 6.6 %shard_map.131.proj_ref = f32[16,4,32,256]{3,2,1,0:T(8,128)} custom-call(bf16[16,4,32,1664]{3,2,1,0:T(8,128)(2,1)} %bitcast.92, bf16[4,1536,256]{2,1,0:T(8,128)(2,1)} %down_ref.1), custom_call_target="tpu_custom_call" | custom-call | tf_op jit(solution)/shard_map/pallas_call | solution.py:217
  171.8 20.2 %all-to-all-done.1 = f32[16,256,128]{2,1,0:T(8,128)S(1)} async-done(((f32[16,256,128]{2,1,0:T(8,128)}), f32[16,256,128]{2,1,0:T(8,128)S(1)}, u32[]{:S(2)}, u32[]{:S(2)}) %all-to-all-start.1) | async-done | bytes 2097184 | tf_op jit(solution)/shard_map/all_to_all | solution.py:269
  194.9 6.4 %collective-permute-done.14 = f32[128,256]{0,1:T(8,128)S(1)} collective-permute-done((f32[128,256]{0,1:T(8,128)S(1)}, f32[128,256]{0,1:T(8,128)S(1)}, u32[]{:S(2)}, u32[]{:S(2)}) %collective-permute-start.14) | collective-permute-done | bytes 131104 | tf_op jit(solution)/shard_map/ppermute | solution.py:283
  201.5 27.9 %all_to_all.21.rows_ref = bf16[16,128,256]{2,1,0:T(8,128)(2,1)S(1)} all-to-all(bf16[16,128,256]{2,1,0:T(8,128)(2,1)S(1)} %broadcast_in_dim.135), channel_id=1, replica_groups=mesh['dp'=16,'mp'=16] {'mp'}, dimensions={0} | all-to-all | bytes 2097152 | tf_op jit(solution)/shard_map/all_to_all | solution.py:286
  229.5 2.8 %shard_map.133 = f32[16,16,128]{2,1,0:T(8,128)} custom-call(bf16[16,4,32,128]{3,2,1,0:T(8,128)(2,1)S(1)} %slice.71.side_ref, bf16[16,128,256]{2,1,0:T(8,128)(2,1)S(1)} %all_to_all.21.rows_ref, f32[16,4,32,256]{3,2,1,0:T(8,128)S(1)} %copy-done.1), custom_call_target="tpu_custom_call" | custom-call | tf_op jit(solution)/shard_map/pallas_call | solution.py:289
  232.3 7.3 %all-to-all-start.3 = ((f32[256,1,128]{2,1,0:T(1,128)}), f32[256,1,128]{2,1,0:T(1,128)S(1)}, u32[]{:S(2)}, u32[]{:S(2)}) async-start(f32[256,1,128]{2,1,0:T(1,128)} %bitcast.34), calls=%async_computation.3 | async-start | bytes 262144 | tf_op jit(solution)/shard_map/all_to_all | solution.py:310
  240.3 7.2 %shard_map.132 = bf16[4,1536,256]{2,1,0:T(8,128)(2,1)} custom-call(bf16[16,4,32,128]{3,2,1,0:T(8,128)(2,1)} %copy-done.7, bf16[16,128,256]{2,1,0:T(8,128)(2,1)} %copy-done, bf16[16,4,32,1664]{3,2,1,0:T(8,128)(2,1)} %bitcast.93), custom_call_target="tpu_custom_call" | custom-call | tf_op jit(solution)/shard_map/pallas_call | solution.py:296
  247.5 5.1 %all-to-all-done.3 = f32[256,1,128]{2,1,0:T(1,128)S(1)} async-done(((f32[256,1,128]{2,1,0:T(1,128)}), f32[256,1,128]{2,1,0:T(1,128)S(1)}, u32[]{:S(2)}, u32[]{:S(2)}) %all-to-all-start.3) | async-done | bytes 131104 | tf_op jit(solution)/shard_map/all_to_all | solution.py:310
  (133 shorter events, 55.5 us)
Async XLA Ops:
  7.2 156.9 %all-gather.3.cloned.1.call-start = ((), (), s32[]{:S(2)}) async-start(), calls=%async_computation.4 | async-start | bytes 7241728 | tf_op jit(solution)/shard_map/all_gather | solution.py:216
  7.2 33.8 %collective-permute-start.4 = (bf16[256,2432]{1,0:T(8,128)(2,1)}, bf16[256,2432]{1,0:T(8,128)(2,1)S(1)}, u32[]{:S(2)}, u32[]{:S(2)}) collective-permute-start(bf16[256,2432]{1,0:T(8,128)(2,1)} %refs_0_.1), channel_id=1, source_target_pairs={{0,32},{16,48},{32,64},{48,80},{64,96},{80,112},{96,128},{112,144}... | collective-permute-start | bytes 3735560 | tf_op jit(solution)/shard_map/ppermute | solution.py:183
  9.8 30.4 %collective-permute-start = (bf16[256,2432]{1,0:T(8,128)(2,1)}, bf16[256,2432]{1,0:T(8,128)(2,1)S(1)}, u32[]{:S(2)}, u32[]{:S(2)}) collective-permute-start(bf16[256,2432]{1,0:T(8,128)(2,1)} %refs_0_.1), channel_id=1, source_target_pairs={{0,224},{16,240},{32,0},{48,16},{64,32},{80,48},{96,64},{112,80},{... | collective-permute-start | bytes 3735560 | tf_op jit(solution)/shard_map/ppermute | solution.py:184
  20.9 17.8 %collective-permute-start.1 = (bf16[8,128,256]{1,2,0:T(8,128)(2,1)}, bf16[8,128,256]{1,2,0:T(8,128)(2,1)}, u32[]{:S(2)}, u32[]{:S(2)}) collective-permute-start(bf16[8,128,256]{1,2,0:T(8,128)(2,1)} %get-tuple-element.54), channel_id=1, source_target_pairs={{0,16},{16,0},{32,48},{48,32},{64,80},{80,64},{96,112},{112,96},{1... | collective-permute-start | bytes 1572872 | tf_op jit(solution)/shard_map/ppermute | solution.py:142
  22.5 14.8 %collective-permute-start.2 = (bf16[128,256]{0,1:T(8,128)(2,1)}, bf16[128,256]{0,1:T(8,128)(2,1)}, u32[]{:S(2)}, u32[]{:S(2)}) collective-permute-start(bf16[128,256]{0,1:T(8,128)(2,1)} %constant_dynamic-slice_fusion.3), channel_id=1, source_target_pairs={{0,16},{16,0},{32,48},{48,32},{64,80},{80,64},{96,112},{112,96},{1... | collective-permute-start | bytes 196616 | tf_op jit(solution)/shard_map/ppermute | solution.py:146
  40.1 34.5 %copy-start.13 = (bf16[8,256,256]{1,2,0:T(8,128)(2,1)}, bf16[8,256,256]{1,2,0:T(8,128)(2,1)S(1)}, u32[]{:S(2)}) copy-start(bf16[8,256,256]{1,2,0:T(8,128)(2,1)S(1)} %pad_maximum_fusion.1) | copy-start | bytes 3145732
  41.0 29.0 %collective-permute-start.6 = (bf16[256,2432]{1,0:T(8,128)(2,1)S(1)}, bf16[256,2432]{1,0:T(8,128)(2,1)}, u32[]{:S(2)}, u32[]{:S(2)}) collective-permute-start(bf16[256,2432]{1,0:T(8,128)(2,1)S(1)} %collective-permute-done.4.refs_1_), channel_id=1, source_target_pairs={{0,32},{16,48},{32,64},{48,80},{64,96},{80,112},{96,128},{112,144}... | collective-permute-start | bytes 3735560 | tf_op jit(solution)/shard_map/ppermute | solution.py:197
  41.0 29.0 %collective-permute-start.3 = (bf16[256,2432]{1,0:T(8,128)(2,1)S(1)}, bf16[256,2432]{1,0:T(8,128)(2,1)}, u32[]{:S(2)}, u32[]{:S(2)}) collective-permute-start(bf16[256,2432]{1,0:T(8,128)(2,1)S(1)} %collective-permute-done.refs_2_), channel_id=1, source_target_pairs={{0,224},{16,240},{32,0},{48,16},{64,32},{80,48},{96,64},{112,80},{... | collective-permute-start | bytes 3735560 | tf_op jit(solution)/shard_map/ppermute | solution.py:198
  70.0 28.1 %collective-permute-start.7 = (bf16[256,2432]{1,0:T(8,128)(2,1)}, bf16[256,2432]{1,0:T(8,128)(2,1)S(1)}, u32[]{:S(2)}, u32[]{:S(2)}) collective-permute-start(bf16[256,2432]{1,0:T(8,128)(2,1)} %collective-permute-done.6.refs_3_), channel_id=1, source_target_pairs={{0,32},{16,48},{32,64},{48,80},{64,96},{80,112},{96,128},{112,144}... | collective-permute-start | bytes 3735560 | tf_op jit(solution)/shard_map/ppermute | solution.py:197
  70.0 28.3 %collective-permute-start.5 = (bf16[256,2432]{1,0:T(8,128)(2,1)}, bf16[256,2432]{1,0:T(8,128)(2,1)S(1)}, u32[]{:S(2)}, u32[]{:S(2)}) collective-permute-start(bf16[256,2432]{1,0:T(8,128)(2,1)} %collective-permute-done.3.refs_4_), channel_id=1, source_target_pairs={{0,224},{16,240},{32,0},{48,16},{64,32},{80,48},{96,64},{112,80},{... | collective-permute-start | bytes 3735560 | tf_op jit(solution)/shard_map/ppermute | solution.py:198
  98.1 13.7 %collective-permute-start.8 = (bf16[128,2432]{1,0:T(8,128)(2,1)S(1)}, bf16[128,2432]{1,0:T(8,128)(2,1)S(1)}, u32[]{:S(2)}, u32[]{:S(2)}) collective-permute-start(bf16[128,2432]{1,0:T(8,128)(2,1)S(1)} %slice.63), channel_id=1, source_target_pairs={{0,32},{16,48},{32,64},{48,80},{64,96},{80,112},{96,128},{112,144}... | collective-permute-start | bytes 1867784 | tf_op jit(solution)/shard_map/ppermute | solution.py:203
  98.3 13.6 %collective-permute-start.9 = (bf16[128,2432]{1,0:T(8,128)(2,1)S(1)}, bf16[128,2432]{1,0:T(8,128)(2,1)}, u32[]{:S(2)}, u32[]{:S(2)}) collective-permute-start(bf16[128,2432]{1,0:T(8,128)(2,1)S(1)} %slice.50), channel_id=1, source_target_pairs={{0,224},{16,240},{32,0},{48,16},{64,32},{80,48},{96,64},{112,80},{... | collective-permute-start | bytes 1867784 | tf_op jit(solution)/shard_map/ppermute | solution.py:204
  119.6 6.9 %collective-permute-start.10 = (f32[128,2432]{1,0:T(8,128)}, f32[128,2432]{1,0:T(8,128)}, u32[]{:S(2)}, u32[]{:S(2)}) collective-permute-start(f32[128,2432]{1,0:T(8,128)} %fusion.5), channel_id=1, source_target_pairs={{0,16},{16,0},{32,48},{48,32},{64,80},{80,64},{96,112},{112,96},{1... | collective-permute-start | bytes 3735560 | tf_op jit(solution)/shard_map/ppermute | solution.py:213
  128.3 14.7 %copy-start.20 = (s32[128]{0:T(128)S(1)}, s32[128]{0:T(128)}, u32[]{:S(2)}) copy-start(s32[128]{0:T(128)} %param.17) | copy-start | bytes 1540
  128.3 14.7 %copy-start.21 = (f32[128]{0:T(128)S(1)}, f32[128]{0:T(128)}, u32[]{:S(2)}) copy-start(f32[128]{0:T(128)} %param.16) | copy-start | bytes 1540
  145.0 3.6 %collective-permute-start.11 = (bf16[128,2432]{1,0:T(8,128)(2,1)S(1)}, bf16[128,2432]{1,0:T(8,128)(2,1)S(1)}, u32[]{:S(2)}, u32[]{:S(2)}) collective-permute-start(bf16[128,2432]{1,0:T(8,128)(2,1)S(1)} %multiply_convert_fusion), channel_id=1, source_target_pairs={{0,16},{16,0},{32,48},{48,32},{64,80},{80,64},{96,112},{112,96},{1... | collective-permute-start | bytes 1867784 | tf_op jit(solution)/shard_map/ppermute | solution.py:257
  155.2 36.8 %all-to-all-start.1 = ((f32[16,256,128]{2,1,0:T(8,128)}), f32[16,256,128]{2,1,0:T(8,128)S(1)}, u32[]{:S(2)}, u32[]{:S(2)}) async-start(f32[16,256,128]{2,1,0:T(8,128)} %shard_map.130), calls=%async_computation.1 | async-start | bytes 4194304 | tf_op jit(solution)/shard_map/all_to_all | solution.py:269
  159.1 1.3 collective-permute-start.12
  165.2 64.3 %copy-start.7 = (bf16[16,4,32,128]{3,2,1,0:T(8,128)(2,1)}, bf16[16,4,32,128]{3,2,1,0:T(8,128)(2,1)S(1)}, u32[]{:S(2)}) copy-start(bf16[16,4,32,128]{3,2,1,0:T(8,128)(2,1)S(1)} %slice.71.side_ref) | copy-start | bytes 1572868
  171.8 20.3 %copy-start.15 = (bf16[128,256]{0,1:T(8,128)(2,1)S(1)}, bf16[128,256]{0,1:T(8,128)(2,1)}, u32[]{:S(2)}) copy-start(bf16[128,256]{0,1:T(8,128)(2,1)} %dynamic-slice_select_fusion) | copy-start | bytes 196612
  192.3 9.0 %collective-permute-start.14 = (f32[128,256]{0,1:T(8,128)S(1)}, f32[128,256]{0,1:T(8,128)S(1)}, u32[]{:S(2)}, u32[]{:S(2)}) collective-permute-start(f32[128,256]{0,1:T(8,128)S(1)} %get-tuple-element.48), channel_id=1, source_target_pairs={{0,0},{1,16},{2,2},{3,18},{4,4},{5,20},{6,6},{7,22},{8,8},{9,24},{... | collective-permute-start | bytes 393224 | tf_op jit(solution)/shard_map/ppermute | solution.py:283
  194.2 0.7 collective-permute-start.13
  201.5 27.9 %copy-start.1 = (f32[16,4,32,256]{3,2,1,0:T(8,128)S(1)}, f32[16,4,32,256]{3,2,1,0:T(8,128)}, u32[]{:S(2)}) copy-start(f32[16,4,32,256]{3,2,1,0:T(8,128)} %shard_map.131.proj_ref) | copy-start | bytes 6291460
  232.3 20.4 %all-to-all-start.3 = ((f32[256,1,128]{2,1,0:T(1,128)}), f32[256,1,128]{2,1,0:T(1,128)S(1)}, u32[]{:S(2)}, u32[]{:S(2)}) async-start(f32[256,1,128]{2,1,0:T(1,128)} %bitcast.34), calls=%async_computation.3 | async-start | bytes 262144 | tf_op jit(solution)/shard_map/all_to_all | solution.py:310
  (18 other events, 90.1 us)
Sparse Core Ops, SparseCore 0:
  112.0 52.0 all-gather.2

commit v8 on v7

--- a/solution.py
+++ b/solution.py
@@ -205,12 +205,17 @@
     ]
     for piece in head_pieces[used:]:
         partial = partial + logits_of(everything, *piece)
-    own_part, other_part = partial[:tokens], partial[tokens:]
+    own_part, early = partial[:tokens], swap(partial[tokens:])
+    late = None
     for piece in last_pieces:
-        other_part = other_part + logits_of(slice(tokens, None), *piece)
+        added = logits_of(slice(tokens, None), *piece)
+        late = added if late is None else late + added
+    late = swap(late)
+    own_part = own_part + early
+    for piece in last_pieces:
         own_part = own_part + logits_of(slice(0, tokens), *piece)
     head_pieces += last_pieces
-    logits = own_part + swap(other_part)
+    logits = own_part + late
 
     acts_block, _ = lax.optimization_barrier((acts_block, tuple(p for _, _, p in last_pieces)))
     acts_all = lax.all_gather(acts_block, "dp", axis=0, tiled=False)

time: 262 us -> 265 us (1.011)
  waiting for transfers between devices: 91.7 us -> 94.8 us
    ppermute x2, waiting for transfers between devices: 42 us -> 0.01 us  [local(): ahead = lax.ppermute(ahead, 'dp', z_shift(1, nz))]
    ppermute x2, waiting for transfers between devices: 0.01 us -> 39.4 us  [local(): back = lax.ppermute(back, 'dp', z_shift(-1, nz))]
    ppermute x1, waiting for transfers between devices: 0.01 us -> 9.61 us  [local(): lax.ppermute(back[half:], 'dp', z_shift(-1, nz))]
    ppermute x1, waiting for transfers between devices: 10.7 us -> 3.44 us  [local(): lax.ppermute(ahead[:half], 'dp', z_shift(1, nz))]
    all_to_all x1, waiting for transfers between devices: 20.2 us -> 23.9 us  [local(): hidden = lax.all_to_all(hidden, 'mp', 0, 0, tiled=True)]
    all_gather x1, waiting for transfers between devices: 3.66 us -> 0.04 us  [local(): acts_all = lax.all_gather(acts_block, 'dp', axis=0, tiled=False)]
    ppermute x1, waiting for transfers between devices: 0.02 us -> 3.58 us  [local(): back = lax.ppermute(head_weight, 'dp', z_shift(-1, nz))]
  transfers between devices with their start and end apart: 18 -> 19, of which waited for: 11 -> 11; matrix products, arithmetic and copies ran while one was open for 20% -> 19% of each run, Pallas kernels for 8% -> 8%
where the time goes in v8:
time: 265 us; the launch traced here: 264 us
  waiting for transfers between devices  94.8 us (36%)
  blocking collectives  40.8 us (15%)
  starting transfers between devices  38 us (14%)
  Pallas kernels  23 us (9%)
  other arithmetic  21 us (8%)
  matrix products  17.7 us (7%)
  between operations  14.6 us (6%)
  local copies, waits for them, and re-layouts  14.2 us (5%)
    ppermute x2, waiting for transfers between devices, local(): back = lax.ppermute(back, 'dp', z_shift(-1, nz))  39.4 us
    all_to_all x1, blocking collectives, local(): lax.all_to_all(jnp.broadcast_to(stream_grad[None], (mp_count, tokens, blo...  27.9 us
    all_to_all x1, waiting for transfers between devices, local(): hidden = lax.all_to_all(hidden, 'mp', 0, 0, tiled=True)  23.9 us
    dot_general x11, matrix products, logits_of(): return jnp.dot(features, piece, preferred_element_type=f32)  17.7 us
    all_to_all x1, blocking collectives, local(): lax.all_to_all(jnp.broadcast_to(stats[None], (mp_count, 4, tokens)), 'mp'...  12.9 us
    ppermute x1, waiting for transfers between devices, local(): lax.ppermute(back[half:], 'dp', z_shift(-1, nz))  9.61 us
    pallas_call x1, Pallas kernels, local(): pl.pallas_call(down_kernel, grid=(per_expert,), in_specs=[pl.BlockSpec((d...  7.17 us
    ppermute x2, starting transfers between devices, local(): back = lax.ppermute(back, 'dp', z_shift(-1, nz))  6.82 us
  transfers between devices with their start and end apart: 19, of which 11 were waited for; matrix products, arithmetic and copies ran while one was open for 19% of the time, Pallas kernels for 8%

profile of v8, /device:TPU:1, one launch (start us, length us, event | category | flops | bytes accessed | tf_op | source)
XLA Modules:
  0.0 264.2 jit_solution(14262995630974006556)
XLA Ops:
  7.2 6.5 %collective-permute-start = (bf16[256,2432]{1,0:T(8,128)(2,1)}, bf16[256,2432]{1,0:T(8,128)(2,1)S(1)}, u32[]{:S(2)}, u32[]{:S(2)}) collective-permute-start(bf16[256,2432]{1,0:T(8,128)(2,1)} %refs_0_.1), channel_id=1, source_target_pairs={{0,224},{16,240},{32,0},{48,16},{64,32},{80,48},{96,64},{112,80},{... | collective-permute-start | bytes 3735560 | tf_op jit(solution)/shard_map/ppermute | solution.py:184
  36.5 3.6 %collective-permute-done.refs_2_ = bf16[256,2432]{1,0:T(8,128)(2,1)S(1)} collective-permute-done((bf16[256,2432]{1,0:T(8,128)(2,1)}, bf16[256,2432]{1,0:T(8,128)(2,1)S(1)}, u32[]{:S(2)}, u32[]{:S(2)}) %collective-permute-start) | collective-permute-done | bytes 1245216 | tf_op jit(solution)/shard_map/ppermute | solution.py:184
  40.0 3.3 %collective-permute-start.3 = (bf16[256,2432]{1,0:T(8,128)(2,1)S(1)}, bf16[256,2432]{1,0:T(8,128)(2,1)}, u32[]{:S(2)}, u32[]{:S(2)}) collective-permute-start(bf16[256,2432]{1,0:T(8,128)(2,1)S(1)} %collective-permute-done.refs_2_), channel_id=1, source_target_pairs={{0,224},{16,240},{32,0},{48,16},{64,32},{80,48},{96,64},{112,80},{... | collective-permute-start | bytes 3735560 | tf_op jit(solution)/shard_map/ppermute | solution.py:198
  43.4 2.2 fusion.18
  48.2 20.3 %collective-permute-done.3.refs_4_ = bf16[256,2432]{1,0:T(8,128)(2,1)} collective-permute-done((bf16[256,2432]{1,0:T(8,128)(2,1)S(1)}, bf16[256,2432]{1,0:T(8,128)(2,1)}, u32[]{:S(2)}, u32[]{:S(2)}) %collective-permute-start.3) | collective-permute-done | bytes 1245216 | tf_op jit(solution)/shard_map/ppermute | solution.py:198
  68.5 3.5 %collective-permute-start.5 = (bf16[256,2432]{1,0:T(8,128)(2,1)}, bf16[256,2432]{1,0:T(8,128)(2,1)S(1)}, u32[]{:S(2)}, u32[]{:S(2)}) collective-permute-start(bf16[256,2432]{1,0:T(8,128)(2,1)} %collective-permute-done.3.refs_4_), channel_id=1, source_target_pairs={{0,224},{16,240},{32,0},{48,16},{64,32},{80,48},{96,64},{112,80},{... | collective-permute-start | bytes 3735560 | tf_op jit(solution)/shard_map/ppermute | solution.py:198
  74.1 3.3 %fusion = f32[256,2432]{1,0:T(8,128)} fusion(f32[256,2432]{1,0:T(8,128)S(1)} %fusion.13, f32[256,2432]{1,0:T(8,128)S(1)} %copy-done.10, bf16[256,2432]{1,0:T(8,128)(2,1)} %collective-permute-done.6.refs_3_, bf16[8,256,256]{1,2,0:T(8,128)(2,1)S(1)} %pad_maximum_fusion.1, s32[]{:T(128)S(6)} %select_n.127), kind=kOutput, calls=%fused_computation.4 | convolution fusion | flops 320012288 | bytes 8847364 | tf_op jit(solution)/shard_map/dot_general | solution.py:180
  77.4 19.1 %collective-permute-done.5.refs_6_ = bf16[256,2432]{1,0:T(8,128)(2,1)S(1)} collective-permute-done((bf16[256,2432]{1,0:T(8,128)(2,1)}, bf16[256,2432]{1,0:T(8,128)(2,1)S(1)}, u32[]{:S(2)}, u32[]{:S(2)}) %collective-permute-start.5) | collective-permute-done | bytes 1245216 | tf_op jit(solution)/shard_map/ppermute | solution.py:198
  96.6 3.4 %collective-permute-start.10 = (bf16[128,2432]{1,0:T(8,128)(2,1)S(1)}, bf16[128,2432]{1,0:T(8,128)(2,1)}, u32[]{:S(2)}, u32[]{:S(2)}) collective-permute-start(bf16[128,2432]{1,0:T(8,128)(2,1)S(1)} %slice.51), channel_id=1, source_target_pairs={{0,224},{16,240},{32,0},{48,16},{64,32},{80,48},{96,64},{112,80},{... | collective-permute-start | bytes 1867784 | tf_op jit(solution)/shard_map/ppermute | solution.py:204
  100.3 9.6 %collective-permute-done.10.refs_8_ = bf16[128,2432]{1,0:T(8,128)(2,1)} collective-permute-done((bf16[128,2432]{1,0:T(8,128)(2,1)S(1)}, bf16[128,2432]{1,0:T(8,128)(2,1)}, u32[]{:S(2)}, u32[]{:S(2)}) %collective-permute-start.10) | collective-permute-done | bytes 622624 | tf_op jit(solution)/shard_map/ppermute | solution.py:204
  109.9 3.4 %collective-permute-done.9.refs_7_ = bf16[128,2432]{1,0:T(8,128)(2,1)S(1)} collective-permute-done((bf16[128,2432]{1,0:T(8,128)(2,1)S(1)}, bf16[128,2432]{1,0:T(8,128)(2,1)S(1)}, u32[]{:S(2)}, u32[]{:S(2)}) %collective-permute-start.9) | collective-permute-done | bytes 622624 | tf_op jit(solution)/shard_map/ppermute | solution.py:203
  119.5 4.6 %collective-permute-start.8 = (f32[128,2432]{1,0:T(8,128)}, f32[128,2432]{1,0:T(8,128)}, u32[]{:S(2)}, u32[]{:S(2)}) collective-permute-start(f32[128,2432]{1,0:T(8,128)} %slice.62), channel_id=1, source_target_pairs={{0,16},{16,0},{32,48},{48,32},{64,80},{80,64},{96,112},{112,96},{1... | collective-permute-start | bytes 3735560 | tf_op jit(solution)/shard_map/ppermute | solution.py:208
  130.3 2.2 fusion.60
  134.0 12.9 %all_to_all.20 = f32[16,4,128]{2,1,0:T(4,128)S(1)} all-to-all(f32[16,4,128]{2,1,0:T(4,128)S(1)} %broadcast_in_dim.134), channel_id=1, replica_groups=mesh['dp'=16,'mp'=16] {'mp'}, dimensions={0} | all-to-all | bytes 65536 | tf_op jit(solution)/shard_map/all_to_all | solution.py:243
  152.6 6.5 %shard_map.130 = f32[16,256,128]{2,1,0:T(8,128)} custom-call(s32[2]{0:T(128)S(1)} %pad_add_fusion.place_ref, bf16[256,2432]{1,0:T(8,128)(2,1)S(1)} %pad_maximum_fusion.grad_ref, bf16[256,2432]{1,0:T(8,128)(2,1)S(1)} %copy-done.6, bf16[256,2432]{1,0:T(8,128)(2,1)S(1)} %copy-done.5, bf16[256,2432]{1,0:T(8,128)(2,1)S(1)} %copy-done.3, ...), custom_call_target="tpu_custom_call" | custom-call | tf_op jit(solution)/shard_map/pallas_call | solution.py:265
  159.1 3.9 %all-to-all-start.1 = ((f32[16,256,128]{2,1,0:T(8,128)}), f32[16,256,128]{2,1,0:T(8,128)S(1)}, u32[]{:S(2)}, u32[]{:S(2)}) async-start(f32[16,256,128]{2,1,0:T(8,128)} %shard_map.130), calls=%async_computation.1 | async-start | bytes 4194304 | tf_op jit(solution)/shard_map/all_to_all | solution.py:274
  165.4 6.6 %shard_map.131.proj_ref = f32[16,4,32,256]{3,2,1,0:T(8,128)} custom-call(bf16[16,4,32,1664]{3,2,1,0:T(8,128)(2,1)} %bitcast.92, bf16[4,1536,256]{2,1,0:T(8,128)(2,1)} %down_ref.1), custom_call_target="tpu_custom_call" | custom-call | tf_op jit(solution)/shard_map/pallas_call | solution.py:222
  172.0 23.9 %all-to-all-done.1 = f32[16,256,128]{2,1,0:T(8,128)S(1)} async-done(((f32[16,256,128]{2,1,0:T(8,128)}), f32[16,256,128]{2,1,0:T(8,128)S(1)}, u32[]{:S(2)}, u32[]{:S(2)}) %all-to-all-start.1) | async-done | bytes 2097184 | tf_op jit(solution)/shard_map/all_to_all | solution.py:274
  198.7 6.4 %collective-permute-done.15 = f32[128,256]{0,1:T(8,128)S(1)} collective-permute-done((f32[128,256]{0,1:T(8,128)S(1)}, f32[128,256]{0,1:T(8,128)S(1)}, u32[]{:S(2)}, u32[]{:S(2)}) %collective-permute-start.15) | collective-permute-done | bytes 131104 | tf_op jit(solution)/shard_map/ppermute | solution.py:288
  205.4 27.9 %all_to_all.21.rows_ref = bf16[16,128,256]{2,1,0:T(8,128)(2,1)S(1)} all-to-all(bf16[16,128,256]{2,1,0:T(8,128)(2,1)S(1)} %broadcast_in_dim.135), channel_id=1, replica_groups=mesh['dp'=16,'mp'=16] {'mp'}, dimensions={0} | all-to-all | bytes 2097152 | tf_op jit(solution)/shard_map/all_to_all | solution.py:291
  233.3 2.8 %shard_map.133 = f32[16,16,128]{2,1,0:T(8,128)} custom-call(bf16[16,4,32,128]{3,2,1,0:T(8,128)(2,1)S(1)} %slice.71.side_ref, bf16[16,128,256]{2,1,0:T(8,128)(2,1)S(1)} %all_to_all.21.rows_ref, f32[16,4,32,256]{3,2,1,0:T(8,128)S(1)} %copy-done.1), custom_call_target="tpu_custom_call" | custom-call | tf_op jit(solution)/shard_map/pallas_call | solution.py:294
  236.1 6.8 %all-to-all-start.3 = ((f32[256,1,128]{2,1,0:T(1,128)}), f32[256,1,128]{2,1,0:T(1,128)S(1)}, u32[]{:S(2)}, u32[]{:S(2)}) async-start(f32[256,1,128]{2,1,0:T(1,128)} %bitcast.34), calls=%async_computation.3 | async-start | bytes 262144 | tf_op jit(solution)/shard_map/all_to_all | solution.py:315
  243.7 7.2 %shard_map.132 = bf16[4,1536,256]{2,1,0:T(8,128)(2,1)} custom-call(bf16[16,4,32,128]{3,2,1,0:T(8,128)(2,1)} %copy-done.7, bf16[16,128,256]{2,1,0:T(8,128)(2,1)} %copy-done, bf16[16,4,32,1664]{3,2,1,0:T(8,128)(2,1)} %bitcast.93), custom_call_target="tpu_custom_call" | custom-call | tf_op jit(solution)/shard_map/pallas_call | solution.py:301
  250.8 5.3 %all-to-all-done.3 = f32[256,1,128]{2,1,0:T(1,128)S(1)} async-done(((f32[256,1,128]{2,1,0:T(1,128)}), f32[256,1,128]{2,1,0:T(1,128)S(1)}, u32[]{:S(2)}, u32[]{:S(2)}) %all-to-all-start.3) | async-done | bytes 131104 | tf_op jit(solution)/shard_map/all_to_all | solution.py:315
  (136 shorter events, 54.5 us)
Async XLA Ops:
  7.2 157.2 %all-gather.3.cloned.1.call-start = ((), (), s32[]{:S(2)}) async-start(), calls=%async_computation.4 | async-start | bytes 7241728 | tf_op jit(solution)/shard_map/all_gather | solution.py:221
  7.2 32.8 %collective-permute-start = (bf16[256,2432]{1,0:T(8,128)(2,1)}, bf16[256,2432]{1,0:T(8,128)(2,1)S(1)}, u32[]{:S(2)}, u32[]{:S(2)}) collective-permute-start(bf16[256,2432]{1,0:T(8,128)(2,1)} %refs_0_.1), channel_id=1, source_target_pairs={{0,224},{16,240},{32,0},{48,16},{64,32},{80,48},{96,64},{112,80},{... | collective-permute-start | bytes 3735560 | tf_op jit(solution)/shard_map/ppermute | solution.py:184
  13.7 29.7 %collective-permute-start.4 = (bf16[256,2432]{1,0:T(8,128)(2,1)}, bf16[256,2432]{1,0:T(8,128)(2,1)S(1)}, u32[]{:S(2)}, u32[]{:S(2)}) collective-permute-start(bf16[256,2432]{1,0:T(8,128)(2,1)} %refs_0_.1), channel_id=1, source_target_pairs={{0,32},{16,48},{32,64},{48,80},{64,96},{80,112},{96,128},{112,144}... | collective-permute-start | bytes 3735560 | tf_op jit(solution)/shard_map/ppermute | solution.py:183
  18.8 16.3 %collective-permute-start.1 = (bf16[8,128,256]{1,2,0:T(8,128)(2,1)}, bf16[8,128,256]{1,2,0:T(8,128)(2,1)}, u32[]{:S(2)}, u32[]{:S(2)}) collective-permute-start(bf16[8,128,256]{1,2,0:T(8,128)(2,1)} %get-tuple-element.54), channel_id=1, source_target_pairs={{0,16},{16,0},{32,48},{48,32},{64,80},{80,64},{96,112},{112,96},{1... | collective-permute-start | bytes 1572872 | tf_op jit(solution)/shard_map/ppermute | solution.py:142
  20.4 13.2 %collective-permute-start.2 = (bf16[128,256]{0,1:T(8,128)(2,1)}, bf16[128,256]{0,1:T(8,128)(2,1)}, u32[]{:S(2)}, u32[]{:S(2)}) collective-permute-start(bf16[128,256]{0,1:T(8,128)(2,1)} %constant_dynamic-slice_fusion.3), channel_id=1, source_target_pairs={{0,16},{16,0},{32,48},{48,32},{64,80},{80,64},{96,112},{112,96},{1... | collective-permute-start | bytes 196616 | tf_op jit(solution)/shard_map/ppermute | solution.py:146
  36.5 37.5 %copy-start.13 = (bf16[8,256,256]{1,2,0:T(8,128)(2,1)}, bf16[8,256,256]{1,2,0:T(8,128)(2,1)S(1)}, u32[]{:S(2)}) copy-start(bf16[8,256,256]{1,2,0:T(8,128)(2,1)S(1)} %pad_maximum_fusion.1) | copy-start | bytes 3145732
  40.0 28.4 %collective-permute-start.3 = (bf16[256,2432]{1,0:T(8,128)(2,1)S(1)}, bf16[256,2432]{1,0:T(8,128)(2,1)}, u32[]{:S(2)}, u32[]{:S(2)}) collective-permute-start(bf16[256,2432]{1,0:T(8,128)(2,1)S(1)} %collective-permute-done.refs_2_), channel_id=1, source_target_pairs={{0,224},{16,240},{32,0},{48,16},{64,32},{80,48},{96,64},{112,80},{... | collective-permute-start | bytes 3735560 | tf_op jit(solution)/shard_map/ppermute | solution.py:198
  43.4 28.6 %collective-permute-start.6 = (bf16[256,2432]{1,0:T(8,128)(2,1)S(1)}, bf16[256,2432]{1,0:T(8,128)(2,1)}, u32[]{:S(2)}, u32[]{:S(2)}) collective-permute-start(bf16[256,2432]{1,0:T(8,128)(2,1)S(1)} %collective-permute-done.4.refs_1_), channel_id=1, source_target_pairs={{0,32},{16,48},{32,64},{48,80},{64,96},{80,112},{96,128},{112,144}... | collective-permute-start | bytes 3735560 | tf_op jit(solution)/shard_map/ppermute | solution.py:197
  68.5 28.0 %collective-permute-start.5 = (bf16[256,2432]{1,0:T(8,128)(2,1)}, bf16[256,2432]{1,0:T(8,128)(2,1)S(1)}, u32[]{:S(2)}, u32[]{:S(2)}) collective-permute-start(bf16[256,2432]{1,0:T(8,128)(2,1)} %collective-permute-done.3.refs_4_), channel_id=1, source_target_pairs={{0,224},{16,240},{32,0},{48,16},{64,32},{80,48},{96,64},{112,80},{... | collective-permute-start | bytes 3735560 | tf_op jit(solution)/shard_map/ppermute | solution.py:198
  72.0 27.9 %collective-permute-start.7 = (bf16[256,2432]{1,0:T(8,128)(2,1)}, bf16[256,2432]{1,0:T(8,128)(2,1)S(1)}, u32[]{:S(2)}, u32[]{:S(2)}) collective-permute-start(bf16[256,2432]{1,0:T(8,128)(2,1)} %collective-permute-done.6.refs_3_), channel_id=1, source_target_pairs={{0,32},{16,48},{32,64},{48,80},{64,96},{80,112},{96,128},{112,144}... | collective-permute-start | bytes 3735560 | tf_op jit(solution)/shard_map/ppermute | solution.py:197
  96.6 13.3 %collective-permute-start.10 = (bf16[128,2432]{1,0:T(8,128)(2,1)S(1)}, bf16[128,2432]{1,0:T(8,128)(2,1)}, u32[]{:S(2)}, u32[]{:S(2)}) collective-permute-start(bf16[128,2432]{1,0:T(8,128)(2,1)S(1)} %slice.51), channel_id=1, source_target_pairs={{0,224},{16,240},{32,0},{48,16},{64,32},{80,48},{96,64},{112,80},{... | collective-permute-start | bytes 1867784 | tf_op jit(solution)/shard_map/ppermute | solution.py:204
  100.0 13.3 %collective-permute-start.9 = (bf16[128,2432]{1,0:T(8,128)(2,1)S(1)}, bf16[128,2432]{1,0:T(8,128)(2,1)S(1)}, u32[]{:S(2)}, u32[]{:S(2)}) collective-permute-start(bf16[128,2432]{1,0:T(8,128)(2,1)S(1)} %slice.64), channel_id=1, source_target_pairs={{0,32},{16,48},{32,64},{48,80},{64,96},{80,112},{96,128},{112,144}... | collective-permute-start | bytes 1867784 | tf_op jit(solution)/shard_map/ppermute | solution.py:203
  119.5 9.3 %collective-permute-start.8 = (f32[128,2432]{1,0:T(8,128)}, f32[128,2432]{1,0:T(8,128)}, u32[]{:S(2)}, u32[]{:S(2)}) collective-permute-start(f32[128,2432]{1,0:T(8,128)} %slice.62), channel_id=1, source_target_pairs={{0,16},{16,0},{32,48},{48,32},{64,80},{80,64},{96,112},{112,96},{1... | collective-permute-start | bytes 3735560 | tf_op jit(solution)/shard_map/ppermute | solution.py:208
  126.9 3.4 %collective-permute-start.11 = (f32[128,2432]{1,0:T(8,128)}, f32[128,2432]{1,0:T(8,128)}, u32[]{:S(2)}, u32[]{:S(2)}) collective-permute-start(f32[128,2432]{1,0:T(8,128)} %convolution_add_fusion.4), channel_id=1, source_target_pairs={{0,16},{16,0},{32,48},{48,32},{64,80},{80,64},{96,112},{112,96},{1... | collective-permute-start | bytes 3735560 | tf_op jit(solution)/shard_map/ppermute | solution.py:213
  132.5 14.6 %copy-start.20 = (s32[128]{0:T(128)S(1)}, s32[128]{0:T(128)}, u32[]{:S(2)}) copy-start(s32[128]{0:T(128)} %param.17) | copy-start | bytes 1540
  149.1 3.4 %collective-permute-start.12 = (bf16[128,2432]{1,0:T(8,128)(2,1)S(1)}, bf16[128,2432]{1,0:T(8,128)(2,1)S(1)}, u32[]{:S(2)}, u32[]{:S(2)}) collective-permute-start(bf16[128,2432]{1,0:T(8,128)(2,1)S(1)} %multiply_convert_fusion), channel_id=1, source_target_pairs={{0,16},{16,0},{32,48},{48,32},{64,80},{80,64},{96,112},{112,96},{1... | collective-permute-start | bytes 1867784 | tf_op jit(solution)/shard_map/ppermute | solution.py:262
  159.1 36.8 %all-to-all-start.1 = ((f32[16,256,128]{2,1,0:T(8,128)}), f32[16,256,128]{2,1,0:T(8,128)S(1)}, u32[]{:S(2)}, u32[]{:S(2)}) async-start(f32[16,256,128]{2,1,0:T(8,128)} %shard_map.130), calls=%async_computation.1 | async-start | bytes 4194304 | tf_op jit(solution)/shard_map/all_to_all | solution.py:274
  163.0 1.3 collective-permute-start.13
  165.4 67.9 %copy-start.7 = (bf16[16,4,32,128]{3,2,1,0:T(8,128)(2,1)}, bf16[16,4,32,128]{3,2,1,0:T(8,128)(2,1)S(1)}, u32[]{:S(2)}) copy-start(bf16[16,4,32,128]{3,2,1,0:T(8,128)(2,1)S(1)} %slice.71.side_ref) | copy-start | bytes 1572868
  172.0 24.0 %copy-start.15 = (bf16[128,256]{0,1:T(8,128)(2,1)S(1)}, bf16[128,256]{0,1:T(8,128)(2,1)}, u32[]{:S(2)}) copy-start(bf16[128,256]{0,1:T(8,128)(2,1)} %dynamic-slice_select_fusion) | copy-start | bytes 196612
  196.1 9.0 %collective-permute-start.15 = (f32[128,256]{0,1:T(8,128)S(1)}, f32[128,256]{0,1:T(8,128)S(1)}, u32[]{:S(2)}, u32[]{:S(2)}) collective-permute-start(f32[128,256]{0,1:T(8,128)S(1)} %get-tuple-element.48), channel_id=1, source_target_pairs={{0,0},{1,16},{2,2},{3,18},{4,4},{5,20},{6,6},{7,22},{8,8},{9,24},{... | collective-permute-start | bytes 393224 | tf_op jit(solution)/shard_map/ppermute | solution.py:288
  198.1 0.7 collective-permute-start.14
  205.4 27.9 %copy-start.1 = (f32[16,4,32,256]{3,2,1,0:T(8,128)S(1)}, f32[16,4,32,256]{3,2,1,0:T(8,128)}, u32[]{:S(2)}) copy-start(f32[16,4,32,256]{3,2,1,0:T(8,128)} %shard_map.131.proj_ref) | copy-start | bytes 6291460
  236.1 20.0 %all-to-all-start.3 = ((f32[256,1,128]{2,1,0:T(1,128)}), f32[256,1,128]{2,1,0:T(1,128)S(1)}, u32[]{:S(2)}, u32[]{:S(2)}) async-start(f32[256,1,128]{2,1,0:T(1,128)} %bitcast.34), calls=%async_computation.3 | async-start | bytes 262144 | tf_op jit(solution)/shard_map/all_to_all | solution.py:315
  (19 other events, 93.3 us)
Sparse Core Ops, SparseCore 0:
  113.5 50.8 all-gather.2

commit v9 on v7

--- a/solution.py
+++ b/solution.py
@@ -212,7 +212,9 @@
     head_pieces += last_pieces
     logits = own_part + swap(other_part)
 
-    acts_block, _ = lax.optimization_barrier((acts_block, tuple(p for _, _, p in last_pieces)))
+    acts_block, _ = lax.optimization_barrier(
+        (acts_block, (partial,) + tuple(p for _, _, p in last_pieces))
+    )
     acts_all = lax.all_gather(acts_block, "dp", axis=0, tiled=False)
     proj = pl.pallas_call(
         proj_kernel,

time: 262 us -> 259 us (0.989)
  waiting for transfers between devices: 91.7 us -> 88.6 us
    ppermute x1, waiting for transfers between devices: 10.7 us -> 6.33 us  [local(): lax.ppermute(ahead[:half], 'dp', z_shift(1, nz))]
    all_to_all x1, waiting for transfers between devices: 20.2 us -> 16.8 us  [local(): hidden = lax.all_to_all(hidden, 'mp', 0, 0, tiled=True)]
    all_gather x1, waiting for transfers between devices: 3.66 us -> 7.06 us  [local(): acts_all = lax.all_gather(acts_block, 'dp', axis=0, tiled=False)]
where the time goes in v9:
time: 259 us; the launch traced here: 257 us
  waiting for transfers between devices  88.6 us (34%)
  blocking collectives  40.9 us (16%)
  starting transfers between devices  36 us (14%)
  Pallas kernels  23.1 us (9%)
  other arithmetic  23 us (9%)
  matrix products  17.6 us (7%)
  between operations  14.5 us (6%)
  local copies, waits for them, and re-layouts  13.5 us (5%)
    ppermute x2, waiting for transfers between devices, local(): ahead = lax.ppermute(ahead, 'dp', z_shift(1, nz))  43.4 us
    all_to_all x1, blocking collectives, local(): lax.all_to_all(jnp.broadcast_to(stream_grad[None], (mp_count, tokens, blo...  27.9 us
    dot_general x11, matrix products, logits_of(): return jnp.dot(features, piece, preferred_element_type=f32)  17.6 us
    all_to_all x1, waiting for transfers between devices, local(): hidden = lax.all_to_all(hidden, 'mp', 0, 0, tiled=True)  16.8 us
    all_to_all x1, blocking collectives, local(): lax.all_to_all(jnp.broadcast_to(stats[None], (mp_count, 4, tokens)), 'mp'...  13 us
    all_to_all x1, starting transfers between devices, local(): lax.all_to_all(gate.reshape(dp_count * mp_count, 1, per_expert * capacity...  7.29 us
    pallas_call x1, Pallas kernels, local(): pl.pallas_call(down_kernel, grid=(per_expert,), in_specs=[pl.BlockSpec((d...  7.17 us
    all_gather x1, waiting for transfers between devices, local(): acts_all = lax.all_gather(acts_block, 'dp', axis=0, tiled=False)  7.06 us
  transfers between devices with their start and end apart: 18, of which 11 were waited for; matrix products, arithmetic and copies ran while one was open for 20% of the time, Pallas kernels for 8%

profile of v9, /device:TPU:1, one launch (start us, length us, event | category | flops | bytes accessed | tf_op | source)
XLA Modules:
  0.0 257.2 jit_solution(12176814710125230629)
XLA Ops:
  7.2 2.5 collective-permute-start.4
  9.8 4.0 %collective-permute-start = (bf16[256,2432]{1,0:T(8,128)(2,1)}, bf16[256,2432]{1,0:T(8,128)(2,1)S(1)}, u32[]{:S(2)}, u32[]{:S(2)}) collective-permute-start(bf16[256,2432]{1,0:T(8,128)(2,1)} %refs_0_.1), channel_id=1, source_target_pairs={{0,224},{16,240},{32,0},{48,16},{64,32},{80,48},{96,64},{112,80},{... | collective-permute-start | bytes 3735560 | tf_op jit(solution)/shard_map/ppermute | solution.py:184
  18.6 2.3 dynamic-slice_bitcast_fusion.1
  41.0 2.7 %collective-permute-start.3 = (bf16[256,2432]{1,0:T(8,128)(2,1)S(1)}, bf16[256,2432]{1,0:T(8,128)(2,1)}, u32[]{:S(2)}, u32[]{:S(2)}) collective-permute-start(bf16[256,2432]{1,0:T(8,128)(2,1)S(1)} %collective-permute-done.refs_2_), channel_id=1, source_target_pairs={{0,224},{16,240},{32,0},{48,16},{64,32},{80,48},{96,64},{112,80},{... | collective-permute-start | bytes 3735560 | tf_op jit(solution)/shard_map/ppermute | solution.py:198
  48.1 21.9 %collective-permute-done.6.refs_3_ = bf16[256,2432]{1,0:T(8,128)(2,1)} collective-permute-done((bf16[256,2432]{1,0:T(8,128)(2,1)S(1)}, bf16[256,2432]{1,0:T(8,128)(2,1)}, u32[]{:S(2)}, u32[]{:S(2)}) %collective-permute-start.6) | collective-permute-done | bytes 1245216 | tf_op jit(solution)/shard_map/ppermute | solution.py:197
  70.0 2.7 %collective-permute-start.5 = (bf16[256,2432]{1,0:T(8,128)(2,1)}, bf16[256,2432]{1,0:T(8,128)(2,1)S(1)}, u32[]{:S(2)}, u32[]{:S(2)}) collective-permute-start(bf16[256,2432]{1,0:T(8,128)(2,1)} %collective-permute-done.3.refs_4_), channel_id=1, source_target_pairs={{0,224},{16,240},{32,0},{48,16},{64,32},{80,48},{96,64},{112,80},{... | collective-permute-start | bytes 3735560 | tf_op jit(solution)/shard_map/ppermute | solution.py:198
  76.6 21.5 %collective-permute-done.7.refs_5_ = bf16[256,2432]{1,0:T(8,128)(2,1)S(1)} collective-permute-done((bf16[256,2432]{1,0:T(8,128)(2,1)}, bf16[256,2432]{1,0:T(8,128)(2,1)S(1)}, u32[]{:S(2)}, u32[]{:S(2)}) %collective-permute-start.7) | collective-permute-done | bytes 1245216 | tf_op jit(solution)/shard_map/ppermute | solution.py:197
  98.3 2.9 %collective-permute-start.9 = (bf16[128,2432]{1,0:T(8,128)(2,1)S(1)}, bf16[128,2432]{1,0:T(8,128)(2,1)}, u32[]{:S(2)}, u32[]{:S(2)}) collective-permute-start(bf16[128,2432]{1,0:T(8,128)(2,1)S(1)} %slice.50), channel_id=1, source_target_pairs={{0,224},{16,240},{32,0},{48,16},{64,32},{80,48},{96,64},{112,80},{... | collective-permute-start | bytes 1867784 | tf_op jit(solution)/shard_map/ppermute | solution.py:204
  102.6 2.9 %fusion.1 = f32[256,2432]{1,0:T(8,128)} fusion(f32[256,2432]{1,0:T(8,128)S(1)} %fusion.10, f32[256,2432]{1,0:T(8,128)S(1)} %fusion, bf16[256,2432]{1,0:T(8,128)(2,1)S(1)} %collective-permute-done.7.refs_5_, bf16[8,256,256]{1,2,0:T(8,128)(2,1)} %copy-done.11, s32[]{:T(128)S(6)} %select_n.129), kind=kOutput, calls=%fused_computation.5 | convolution fusion | flops 320012288 | bytes 8847364 | tf_op jit(solution)/shard_map/dot_general | solution.py:180
  105.6 6.3 %collective-permute-done.8.refs_7_ = bf16[128,2432]{1,0:T(8,128)(2,1)S(1)} collective-permute-done((bf16[128,2432]{1,0:T(8,128)(2,1)S(1)}, bf16[128,2432]{1,0:T(8,128)(2,1)S(1)}, u32[]{:S(2)}, u32[]{:S(2)}) %collective-permute-start.8) | collective-permute-done | bytes 622624 | tf_op jit(solution)/shard_map/ppermute | solution.py:203
  113.3 2.9 %fusion.5 = f32[128,2432]{1,0:T(8,128)} fusion(f32[128,2432]{1,0:T(8,128)S(1)} %fusion.35, f32[256,2432]{1,0:T(8,128)} %fusion.1, bf16[128,2432]{1,0:T(8,128)(2,1)} %collective-permute-done.9.refs_8_, bf16[256,256]{1,0:T(8,128)(2,1)S(1)} %bitcast.97), kind=kOutput, calls=%fused_computation.12 | convolution fusion | flops 80314368 | bytes 4390912 | tf_op jit(solution)/shard_map/dot_general | solution.py:180
  116.2 4.0 %collective-permute-start.10 = (f32[128,2432]{1,0:T(8,128)}, f32[128,2432]{1,0:T(8,128)}, u32[]{:S(2)}, u32[]{:S(2)}) collective-permute-start(f32[128,2432]{1,0:T(8,128)} %fusion.5), channel_id=1, source_target_pairs={{0,16},{16,0},{32,48},{48,32},{64,80},{80,64},{96,112},{112,96},{1... | collective-permute-start | bytes 3735560 | tf_op jit(solution)/shard_map/ppermute | solution.py:213
  126.4 13.0 %all_to_all.20 = f32[16,4,128]{2,1,0:T(4,128)S(1)} all-to-all(f32[16,4,128]{2,1,0:T(4,128)S(1)} %broadcast_in_dim.134), channel_id=1, replica_groups=mesh['dp'=16,'mp'=16] {'mp'}, dimensions={0} | all-to-all | bytes 65536 | tf_op jit(solution)/shard_map/all_to_all | solution.py:240
  145.3 6.5 %shard_map.130 = f32[16,256,128]{2,1,0:T(8,128)} custom-call(s32[2]{0:T(128)S(1)} %pad_add_fusion.place_ref, bf16[256,2432]{1,0:T(8,128)(2,1)S(1)} %pad_maximum_fusion.grad_ref, bf16[256,2432]{1,0:T(8,128)(2,1)S(1)} %copy-done.6, bf16[256,2432]{1,0:T(8,128)(2,1)S(1)} %copy-done.3, bf16[256,2432]{1,0:T(8,128)(2,1)S(1)} %copy-done.5, ...), custom_call_target="tpu_custom_call" | custom-call | tf_op jit(solution)/shard_map/pallas_call | solution.py:262
  151.8 3.9 %all-to-all-start.1 = ((f32[16,256,128]{2,1,0:T(8,128)}), f32[16,256,128]{2,1,0:T(8,128)S(1)}, u32[]{:S(2)}, u32[]{:S(2)}) async-start(f32[16,256,128]{2,1,0:T(8,128)} %shard_map.130), calls=%async_computation.1 | async-start | bytes 4194304 | tf_op jit(solution)/shard_map/all_to_all | solution.py:271
  157.1 7.1 %all-gather.3.cloned.1.call-done = bf16[64,32,1664]{2,1,0:T(8,128)(2,1)} async-done(((bf16[4,32,1664]{2,1,0:T(8,128)(2,1)}), bf16[64,32,1664]{2,1,0:T(8,128)(2,1)}) %all-gather.3.cloned.1.call-update) | async-done | bytes 6815760 | tf_op jit(solution)/shard_map/all_gather | solution.py:218
  165.2 6.6 %shard_map.131.proj_ref = f32[16,4,32,256]{3,2,1,0:T(8,128)} custom-call(bf16[16,4,32,1664]{3,2,1,0:T(8,128)(2,1)} %bitcast.92, bf16[4,1536,256]{2,1,0:T(8,128)(2,1)} %down_ref.1), custom_call_target="tpu_custom_call" | custom-call | tf_op jit(solution)/shard_map/pallas_call | solution.py:219
  171.9 16.8 %all-to-all-done.1 = f32[16,256,128]{2,1,0:T(8,128)S(1)} async-done(((f32[16,256,128]{2,1,0:T(8,128)}), f32[16,256,128]{2,1,0:T(8,128)S(1)}, u32[]{:S(2)}, u32[]{:S(2)}) %all-to-all-start.1) | async-done | bytes 2097184 | tf_op jit(solution)/shard_map/all_to_all | solution.py:271
  191.5 6.4 %collective-permute-done.14 = f32[128,256]{0,1:T(8,128)S(1)} collective-permute-done((f32[128,256]{0,1:T(8,128)S(1)}, f32[128,256]{0,1:T(8,128)S(1)}, u32[]{:S(2)}, u32[]{:S(2)}) %collective-permute-start.14) | collective-permute-done | bytes 131104 | tf_op jit(solution)/shard_map/ppermute | solution.py:285
  198.1 27.9 %all_to_all.21.rows_ref = bf16[16,128,256]{2,1,0:T(8,128)(2,1)S(1)} all-to-all(bf16[16,128,256]{2,1,0:T(8,128)(2,1)S(1)} %broadcast_in_dim.135), channel_id=1, replica_groups=mesh['dp'=16,'mp'=16] {'mp'}, dimensions={0} | all-to-all | bytes 2097152 | tf_op jit(solution)/shard_map/all_to_all | solution.py:288
  226.1 2.8 %shard_map.133 = f32[16,16,128]{2,1,0:T(8,128)} custom-call(bf16[16,4,32,128]{3,2,1,0:T(8,128)(2,1)S(1)} %slice.71.side_ref, bf16[16,128,256]{2,1,0:T(8,128)(2,1)S(1)} %all_to_all.21.rows_ref, f32[16,4,32,256]{3,2,1,0:T(8,128)S(1)} %copy-done.1), custom_call_target="tpu_custom_call" | custom-call | tf_op jit(solution)/shard_map/pallas_call | solution.py:291
  228.8 7.3 %all-to-all-start.3 = ((f32[256,1,128]{2,1,0:T(1,128)}), f32[256,1,128]{2,1,0:T(1,128)S(1)}, u32[]{:S(2)}, u32[]{:S(2)}) async-start(f32[256,1,128]{2,1,0:T(1,128)} %bitcast.34), calls=%async_computation.3 | async-start | bytes 262144 | tf_op jit(solution)/shard_map/all_to_all | solution.py:312
  236.9 7.2 %shard_map.132 = bf16[4,1536,256]{2,1,0:T(8,128)(2,1)} custom-call(bf16[16,4,32,128]{3,2,1,0:T(8,128)(2,1)} %copy-done.7, bf16[16,128,256]{2,1,0:T(8,128)(2,1)} %copy-done, bf16[16,4,32,1664]{3,2,1,0:T(8,128)(2,1)} %bitcast.93), custom_call_target="tpu_custom_call" | custom-call | tf_op jit(solution)/shard_map/pallas_call | solution.py:298
  244.1 5.1 %all-to-all-done.3 = f32[256,1,128]{2,1,0:T(1,128)S(1)} async-done(((f32[256,1,128]{2,1,0:T(1,128)}), f32[256,1,128]{2,1,0:T(1,128)S(1)}, u32[]{:S(2)}, u32[]{:S(2)}) %all-to-all-start.3) | async-done | bytes 131104 | tf_op jit(solution)/shard_map/all_to_all | solution.py:312
  (129 shorter events, 55.5 us)
Async XLA Ops:
  7.2 156.9 %all-gather.3.cloned.1.call-start = ((), (), s32[]{:S(2)}) async-start(), calls=%async_computation.4 | async-start | bytes 7241728 | tf_op jit(solution)/shard_map/all_gather | solution.py:218
  7.2 33.8 %collective-permute-start.4 = (bf16[256,2432]{1,0:T(8,128)(2,1)}, bf16[256,2432]{1,0:T(8,128)(2,1)S(1)}, u32[]{:S(2)}, u32[]{:S(2)}) collective-permute-start(bf16[256,2432]{1,0:T(8,128)(2,1)} %refs_0_.1), channel_id=1, source_target_pairs={{0,32},{16,48},{32,64},{48,80},{64,96},{80,112},{96,128},{112,144}... | collective-permute-start | bytes 3735560 | tf_op jit(solution)/shard_map/ppermute | solution.py:183
  9.8 30.5 %collective-permute-start = (bf16[256,2432]{1,0:T(8,128)(2,1)}, bf16[256,2432]{1,0:T(8,128)(2,1)S(1)}, u32[]{:S(2)}, u32[]{:S(2)}) collective-permute-start(bf16[256,2432]{1,0:T(8,128)(2,1)} %refs_0_.1), channel_id=1, source_target_pairs={{0,224},{16,240},{32,0},{48,16},{64,32},{80,48},{96,64},{112,80},{... | collective-permute-start | bytes 3735560 | tf_op jit(solution)/shard_map/ppermute | solution.py:184
  21.0 17.9 %collective-permute-start.1 = (bf16[8,128,256]{1,2,0:T(8,128)(2,1)}, bf16[8,128,256]{1,2,0:T(8,128)(2,1)}, u32[]{:S(2)}, u32[]{:S(2)}) collective-permute-start(bf16[8,128,256]{1,2,0:T(8,128)(2,1)} %get-tuple-element.54), channel_id=1, source_target_pairs={{0,16},{16,0},{32,48},{48,32},{64,80},{80,64},{96,112},{112,96},{1... | collective-permute-start | bytes 1572872 | tf_op jit(solution)/shard_map/ppermute | solution.py:142
  22.5 14.8 %collective-permute-start.2 = (bf16[128,256]{0,1:T(8,128)(2,1)}, bf16[128,256]{0,1:T(8,128)(2,1)}, u32[]{:S(2)}, u32[]{:S(2)}) collective-permute-start(bf16[128,256]{0,1:T(8,128)(2,1)} %constant_dynamic-slice_fusion.3), channel_id=1, source_target_pairs={{0,16},{16,0},{32,48},{48,32},{64,80},{80,64},{96,112},{112,96},{1... | collective-permute-start | bytes 196616 | tf_op jit(solution)/shard_map/ppermute | solution.py:146
  40.2 34.4 %copy-start.11 = (bf16[8,256,256]{1,2,0:T(8,128)(2,1)}, bf16[8,256,256]{1,2,0:T(8,128)(2,1)S(1)}, u32[]{:S(2)}) copy-start(bf16[8,256,256]{1,2,0:T(8,128)(2,1)S(1)} %pad_maximum_fusion.1) | copy-start | bytes 3145732
  41.0 29.0 %collective-permute-start.6 = (bf16[256,2432]{1,0:T(8,128)(2,1)S(1)}, bf16[256,2432]{1,0:T(8,128)(2,1)}, u32[]{:S(2)}, u32[]{:S(2)}) collective-permute-start(bf16[256,2432]{1,0:T(8,128)(2,1)S(1)} %collective-permute-done.4.refs_1_), channel_id=1, source_target_pairs={{0,32},{16,48},{32,64},{48,80},{64,96},{80,112},{96,128},{112,144}... | collective-permute-start | bytes 3735560 | tf_op jit(solution)/shard_map/ppermute | solution.py:197
  41.0 29.0 %collective-permute-start.3 = (bf16[256,2432]{1,0:T(8,128)(2,1)S(1)}, bf16[256,2432]{1,0:T(8,128)(2,1)}, u32[]{:S(2)}, u32[]{:S(2)}) collective-permute-start(bf16[256,2432]{1,0:T(8,128)(2,1)S(1)} %collective-permute-done.refs_2_), channel_id=1, source_target_pairs={{0,224},{16,240},{32,0},{48,16},{64,32},{80,48},{96,64},{112,80},{... | collective-permute-start | bytes 3735560 | tf_op jit(solution)/shard_map/ppermute | solution.py:198
  70.0 28.1 %collective-permute-start.7 = (bf16[256,2432]{1,0:T(8,128)(2,1)}, bf16[256,2432]{1,0:T(8,128)(2,1)S(1)}, u32[]{:S(2)}, u32[]{:S(2)}) collective-permute-start(bf16[256,2432]{1,0:T(8,128)(2,1)} %collective-permute-done.6.refs_3_), channel_id=1, source_target_pairs={{0,32},{16,48},{32,64},{48,80},{64,96},{80,112},{96,128},{112,144}... | collective-permute-start | bytes 3735560 | tf_op jit(solution)/shard_map/ppermute | solution.py:197
  70.0 28.3 %collective-permute-start.5 = (bf16[256,2432]{1,0:T(8,128)(2,1)}, bf16[256,2432]{1,0:T(8,128)(2,1)S(1)}, u32[]{:S(2)}, u32[]{:S(2)}) collective-permute-start(bf16[256,2432]{1,0:T(8,128)(2,1)} %collective-permute-done.3.refs_4_), channel_id=1, source_target_pairs={{0,224},{16,240},{32,0},{48,16},{64,32},{80,48},{96,64},{112,80},{... | collective-permute-start | bytes 3735560 | tf_op jit(solution)/shard_map/ppermute | solution.py:198
  98.1 13.7 %collective-permute-start.8 = (bf16[128,2432]{1,0:T(8,128)(2,1)S(1)}, bf16[128,2432]{1,0:T(8,128)(2,1)S(1)}, u32[]{:S(2)}, u32[]{:S(2)}) collective-permute-start(bf16[128,2432]{1,0:T(8,128)(2,1)S(1)} %slice.63), channel_id=1, source_target_pairs={{0,32},{16,48},{32,64},{48,80},{64,96},{80,112},{96,128},{112,144}... | collective-permute-start | bytes 1867784 | tf_op jit(solution)/shard_map/ppermute | solution.py:203
  98.3 13.6 %collective-permute-start.9 = (bf16[128,2432]{1,0:T(8,128)(2,1)S(1)}, bf16[128,2432]{1,0:T(8,128)(2,1)}, u32[]{:S(2)}, u32[]{:S(2)}) collective-permute-start(bf16[128,2432]{1,0:T(8,128)(2,1)S(1)} %slice.50), channel_id=1, source_target_pairs={{0,224},{16,240},{32,0},{48,16},{64,32},{80,48},{96,64},{112,80},{... | collective-permute-start | bytes 1867784 | tf_op jit(solution)/shard_map/ppermute | solution.py:204
  116.2 6.9 %collective-permute-start.10 = (f32[128,2432]{1,0:T(8,128)}, f32[128,2432]{1,0:T(8,128)}, u32[]{:S(2)}, u32[]{:S(2)}) collective-permute-start(f32[128,2432]{1,0:T(8,128)} %fusion.5), channel_id=1, source_target_pairs={{0,16},{16,0},{32,48},{48,32},{64,80},{80,64},{96,112},{112,96},{1... | collective-permute-start | bytes 3735560 | tf_op jit(solution)/shard_map/ppermute | solution.py:213
  124.9 14.7 %copy-start.18 = (s32[128]{0:T(128)S(1)}, s32[128]{0:T(128)}, u32[]{:S(2)}) copy-start(s32[128]{0:T(128)} %param.17) | copy-start | bytes 1540
  124.9 14.7 %copy-start.19 = (f32[128]{0:T(128)S(1)}, f32[128]{0:T(128)}, u32[]{:S(2)}) copy-start(f32[128]{0:T(128)} %param.16) | copy-start | bytes 1540
  141.6 3.6 %collective-permute-start.11 = (bf16[128,2432]{1,0:T(8,128)(2,1)S(1)}, bf16[128,2432]{1,0:T(8,128)(2,1)S(1)}, u32[]{:S(2)}, u32[]{:S(2)}) collective-permute-start(bf16[128,2432]{1,0:T(8,128)(2,1)S(1)} %multiply_convert_fusion), channel_id=1, source_target_pairs={{0,16},{16,0},{32,48},{48,32},{64,80},{80,64},{96,112},{112,96},{1... | collective-permute-start | bytes 1867784 | tf_op jit(solution)/shard_map/ppermute | solution.py:259
  151.8 36.8 %all-to-all-start.1 = ((f32[16,256,128]{2,1,0:T(8,128)}), f32[16,256,128]{2,1,0:T(8,128)S(1)}, u32[]{:S(2)}, u32[]{:S(2)}) async-start(f32[16,256,128]{2,1,0:T(8,128)} %shard_map.130), calls=%async_computation.1 | async-start | bytes 4194304 | tf_op jit(solution)/shard_map/all_to_all | solution.py:271
  155.7 1.3 collective-permute-start.12
  165.2 60.9 %copy-start.7 = (bf16[16,4,32,128]{3,2,1,0:T(8,128)(2,1)}, bf16[16,4,32,128]{3,2,1,0:T(8,128)(2,1)S(1)}, u32[]{:S(2)}) copy-start(bf16[16,4,32,128]{3,2,1,0:T(8,128)(2,1)S(1)} %slice.71.side_ref) | copy-start | bytes 1572868
  171.8 16.9 %copy-start.13 = (bf16[128,256]{0,1:T(8,128)(2,1)S(1)}, bf16[128,256]{0,1:T(8,128)(2,1)}, u32[]{:S(2)}) copy-start(bf16[128,256]{0,1:T(8,128)(2,1)} %dynamic-slice_select_fusion) | copy-start | bytes 196612
  188.9 9.0 %collective-permute-start.14 = (f32[128,256]{0,1:T(8,128)S(1)}, f32[128,256]{0,1:T(8,128)S(1)}, u32[]{:S(2)}, u32[]{:S(2)}) collective-permute-start(f32[128,256]{0,1:T(8,128)S(1)} %get-tuple-element.48), channel_id=1, source_target_pairs={{0,0},{1,16},{2,2},{3,18},{4,4},{5,20},{6,6},{7,22},{8,8},{9,24},{... | collective-permute-start | bytes 393224 | tf_op jit(solution)/shard_map/ppermute | solution.py:285
  190.8 0.7 collective-permute-start.13
  198.1 27.9 %copy-start.1 = (f32[16,4,32,256]{3,2,1,0:T(8,128)S(1)}, f32[16,4,32,256]{3,2,1,0:T(8,128)}, u32[]{:S(2)}) copy-start(f32[16,4,32,256]{3,2,1,0:T(8,128)} %shard_map.131.proj_ref) | copy-start | bytes 6291460
  228.8 20.3 %all-to-all-start.3 = ((f32[256,1,128]{2,1,0:T(1,128)}), f32[256,1,128]{2,1,0:T(1,128)S(1)}, u32[]{:S(2)}, u32[]{:S(2)}) async-start(f32[256,1,128]{2,1,0:T(1,128)} %bitcast.34), calls=%async_computation.3 | async-start | bytes 262144 | tf_op jit(solution)/shard_map/all_to_all | solution.py:312
  (16 other events, 84.8 us)
Sparse Core Ops, SparseCore 0:
  112.0 52.0 all-gather.2
